TPU v7x, 32 devices: a whole 2x2x4 slice. The times are simulated.
32 devices in a mesh: dp: 4 (over y, x), ctx: 8 (over z, core).
Axes of the slice: x: 2, y: 2, z: 4, core: 2. Of those that a mesh axis runs over, the one named last changes fastest.
Arguments:
- tokens: bfloat16 [4, 1536, 2048], P('dp', 'ctx'), may hold values from -6 to 6
- prefix: int32 [4], P('dp'), may hold values from 153 to 768
- g_attn: bfloat16 [2048], P(('dp', 'ctx')), may hold values from 0.099609375 to 1.8984375
- w_query: bfloat16 [2048, 2048], P(('dp', 'ctx')), may hold values from -0.125 to 0.125
- w_key: bfloat16 [2048, 1024], P(('dp', 'ctx')), may hold values from -0.125 to 0.125
- w_value: bfloat16 [2048, 1024], P(('dp', 'ctx')), may hold values from -0.125 to 0.125
- w_output: bfloat16 [2048, 2048], P(('dp', 'ctx')), may hold values from -3 to 3
- g_mlp: bfloat16 [2048], P(('dp', 'ctx')), may hold values from 0.099609375 to 1.8984375
- w_gate: bfloat16 [2048, 8192], P(('dp', 'ctx')), may hold values from -0.125 to 0.125
- w_up: bfloat16 [2048, 8192], P(('dp', 'ctx')), may hold values from -0.125 to 0.125
- w_down: bfloat16 [8192, 2048], P(('dp', 'ctx')), may hold values from -0.0625 to 0.0625
- cotangent: bfloat16 [4, 1536, 2048], P('dp', 'ctx'), may hold values from -6 to 6
Outputs:
- out: bfloat16 [4, 1536, 2048], P('dp', 'ctx')
- input_grad: bfloat16 [4, 1536, 2048], P('dp', 'ctx')
- grad_g_attn: float32 [2048], P(('dp', 'ctx'))
- grad_query: float32 [2048, 2048], P(('dp', 'ctx'))
- grad_key: float32 [2048, 1024], P(('dp', 'ctx'))
- grad_value: float32 [2048, 1024], P(('dp', 'ctx'))
- grad_output: float32 [2048, 2048], P(('dp', 'ctx'))
- grad_g_mlp: float32 [2048], P(('dp', 'ctx'))
- grad_gate: float32 [2048, 8192], P(('dp', 'ctx'))
- grad_up: float32 [2048, 8192], P(('dp', 'ctx'))
- grad_down: float32 [8192, 2048], P(('dp', 'ctx'))
All inputs are finite; a program needn't handle non-finite values.
Results may differ from a plain program's by a relative error of at most 0.018.
Values may be sent and summed in bfloat16 or wider, within the bound.
No kernel may reach another device: no remote copies, remote signals or barrier semaphores. Data moves between devices by JAX's collectives and lax.ppermute only.
A program may use at most 704 MiB of HBM per device.

v0:
```python
import jax
import jax.numpy as jnp
from jax import lax
from jax.sharding import PartitionSpec as P

FF = 8192
H = 8
KVH = 4
HD = 256
KEYBLK = 512


EPS = 1e-06
THETA = 1000042.0
NEG = -1e30


def mul_plain(first_op, second_op):
    return jnp.dot(first_op, second_op, preferred_element_type=jnp.float32)


def mul_right(first_op, second_op):
    return lax.dot_general(
        first_op, second_op, (((1,), (1,)), ((), ())), preferred_element_type=jnp.float32
    )


def mul_left(first_op, second_op):
    return lax.dot_general(
        first_op, second_op, (((0,), (0,)), ((), ())), preferred_element_type=jnp.float32
    )


def normalize(values):
    return values * lax.rsqrt(jnp.mean(values * values, axis=-1, keepdims=True) + EPS)


def norm_back(values, normed, grad_normed):
    factor = lax.rsqrt(jnp.mean(values * values, axis=-1, keepdims=True) + EPS)
    return factor * (grad_normed - normed * jnp.mean(grad_normed * normed, axis=-1, keepdims=True))


def rotary(first_pos, length, head_dim):
    half_dim = head_dim // 2
    frequency = 1.0 / THETA ** (lax.iota(jnp.float32, half_dim) * (2.0 / head_dim))
    angles = (first_pos + lax.iota(jnp.int32, length)).astype(jnp.float32)[:, None] * frequency[
        None, :
    ]
    cosine = jnp.concatenate((jnp.cos(angles), jnp.cos(angles)), axis=1)
    sine_table = jnp.concatenate((jnp.sin(angles), jnp.sin(angles)), axis=1)
    return (cosine, sine_table)


def rotate(values, cosine, sine_table):
    half_dim = values.shape[-1] // 2
    rolled = jnp.concatenate((-values[..., half_dim:], values[..., :half_dim]), axis=-1)
    return values * cosine[:, None, :] + rolled * sine_table[:, None, :]


def per_device(
    tokens,
    prefix,
    g_attn,
    w_query,
    w_key,
    w_value,
    w_output,
    g_mlp,
    w_gate,
    w_up,
    w_down,
    cotangent,
):
    tok_rows = tokens.shape[1]
    key_span = lax.axis_size("ctx") * tok_rows
    first_pos = lax.axis_index("ctx") * tok_rows
    head_group = H // KVH
    query_width = H * HD
    key_width = KVH * HD
    score_scale = HD ** (-0.5)
    key_blocks = key_span // KEYBLK
    prefix_len = prefix[0]
    tok_in = tokens[0].astype(jnp.float32)
    nrm_one = normalize(tok_in)
    cosine, sine_table = rotary(first_pos, tok_rows, HD)
    query_pos = first_pos + lax.iota(jnp.int32, tok_rows)

    def visible(key_first, length):
        key_pos = key_first + lax.iota(jnp.int32, length)
        return (key_pos[None, :] <= query_pos[:, None]) | (key_pos[None, :] < prefix_len)

    gain_piece = lax.all_gather(g_attn, ("dp", "ctx"), axis=0, tiled=True)
    query_piece = lax.all_gather(w_query, ("dp", "ctx"), axis=0, tiled=True)
    key_piece = lax.all_gather(w_key, ("dp", "ctx"), axis=0, tiled=True)
    value_piece = lax.all_gather(w_value, ("dp", "ctx"), axis=0, tiled=True)
    length = gain_piece.shape[0]
    scaled = (nrm_one * gain_piece.astype(jnp.float32)).astype(jnp.bfloat16)
    q_raw = mul_plain(scaled, query_piece)
    k_raw = mul_plain(scaled, key_piece)
    v_raw = mul_plain(scaled, value_piece)
    xn_one = scaled
    query_low = rotate(q_raw.reshape(tok_rows, H, HD), cosine, sine_table).astype(jnp.bfloat16)
    query_low = query_low.reshape(tok_rows, KVH, head_group, HD)
    key_low = (
        rotate(k_raw.reshape(tok_rows, KVH, HD), cosine, sine_table)
        .astype(jnp.bfloat16)
        .reshape(tok_rows, key_width)
    )
    value_low = v_raw.astype(jnp.bfloat16)
    key_all, value_all = (
        lax.all_gather(key_low, "ctx", axis=0, tiled=True),
        lax.all_gather(value_low, "ctx", axis=0, tiled=True),
    )
    keys_heads = key_all.reshape(key_span, KVH, HD)
    values_heads = value_all.reshape(key_span, KVH, HD)
    scores = (
        jnp.einsum("tkgd,skd->kgts", query_low, keys_heads, preferred_element_type=jnp.float32)
        * score_scale
    )
    scores = jnp.where(visible(0, key_span), scores, NEG)
    row_max = jnp.max(scores, axis=-1, keepdims=True)
    log_total = row_max + jnp.log(jnp.sum(jnp.exp(scores - row_max), axis=-1, keepdims=True))
    prob_low = jnp.exp(scores - log_total).astype(jnp.bfloat16)
    attn_o = jnp.einsum(
        "kgts,skd->tkgd", prob_low, values_heads, preferred_element_type=jnp.float32
    )
    attn_o = attn_o.reshape(tok_rows, query_width).astype(jnp.bfloat16)
    attn_out = mul_plain(attn_o, lax.all_gather(w_output, ("dp", "ctx"), axis=0, tiled=True))
    hid_res = tok_in + attn_out
    nrm_two = normalize(hid_res)
    gain_piece = lax.all_gather(g_mlp, ("dp", "ctx"), axis=0, tiled=True)
    gate_piece = lax.all_gather(w_gate, ("dp", "ctx"), axis=0, tiled=True)
    up_piece = lax.all_gather(w_up, ("dp", "ctx"), axis=0, tiled=True)
    length = gain_piece.shape[0]
    scaled = (nrm_two * gain_piece.astype(jnp.float32)).astype(jnp.bfloat16)
    gate = mul_plain(scaled, gate_piece)
    up_val = mul_plain(scaled, up_piece)
    sigmoid_gate = jax.nn.sigmoid(gate)
    hidden = (gate * sigmoid_gate * up_val).astype(jnp.bfloat16)
    mlp_out = mul_plain(hidden, lax.all_gather(w_down, ("dp", "ctx"), axis=0, tiled=True))
    result = (hid_res + mlp_out).astype(jnp.bfloat16)[None]
    grad_y = cotangent[0]
    grad_hidden = mul_right(grad_y, lax.all_gather(w_down, ("dp", "ctx"), axis=0, tiled=True))
    grad_gate_low = (
        grad_hidden * up_val * sigmoid_gate * (1.0 + gate * (1.0 - sigmoid_gate))
    ).astype(jnp.bfloat16)
    grad_up_low = (grad_hidden * gate * sigmoid_gate).astype(jnp.bfloat16)
    gain_piece = lax.all_gather(g_mlp, ("dp", "ctx"), axis=0, tiled=True)
    gate_piece = lax.all_gather(w_gate, ("dp", "ctx"), axis=0, tiled=True)
    up_piece = lax.all_gather(w_up, ("dp", "ctx"), axis=0, tiled=True)
    summed = mul_right(grad_gate_low, gate_piece) + mul_right(grad_up_low, up_piece)
    stacked = jnp.stack((summed * gain_piece.astype(jnp.float32), summed))
    mlp_pair = stacked
    gain_two_grad = jnp.sum(mlp_pair[1] * nrm_two, axis=0)
    d_res = grad_y.astype(jnp.float32) + norm_back(hid_res, nrm_two, mlp_pair[0])
    gate_up_low = jnp.concatenate((grad_gate_low, grad_up_low), axis=1)
    gate_up_grad = lax.psum_scatter(
        mul_left(scaled, gate_up_low), ("dp", "ctx"), scatter_dimension=0, tiled=True
    )
    down_grad = lax.psum_scatter(
        mul_left(hidden, grad_y), ("dp", "ctx"), scatter_dimension=0, tiled=True
    )
    d_res_low = d_res.astype(jnp.bfloat16)
    grad_attn = mul_right(d_res_low, lax.all_gather(w_output, ("dp", "ctx"), axis=0, tiled=True))
    grad_attn_low = grad_attn.astype(jnp.bfloat16).reshape(tok_rows, KVH, head_group, HD)

    def block_parts(block_id):
        key_first = block_id * KEYBLK
        key_block = lax.dynamic_slice_in_dim(keys_heads, key_first, KEYBLK, 0)
        value_block = lax.dynamic_slice_in_dim(values_heads, key_first, KEYBLK, 0)
        block_scores = (
            jnp.einsum("tkgd,skd->kgts", query_low, key_block, preferred_element_type=jnp.float32)
            * score_scale
        )
        block_scores = jnp.where(visible(key_first, KEYBLK), block_scores, NEG)
        prob_full = jnp.exp(block_scores - log_total)
        grad_prob = jnp.einsum(
            "tkgd,skd->kgts", grad_attn_low, value_block, preferred_element_type=jnp.float32
        )
        return (key_block, prob_full, grad_prob)

    def delta_step(summed, block_id):
        unused_keys, prob_full, grad_prob = block_parts(block_id)
        return (summed + jnp.sum(prob_full * grad_prob, axis=-1, keepdims=True), None)

    row_delta, unused_out = lax.scan(
        delta_step, jnp.zeros(log_total.shape, jnp.float32), lax.iota(jnp.int32, key_blocks)
    )

    def grad_step(grad_query, block_id):
        key_block, prob_full, grad_prob = block_parts(block_id)
        grad_score = (prob_full * (grad_prob - row_delta)).astype(jnp.bfloat16)
        grad_query = (
            grad_query
            + jnp.einsum(
                "kgts,skd->tkgd", grad_score, key_block, preferred_element_type=jnp.float32
            )
            * score_scale
        )
        grad_key_block = (
            jnp.einsum("kgts,tkgd->skd", grad_score, query_low, preferred_element_type=jnp.float32)
            * score_scale
        )
        grad_value_block = jnp.einsum(
            "kgts,tkgd->skd",
            prob_full.astype(jnp.bfloat16),
            grad_attn_low,
            preferred_element_type=jnp.float32,
        )
        return (
            grad_query,
            (
                grad_key_block.reshape(KEYBLK, key_width),
                grad_value_block.reshape(KEYBLK, key_width),
            ),
        )

    grad_query, block_grads = lax.scan(
        grad_step,
        jnp.zeros((tok_rows, KVH, head_group, HD), jnp.float32),
        lax.iota(jnp.int32, key_blocks),
    )
    keys_grad_all = block_grads[0].reshape(key_span, key_width)
    values_grad_all = block_grads[1].reshape(key_span, key_width)
    key_grad_own, value_grad_own = (
        lax.psum_scatter(
            keys_grad_all.astype(jnp.bfloat16), "ctx", scatter_dimension=0, tiled=True
        ).astype(jnp.float32),
        lax.psum_scatter(
            values_grad_all.astype(jnp.bfloat16), "ctx", scatter_dimension=0, tiled=True
        ).astype(jnp.float32),
    )
    query_grad_low = rotate(grad_query.reshape(tok_rows, H, HD), cosine, -sine_table).astype(
        jnp.bfloat16
    )
    query_grad_low = query_grad_low.reshape(tok_rows, query_width)
    key_grad_low = rotate(key_grad_own.reshape(tok_rows, KVH, HD), cosine, -sine_table).astype(
        jnp.bfloat16
    )
    key_grad_low = key_grad_low.reshape(tok_rows, key_width)
    value_grad_low = value_grad_own.astype(jnp.bfloat16)
    gain_piece = lax.all_gather(g_attn, ("dp", "ctx"), axis=0, tiled=True)
    query_piece = lax.all_gather(w_query, ("dp", "ctx"), axis=0, tiled=True)
    key_piece = lax.all_gather(w_key, ("dp", "ctx"), axis=0, tiled=True)
    value_piece = lax.all_gather(w_value, ("dp", "ctx"), axis=0, tiled=True)
    summed = (
        mul_right(query_grad_low, query_piece)
        + mul_right(key_grad_low, key_piece)
        + mul_right(value_grad_low, value_piece)
    )
    stacked = jnp.stack((summed * gain_piece.astype(jnp.float32), summed))
    gain_one_grad = jnp.sum(stacked[1] * nrm_one, axis=0)
    input_grad = (d_res + norm_back(tok_in, nrm_one, stacked[0])).astype(jnp.bfloat16)[None]
    qkv_grad_low = jnp.concatenate((query_grad_low, key_grad_low, value_grad_low), axis=1)
    first_part = mul_left(xn_one, qkv_grad_low)
    second_part = mul_left(attn_o, d_res_low)
    attn_grad = lax.psum_scatter(
        jnp.concatenate((first_part, second_part), axis=1),
        ("dp", "ctx"),
        scatter_dimension=0,
        tiled=True,
    )
    gain_grads = (
        lax.psum_scatter(gain_one_grad, ("dp", "ctx"), scatter_dimension=0, tiled=True),
        lax.psum_scatter(gain_two_grad, ("dp", "ctx"), scatter_dimension=0, tiled=True),
    )
    return (
        result,
        input_grad,
        gain_grads[0],
        attn_grad[:, :query_width],
        attn_grad[:, query_width : query_width + key_width],
        attn_grad[:, query_width + key_width : query_width + 2 * key_width],
        attn_grad[:, query_width + 2 * key_width :],
        gain_grads[1],
        gate_up_grad[:, :FF],
        gate_up_grad[:, FF:],
        down_grad,
    )


def solution(mesh):
    in_specs = (
        P("dp", "ctx", None),
        P("dp"),
        P(("dp", "ctx")),
        P(("dp", "ctx"), None),
        P(("dp", "ctx"), None),
        P(("dp", "ctx"), None),
        P(("dp", "ctx"), None),
        P(("dp", "ctx")),
        P(("dp", "ctx"), None),
        P(("dp", "ctx"), None),
        P(("dp", "ctx"), None),
        P("dp", "ctx", None),
    )
    out_specs = (
        P("dp", "ctx", None),
        P("dp", "ctx", None),
        P(("dp", "ctx")),
        P(("dp", "ctx"), None),
        P(("dp", "ctx"), None),
        P(("dp", "ctx"), None),
        P(("dp", "ctx"), None),
        P(("dp", "ctx")),
        P(("dp", "ctx"), None),
        P(("dp", "ctx"), None),
        P(("dp", "ctx"), None),
    )
    return jax.shard_map(
        per_device, mesh=mesh, in_specs=in_specs, out_specs=out_specs, check_vma=False
    )
```

profile of v0, /device:TPU:8, one launch (start us, length us, event | category | flops | bytes accessed | tf_op | source)
XLA Modules:
  0.0 4225.9 jit_solution(6816871058698533725)
XLA Ops:
  10.4 40.7 all-reduce.6
  52.5 21.8 all-gather.10.cloned.1.call-done
  74.3 4.2 convolution_convert_fusion.1
  79.8 58.2 %all-gather.14.cloned.1.call-done = bf16[2048,1024]{1,0:T(8,128)(2,1)} async-done(((bf16[64,1024]{1,0:T(8,128)(2,1)}), bf16[2048,1024]{1,0:T(8,128)(2,1)}) %all-gather.14.cloned.1.call-update) | async-done | bytes 4194320 | tf_op jit(solution)/shard_map/all_gather | solution.py:94
  138.0 6.6 copy.54
  144.5 3.9 fusion.96
  153.9 22.2 all-gather.12.cloned.1.call-done
  176.2 3.7 copy.118
  179.9 35.5 all-gather.16.cloned.1.call-done
  215.4 4.9 copy.56
  220.3 4.7 copy.64
  225.0 6.2 reshape.212
  231.2 64.4 %all-gather.18.cloned.1.call-done = bf16[2048,2048]{1,0:T(8,128)(2,1)} async-done(((bf16[64,2048]{1,0:T(8,128)(2,1)}), bf16[2048,2048]{1,0:T(8,128)(2,1)}) %all-gather.18.cloned.1.call-update) | async-done | bytes 8388624 | tf_op jit(solution)/shard_map/all_gather | solution.py:93
  295.5 12.3 copy.57
  307.9 6.3 fusion.94
  316.1 2.0 fusion.38
  318.1 2.6 exponential_reduce_fusion
  320.7 2.6 fusion.78
  325.6 48.8 %all-gather.20.cloned.1.call-done = bf16[2048,2048]{1,0:T(8,128)(2,1)} async-done(((bf16[64,2048]{1,0:T(8,128)(2,1)}), bf16[2048,2048]{1,0:T(8,128)(2,1)}) %all-gather.20.cloned.1.call-update) | async-done | bytes 8388624 | tf_op jit(solution)/shard_map/all_gather | solution.py:128
  374.4 5.6 multiply_reduce_fusion.2
  380.2 188.7 %all-gather.24.cloned.1.call-done = bf16[2048,8192]{1,0:T(8,128)(2,1)} async-done(((bf16[64,8192]{1,0:T(8,128)(2,1)}), bf16[2048,8192]{1,0:T(8,128)(2,1)}) %all-gather.24.cloned.1.call-update) | async-done | bytes 33554448 | tf_op jit(solution)/shard_map/all_gather | solution.py:133
  568.9 16.8 fusion.111
  585.8 179.1 %all-gather.22.cloned.1.call-done = bf16[2048,8192]{1,0:T(8,128)(2,1)} async-done(((bf16[64,8192]{1,0:T(8,128)(2,1)}), bf16[2048,8192]{1,0:T(8,128)(2,1)}) %all-gather.22.cloned.1.call-update) | async-done | bytes 33554448 | tf_op jit(solution)/shard_map/all_gather | solution.py:132
  764.9 17.0 fusion.110
  781.9 179.0 %all-gather.26.cloned.1.call-done = bf16[8192,2048]{1,0:T(8,128)(2,1)} async-done(((bf16[256,2048]{1,0:T(8,128)(2,1)}), bf16[8192,2048]{1,0:T(8,128)(2,1)}) %all-gather.26.cloned.1.call-update) | async-done | bytes 33554448 | tf_op jit(solution)/shard_map/all_gather | solution.py:140
  960.9 21.1 multiply_convert_fusion
  982.0 18.3 fusion.112
  1000.3 19.8 multiply_reduce_fusion
  1023.1 6.3 convolution_convert_fusion
  1031.0 19.8 while.26
  1035.0 2.7 fusion.178
  1041.6 2.7 fusion.178
  1046.3 1.8 fusion.177
  1048.2 2.7 fusion.178
  1050.9 57.9 %while.27 = (s32[]{:T(128)}, f32[192,4,2,256]{3,0,2,1:T(8,128)}, bf16[3,512,1024]{2,1,0:T(8,128)(2,1)}, bf16[3,512,1024]{2,1,0:T(8,128)(2,1)}, s32[3]{0:T(128)S(...) while((s32[]{:T(128)}, f32[192,4,2,256]{3,0,2,1:T(8,128)}, ...), condition=%wide.region_9.10_spmd.clone, body=%wide.region_8.9_spmd.clone.sunk | while | flops 2023556864 | bytes 34398984 | solution.py:218
  1055.0 3.3 fusion.192
  1058.2 2.5 fusion.191
  1064.0 3.0 bitcast_add_fusion.2
  1072.0 1.8 fusion.190
  1073.9 3.3 fusion.192
  1077.1 2.5 fusion.191
  1082.9 3.5 bitcast_add_fusion.2
  1093.2 3.3 fusion.192
  1096.5 2.5 fusion.191
  1102.3 3.5 bitcast_add_fusion.2
  1109.9 47.5 %fusion.39 = f32[2048,16384]{1,0:T(8,128)} fusion(bf16[192,2048]{1,0:T(8,128)(2,1)S(1)} %copy-done.15, bf16[192,8192]{1,0:T(8,128)(2,1)} %get-tuple-element.344, bf16[192,8192]{1,0:T(8,128)(2,1)} %copy-done.20), kind=kOutput, calls=%fused_computation.57 | convolution fusion | flops 12897484800 | bytes 141295616 | tf_op jit(solution)/shard_map/dot_general | solution.py:29
  1160.3 2.6 copy.68
  1163.0 2.4 reshape.217
  1170.6 8.2 fusion.91
  1181.4 5.2 reduce-scatter.7.cloned.1.call-done
  1186.6 14.5 fusion.69
  1201.1 35.5 pad_maximum_fusion
  1237.7 28.1 fusion.86
  1267.0 6.7 fusion.113
  1273.7 16.3 fusion.50
  1292.3 2.9 fusion.63
  1295.2 45.7 %all-reduce.5 = (f32[2048]{0:T(1024)S(1)}, f32[2048]{0:T(1024)S(1)}) all-reduce(f32[2048]{0:T(1024)S(1)} %get-tuple-element.288, f32[2048]{0:T(1024)S(1)} %copy-done.29), channel_id=4, replica_groups=mesh['dp'=4,'ctx'=8] {'dp','ctx'}, use_global_device_ids=true, to_apply=%region_14.15.clone | all-reduce | flops 4096 | bytes 32768
  1342.1 2.7 fusion.83
  1344.8 1729.6 %all-reduce.9.cloned.1.call-done = f32[2048,16384]{1,0:T(8,128)} async-done(((f32[2048,16384]{1,0:T(8,128)}), f32[2048,16384]{1,0:T(8,128)}) %all-reduce.9.cloned.1.call-update) | async-done | bytes 134217744
  3074.4 4.9 fusion.106
  3079.3 431.7 %reduce-scatter.9.cloned.1.call-done = f32[64,6144]{1,0:T(8,128)} async-done(((f32[2048,6144]{1,0:T(8,128)}), f32[64,6144]{1,0:T(8,128)}) %reduce-scatter.9.cloned.1.call-update) | async-done | bytes 1572880 | tf_op jit(solution)/shard_map/reduce_scatter | solution.py:257
  3511.0 1.9 fusion.108
  3512.9 2.3 fusion.107
  3515.2 703.7 %reduce-scatter.11.cloned.1.call-done = f32[256,2048]{1,0:T(8,128)} async-done(((f32[8192,2048]{1,0:T(8,128)}), f32[256,2048]{1,0:T(8,128)}) %reduce-scatter.11.cloned.1.call-update) | async-done | bytes 2097168 | tf_op jit(solution)/shard_map/reduce_scatter | solution.py:160
  (194 shorter events, 71.4 us)
Async XLA Ops:
  7.2 67.1 %all-gather.10.cloned.1.call-start = ((), (), s32[]{:S(2)}) async-start(), calls=%async_computation.4 | async-start | bytes 4325376 | tf_op jit(solution)/shard_map/all_gather | solution.py:95
  7.9 130.1 %all-gather.14.cloned.1.call-start = ((), (), s32[]{:S(2)}) async-start(), calls=%async_computation.6 | async-start | bytes 4325376 | tf_op jit(solution)/shard_map/all_gather | solution.py:94
  8.7 167.5 %all-gather.12.cloned.1.call-start = ((), (), s32[]{:S(2)}) async-start(), calls=%async_computation.5 | async-start | bytes 3538944 | tf_op jit(solution)/shard_map/all_gather | solution.py:112
  51.1 256.8 %copy-start.25 = (f32[2048]{0:T(1024)}, f32[2048]{0:T(1024)S(1)}, u32[]{:S(2)}) copy-start(f32[2048]{0:T(1024)S(1)} %convert_element_type.115) | copy-start | bytes 24580
  52.5 255.4 %copy-start.27 = (f32[192]{0:T(256)}, f32[192]{0:T(256)S(1)}, u32[]{:S(2)}) copy-start(f32[192]{0:T(256)S(1)} %add_rsqrt_fusion.1) | copy-start | bytes 2308
  78.5 136.9 %all-gather.16.cloned.1.call-start = ((), (), s32[]{:S(2)}) async-start(), calls=%async_computation.7 | async-start | bytes 3538944 | tf_op jit(solution)/shard_map/all_gather | solution.py:111
  79.0 235.3 %copy-start.9 = (f32[192,256]{1,0:T(8,128)}, f32[192,256]{1,0:T(8,128)S(1)}, u32[]{:S(2)}) copy-start(f32[192,256]{1,0:T(8,128)S(1)} %pad_maximum_fusion.1) | copy-start | bytes 589828
  138.0 6.6 copy-start.3
  149.5 146.0 %all-gather.18.cloned.1.call-start = ((), (), s32[]{:S(2)}) async-start(), calls=%async_computation.8 | async-start | bytes 8650752 | tf_op jit(solution)/shard_map/all_gather | solution.py:93
  150.1 224.3 %all-gather.20.cloned.1.call-start = ((), (), s32[]{:S(2)}) async-start(), calls=%async_computation.9 | async-start | bytes 8650752 | tf_op jit(solution)/shard_map/all_gather | solution.py:128
  150.7 418.2 %all-gather.24.cloned.1.call-start = ((), (), s32[]{:S(2)}) async-start(), calls=%async_computation.11 | async-start | bytes 34603008 | tf_op jit(solution)/shard_map/all_gather | solution.py:133
  151.4 613.5 %all-gather.22.cloned.1.call-start = ((), (), s32[]{:S(2)}) async-start(), calls=%async_computation.10 | async-start | bytes 34603008 | tf_op jit(solution)/shard_map/all_gather | solution.py:132
  152.2 808.7 %all-gather.26.cloned.1.call-start = ((), (), s32[]{:S(2)}) async-start(), calls=%async_computation.12 | async-start | bytes 34603008 | tf_op jit(solution)/shard_map/all_gather | solution.py:140
  152.9 1025.8 %reduce-scatter.5.cloned.1.call-start = ((), (), s32[]{:S(2)}) async-start(), calls=%async_computation.13 | async-start | bytes 3538944 | tf_op jit(solution)/shard_map/reduce_scatter | solution.py:226
  314.2 1.9 copy-start.5
  318.1 2.6 copy-start.17
  380.0 640.1 %copy-start.7 = (f32[192,2048]{1,0:T(8,128)}, f32[192,2048]{1,0:T(8,128)S(1)}, u32[]{:S(2)}) copy-start(f32[192,2048]{1,0:T(8,128)S(1)} %get-tuple-element.366) | copy-start | bytes 4718596
  380.2 188.7 %copy-start.14 = (bf16[192,2048]{1,0:T(8,128)(2,1)}, bf16[192,2048]{1,0:T(8,128)(2,1)S(1)}, u32[]{:S(2)}) copy-start(bf16[192,2048]{1,0:T(8,128)(2,1)S(1)} %multiply_convert_fusion.3) | copy-start | bytes 2359300
  585.8 375.1 %copy-start.12 = (bf16[1,192,2048]{2,1,0:T(8,128)(2,1)S(1)}, bf16[1,192,2048]{2,1,0:T(8,128)(2,1)}, u32[]{:S(2)}) copy-start(bf16[1,192,2048]{2,1,0:T(8,128)(2,1)} %param.27) | copy-start | bytes 2359300
  982.0 18.3 copy-start.20
  1022.0 1.1 copy-start.1
  1108.8 1.1 copy-start.15
  1108.8 77.7 %reduce-scatter.7.cloned.1.call-start = ((), (), s32[]{:S(2)}) async-start(), calls=%async_computation.14 | async-start | bytes 3538944 | tf_op jit(solution)/shard_map/reduce_scatter | solution.py:229
  1109.5 1964.9 %all-reduce.9.cloned.1.call-start = ((), (), s32[]{:S(2)}) async-start(), calls=%async_computation.17 | async-start | bytes 268435456
  1157.5 0.9 copy-start.10
  1157.5 2353.6 %reduce-scatter.9.cloned.1.call-start = ((), (), s32[]{:S(2)}) async-start(), calls=%async_computation.15 | async-start | bytes 51904512 | tf_op jit(solution)/shard_map/reduce_scatter | solution.py:257
  1165.4 2.5 copy-start.21
  1168.0 1.4 copy-start.6
  1168.8 1.8 copy-start.2
  1168.8 1.8 copy-start.16
  1170.6 9.8 copy-start.22
  1178.8 2.1 copy-start.18
  1180.2 1.0 copy-start.24
  1180.4 6.2 copy-start.4
  1180.4 6.2 copy-start.26
  1180.4 6.2 copy-start.28
  1236.6 1.1 copy-start.13
  1236.6 2982.3 %reduce-scatter.11.cloned.1.call-start = ((), (), s32[]{:S(2)}) async-start(), calls=%async_computation.16 | async-start | bytes 69206016 | tf_op jit(solution)/shard_map/reduce_scatter | solution.py:160
  1265.8 1.1 copy-start.19
  1267.0 6.7 copy-start.8
  1273.6 16.3 copy-start
  1289.9 2.3 copy-start.11
  1289.9 2.4 copy-start.23
  1292.3 2.9 copy-start.29
Sparse Core Ops, SparseCore 0:
  11.0 63.1 all-gather.9
  77.3 60.6 all-gather.13
  140.2 35.9 all-gather.11
  178.2 37.1 all-gather.15
  218.2 77.2 all-gather.17
  298.4 75.9 all-gather.19
  377.4 191.4 all-gather.23
  571.9 192.9 all-gather.21
  767.9 192.9 all-gather.25
  1108.9 35.8 reduce-scatter.4
  1147.2 39.3 reduce-scatter.6
  1192.8 1881.5 all-reduce.8
  3080.9 430.1 reduce-scatter.8
  3513.8 705.0 reduce-scatter.10
where the time goes:
time: 4240 us; the launch traced here: 4230 us
  waiting for transfers between devices  3670 us (87%)
  matrix products  301 us (7%)
  local copies, waits for them, and re-layouts  90.8 us (2%)
  blocking collectives  86.4 us (2%)
  other arithmetic  53.8 us (1%)
    unnamed x15, waiting for transfers between devices  1730 us
    reduce_scatter x1, waiting for transfers between devices, per_device(): lax.psum_scatter(mul_left(hidden, grad_y), ('dp', 'ctx'), scatter_dimensi...  704 us
    reduce_scatter x1, waiting for transfers between devices, per_device(): lax.psum_scatter(jnp.concatenate((first_part, second_part), axis=1), ('dp...  432 us
    all_gather x1, waiting for transfers between devices, per_device(): up_piece = lax.all_gather(w_up, ('dp', 'ctx'), axis=0, tiled=True)  189 us
    all_gather x1, waiting for transfers between devices, per_device(): gate_piece = lax.all_gather(w_gate, ('dp', 'ctx'), axis=0, tiled=True)  179 us
    all_gather x1, waiting for transfers between devices, per_device(): lax.all_gather(w_down, ('dp', 'ctx'), axis=0, tiled=True)  179 us
    dot_general x4, matrix products, mul_left(): lax.dot_general(first_op, second_op, (((0,), (0,)), ((), ())), preferred_...  98.3 us
    unnamed x2, blocking collectives  86.4 us
  transfers between devices with their start and end apart: 14, of which 13 were waited for; matrix products, arithmetic and copies ran while one was open for 7% of the time, Pallas kernels for 0%

commit v1 on v0

--- a/solution.py
+++ b/solution.py
@@ -57,7 +57,7 @@
     return values * cosine[:, None, :] + rolled * sine_table[:, None, :]
 
 
-def per_device(
+def gathered_weights(
     tokens,
     prefix,
     g_attn,
@@ -279,34 +279,179 @@
     )
 
 
+def scatter_ctx(values):
+    return lax.psum_scatter(values, "ctx", scatter_dimension=0, tiled=True)
+
+
+def gather_ctx(values):
+    return lax.all_gather(values, "ctx", axis=0, tiled=True)
+
+
+def swap_ctx(values):
+    return lax.all_to_all(values, "ctx", split_axis=0, concat_axis=0, tiled=True)
+
+
+def head_split(
+    tokens,
+    prefix,
+    g_attn,
+    w_query,
+    w_key,
+    w_value,
+    w_output,
+    g_mlp,
+    w_gate,
+    w_up,
+    w_down,
+    cotangent,
+):
+    bf16, f32 = jnp.bfloat16, jnp.float32
+    groups, pieces = lax.axis_size("ctx"), lax.axis_size("dp")
+    tok_rows, width = tokens.shape[1:]
+    span = groups * tok_rows
+    shard = w_query.shape[0]
+    share = w_down.shape[0]
+    per_key = H // KVH
+
+    tok_in = tokens[0].astype(f32)
+    gain_one, gain_two = g_attn.astype(f32)[:, None], g_mlp.astype(f32)[:, None]
+
+    q_cols = (gain_one * w_query).astype(bf16).reshape(shard, H, HD)
+    k_cols = jnp.repeat((gain_one * w_key).astype(bf16).reshape(shard, KVH, HD), per_key, axis=1)
+    v_cols = jnp.repeat((gain_one * w_value).astype(bf16).reshape(shard, KVH, HD), per_key, axis=1)
+    qkv_cols = jnp.concatenate((q_cols, k_cols, v_cols), axis=2).transpose(1, 0, 2)
+    qkv_w = lax.all_gather(
+        swap_ctx(qkv_cols).reshape(groups * shard, 3 * HD), "dp", axis=0, tiled=True
+    )
+    tok_all = gather_ctx(tokens[0])
+    xn_one = normalize(tok_all.astype(f32)).astype(bf16)
+    qkv = mul_plain(xn_one, qkv_w)
+
+    def gated(weight):
+        scaled = (gain_two * weight).astype(bf16).reshape(shard, pieces, groups, share)
+        return scaled.transpose(2, 0, 1, 3).reshape(groups, shard, pieces * share)
+
+    gate_up_w = lax.all_gather(
+        swap_ctx(jnp.concatenate((gated(w_gate), gated(w_up)), axis=2)).reshape(
+            groups * shard, 2 * pieces * share
+        ),
+        "dp",
+        axis=0,
+        tiled=True,
+    )
+    down_w = lax.all_gather(w_down, "dp", axis=0, tiled=True)
+    output_w = lax.all_gather(w_output, ("dp", "ctx"), axis=0, tiled=True)
+
+    cosine, sine = rotary(0, span, HD)
+
+    def turn(values, sine_table):
+        half = HD // 2
+        rolled = jnp.concatenate((-values[:, half:], values[:, :half]), axis=-1)
+        return values * cosine + rolled * sine_table
+
+    query = turn(qkv[:, :HD], sine).astype(bf16)
+    key = turn(qkv[:, HD : 2 * HD], sine).astype(bf16)
+    value = qkv[:, 2 * HD :].astype(bf16)
+    scores = mul_right(query, key) * HD ** (-0.5)
+    pos = lax.iota(jnp.int32, span)
+    seen = (pos[None, :] <= pos[:, None]) | (pos[None, :] < prefix[0])
+    scores = jnp.where(seen, scores, NEG)
+    prob = jax.nn.softmax(scores, axis=-1)
+    prob_low = prob.astype(bf16)
+    head_o = mul_plain(prob_low, value)
+
+    attn_o = swap_ctx(head_o.astype(bf16).reshape(groups, tok_rows, HD))
+    attn_o = attn_o.transpose(1, 0, 2).reshape(tok_rows, H * HD)
+    hid_res = tok_in + mul_plain(attn_o, output_w)
+    nrm_two = normalize(hid_res)
+    xn_two = gather_ctx(nrm_two.astype(bf16))
+    gate_up = mul_plain(xn_two, gate_up_w)
+    gate, up_val = gate_up[:, : pieces * share], gate_up[:, pieces * share :]
+    sigmoid_gate = jax.nn.sigmoid(gate)
+    hidden = (gate * sigmoid_gate * up_val).astype(bf16)
+    result = hid_res + scatter_ctx(mul_plain(hidden, down_w).astype(bf16)).astype(f32)
+    result = result.astype(bf16)[None]
+
+    dy_all = gather_ctx(cotangent[0])
+    d_hidden = mul_right(dy_all, down_w)
+    d_gate = d_hidden * up_val * sigmoid_gate * (1.0 + gate * (1.0 - sigmoid_gate))
+    d_up = d_hidden * gate * sigmoid_gate
+    d_gate_up = jnp.concatenate((d_gate.astype(bf16), d_up.astype(bf16)), axis=1)
+    dn_two = scatter_ctx(mul_right(d_gate_up, gate_up_w).astype(bf16)).astype(f32)
+    d_res = cotangent[0].astype(f32) + norm_back(hid_res, nrm_two, dn_two)
+    d_res_low = d_res.astype(bf16)
+
+    def scatter_dp(values):
+        return lax.psum_scatter(values.astype(bf16), "dp", scatter_dimension=0, tiled=True)
+
+    down_grad = scatter_dp(mul_left(hidden, dy_all)).astype(f32)
+    gate_up_sum = swap_ctx(
+        scatter_dp(mul_left(xn_two, d_gate_up)).reshape(groups, shard, 2 * pieces * share)
+    ).astype(f32)
+
+    def ungated(summed):
+        return summed.reshape(groups, shard, pieces, share).transpose(1, 2, 0, 3).reshape(shard, FF)
+
+    gate_sum = ungated(gate_up_sum[:, :, : pieces * share])
+    up_sum = ungated(gate_up_sum[:, :, pieces * share :])
+    gain_two_grad = jnp.sum(w_gate * gate_sum + w_up * up_sum, axis=1)
+
+    d_attn = mul_right(d_res_low, output_w).astype(bf16)
+    d_head = swap_ctx(d_attn.reshape(tok_rows, groups, HD).transpose(1, 0, 2)).reshape(span, HD)
+    output_grad = lax.psum_scatter(
+        mul_left(attn_o, d_res_low).astype(bf16), ("dp", "ctx"), scatter_dimension=0, tiled=True
+    ).astype(f32)
+
+    d_prob = mul_right(d_head, value)
+    row_delta = jnp.sum(prob * d_prob, axis=-1, keepdims=True)
+    d_score = (prob * (d_prob - row_delta)).astype(bf16)
+    d_query = turn(mul_plain(d_score, key) * HD ** (-0.5), -sine)
+    d_key = turn(mul_left(d_score, query) * HD ** (-0.5), -sine)
+    d_value = mul_left(prob_low, d_head)
+    d_qkv = jnp.concatenate((d_query, d_key, d_value), axis=1).astype(bf16)
+    dn_one = scatter_ctx(mul_right(d_qkv, qkv_w).astype(bf16)).astype(f32)
+    input_grad = d_res + norm_back(tok_in, normalize(tok_in), dn_one)
+    input_grad = input_grad.astype(bf16)[None]
+
+    qkv_sum = swap_ctx(scatter_dp(mul_left(xn_one, d_qkv)).reshape(groups, shard, 3 * HD))
+    qkv_sum = qkv_sum.astype(f32).transpose(1, 0, 2)
+    q_sum = qkv_sum[:, :, :HD].reshape(shard, H * HD)
+
+    def per_group(summed):
+        return jnp.sum(summed.reshape(shard, KVH, per_key, HD), axis=2).reshape(shard, KVH * HD)
+
+    k_sum = per_group(qkv_sum[:, :, HD : 2 * HD])
+    v_sum = per_group(qkv_sum[:, :, 2 * HD :])
+    gain_one_grad = (
+        jnp.sum(w_query * q_sum, axis=1)
+        + jnp.sum(w_key * k_sum, axis=1)
+        + jnp.sum(w_value * v_sum, axis=1)
+    )
+    return (
+        result,
+        input_grad,
+        gain_one_grad,
+        gain_one * q_sum,
+        gain_one * k_sum,
+        gain_one * v_sum,
+        output_grad,
+        gain_two_grad,
+        gain_two * gate_sum,
+        gain_two * up_sum,
+        down_grad,
+    )
+
+
 def solution(mesh):
-    in_specs = (
-        P("dp", "ctx", None),
-        P("dp"),
-        P(("dp", "ctx")),
-        P(("dp", "ctx"), None),
-        P(("dp", "ctx"), None),
-        P(("dp", "ctx"), None),
-        P(("dp", "ctx"), None),
-        P(("dp", "ctx")),
-        P(("dp", "ctx"), None),
-        P(("dp", "ctx"), None),
-        P(("dp", "ctx"), None),
-        P("dp", "ctx", None),
-    )
-    out_specs = (
-        P("dp", "ctx", None),
-        P("dp", "ctx", None),
-        P(("dp", "ctx")),
-        P(("dp", "ctx"), None),
-        P(("dp", "ctx"), None),
-        P(("dp", "ctx"), None),
-        P(("dp", "ctx"), None),
-        P(("dp", "ctx")),
-        P(("dp", "ctx"), None),
-        P(("dp", "ctx"), None),
-        P(("dp", "ctx"), None),
-    )
+    one_head_each = mesh.shape["ctx"] == H
+    rows, whole = P(("dp", "ctx")), P(("dp", "ctx"), None)
+    acts = P("dp", "ctx", None)
+    in_specs = (acts, P("dp"), rows, whole, whole, whole, whole, rows, whole, whole, whole, acts)
+    out_specs = (acts, acts, rows, whole, whole, whole, whole, rows, whole, whole, whole)
     return jax.shard_map(
-        per_device, mesh=mesh, in_specs=in_specs, out_specs=out_specs, check_vma=False
-    )
+        head_split if one_head_each else gathered_weights,
+        mesh=mesh,
+        in_specs=in_specs,
+        out_specs=out_specs,
+        check_vma=False,
+    )

time: 4240 us -> 1140 us (0.27)
  waiting for transfers between devices: 3670 us -> 703 us
  matrix products: 301 us -> 154 us
  blocking collectives: 86.4 us -> 174 us
  local copies, waits for them, and re-layouts: 90.8 us -> 27.8 us
    unnamed x15 -> x14, waiting for transfers between devices: 1730 us -> 2.74 us
    reduce_scatter x4 -> x7, waiting for transfers between devices: 1140 us -> 386 us  [the longest x3 151 us: scatter_ctx(): return lax.psum_scatter(values, 'ctx', scatter_dimension=0, tiled=True)]
    all_gather x9 -> x7, waiting for transfers between devices: 798 us -> 311 us  [the longest x3 129 us: gather_ctx(): return lax.all_gather(values, 'ctx', axis=0, tiled=True)]
    all_to_all x0 -> x4, blocking collectives: none -> 174 us  [swap_ctx(): lax.all_to_all(values, 'ctx', split_axis=0, concat_axis=0, tiled=True)]
    unnamed x2 -> x0, blocking collectives: 86.4 us -> none
    dot_general x23 -> x0, matrix products: 56 us -> none  [the longest x6 15.5 us: block_parts(): jnp.einsum('tkgd,skd->kgts', grad_attn_low, value_block, preferred_elemen...]
    dot_general x4 -> x6, matrix products: 98.3 us -> 47.8 us  [mul_left(): lax.dot_general(first_op, second_op, (((0,), (0,)), ((), ())), preferred_...]
  transfers between devices with their start and end apart: 14 -> 16, of which waited for: 13 -> 14; matrix products, arithmetic and copies ran while one was open for 7% -> 15% of each run, Pallas kernels for 0% -> 0%
where the time goes in v1:
time: 1140 us; the launch traced here: 1130 us
  waiting for transfers between devices  703 us (62%)
  blocking collectives  174 us (15%)
  matrix products  154 us (14%)
  other arithmetic  37.8 us (3%)
  local copies, waits for them, and re-layouts  27.8 us (2%)
  between operations  15.7 us (1%)
  starting transfers between devices  13.6 us (1%)
    all_to_all x4, blocking collectives, swap_ctx(): lax.all_to_all(values, 'ctx', split_axis=0, concat_axis=0, tiled=True)  174 us
    reduce_scatter x3, waiting for transfers between devices, scatter_ctx(): return lax.psum_scatter(values, 'ctx', scatter_dimension=0, tiled=True)  151 us
    reduce_scatter x1, waiting for transfers between devices, head_split(): lax.psum_scatter(mul_left(attn_o, d_res_low).astype(bf16), ('dp', 'ctx'),...  146 us
    all_gather x3, waiting for transfers between devices, gather_ctx(): return lax.all_gather(values, 'ctx', axis=0, tiled=True)  129 us
    reduce_scatter x3, waiting for transfers between devices, scatter_dp(): lax.psum_scatter(values.astype(bf16), 'dp', scatter_dimension=0, tiled=True)  89.1 us
    all_gather x1, waiting for transfers between devices, head_split(): lax.all_gather(swap_ctx(jnp.concatenate((gated(w_gate), gated(w_up)), axi...  80.1 us
    dot_general x6, matrix products, mul_right(): lax.dot_general(first_op, second_op, (((1,), (1,)), ((), ())), preferred_...  58.3 us
    dot_general x6, matrix products, mul_plain(): return jnp.dot(first_op, second_op, preferred_element_type=jnp.float32)  48 us
  transfers between devices with their start and end apart: 16, of which 14 were waited for; matrix products, arithmetic and copies ran while one was open for 15% of the time, Pallas kernels for 0%

profile of v1, /device:TPU:8, one launch (start us, length us, event | category | flops | bytes accessed | tf_op | source)
XLA Modules:
  0.0 1126.1 jit_solution(15248109581702581400)
XLA Ops:
  8.6 1.1 fusion.52
  10.9 42.2 %all_to_all.30 = bf16[8,64,768]{2,1,0:T(8,128)(2,1)} all-to-all(bf16[8,64,768]{2,1,0:T(8,128)(2,1)S(1)} %copy.59), channel_id=1, replica_groups=mesh['dp'=4,'ctx'=8] {'ctx'}, dimensions={0} | all-to-all | bytes 1572864 | tf_op jit(solution)/shard_map/all_to_all | solution.py:291
  57.4 73.3 %all_to_all.31 = bf16[8,64,2048]{2,1,0:T(8,128)(2,1)} all-to-all(bf16[8,64,2048]{2,1,0:T(8,128)(2,1)S(1)} %pad_maximum_fusion.4), channel_id=1, replica_groups=mesh['dp'=4,'ctx'=8] {'ctx'}, dimensions={0} | all-to-all | bytes 4194304 | tf_op jit(solution)/shard_map/all_to_all | solution.py:291
  131.5 2.8 multiply_sine_fusion
  134.3 4.6 fusion
  138.9 29.7 %all-gather.10.cloned.1.call-done = bf16[2048,768]{1,0:T(8,128)(2,1)} async-done(((bf16[512,768]{1,0:T(8,128)(2,1)}), bf16[2048,768]{1,0:T(8,128)(2,1)}) %all-gather.10.cloned.1.call-update) | async-done | bytes 3145744 | tf_op jit(solution)/shard_map/all_gather | solution.py:323
  168.7 9.2 fusion.14
  179.2 1.9 fusion.63
  181.1 1.3 fusion.5
  182.4 2.2 copy-done
  184.6 1.8 convolution_convert_fusion.7
  186.4 33.7 %all_to_all.32 = bf16[8,192,256]{2,1,0:T(8,128)(2,1)S(1)} all-to-all(bf16[8,192,256]{2,1,0:T(8,128)(2,1)S(1)} %bitcast.137), channel_id=1, replica_groups=mesh['dp'=4,'ctx'=8] {'ctx'}, dimensions={0} | all-to-all | bytes 1572864 | tf_op jit(solution)/shard_map/all_to_all | solution.py:291
  220.2 36.6 %all-gather.12.cloned.1.call-done = bf16[2048,2048]{1,0:T(8,128)(2,1)} async-done(((bf16[64,2048]{1,0:T(8,128)(2,1)}), bf16[2048,2048]{1,0:T(8,128)(2,1)}) %all-gather.12.cloned.1.call-update) | async-done | bytes 8388624 | tf_op jit(solution)/shard_map/all_gather | solution.py:343
  256.7 5.3 multiply_reduce_fusion.1
  262.1 1.0 multiply_convert_fusion.4
  264.5 80.1 %all-gather.16.cloned.1.call-done = bf16[2048,2048]{1,0:T(8,128)(2,1)} async-done(((bf16[512,2048]{1,0:T(8,128)(2,1)}), bf16[2048,2048]{1,0:T(8,128)(2,1)}) %all-gather.16.cloned.1.call-update) | async-done | bytes 8388624 | tf_op jit(solution)/shard_map/all_gather | solution.py:334
  344.6 64.6 %all-gather.14.cloned.1.call-done = bf16[1536,2048]{1,0:T(8,128)(2,1)} async-done(((bf16[192,2048]{1,0:T(8,128)(2,1)}), bf16[1536,2048]{1,0:T(8,128)(2,1)}) %all-gather.14.cloned.1.call-update) | async-done | bytes 6291472 | tf_op jit(solution)/shard_map/all_gather | solution.py:287
  409.3 19.1 %fusion.64 = f32[1536,2048]{1,0:T(8,128)} fusion(bf16[1536,2048]{1,0:T(8,128)(2,1)} %all-gather.14.cloned.1.call-done, bf16[2048,2048]{1,0:T(8,128)(2,1)} %all-gather.16.cloned.1.call-done), kind=kOutput, calls=%fused_computation.137 | convolution fusion | flops 12884901888 | bytes 27262976 | tf_op jit(solution)/shard_map/dot_general | solution.py:19
  428.4 36.2 %all-gather.18.cloned.1.call-done = bf16[1024,2048]{1,0:T(8,128)(2,1)} async-done(((bf16[256,2048]{1,0:T(8,128)(2,1)}), bf16[1024,2048]{1,0:T(8,128)(2,1)}) %all-gather.18.cloned.1.call-update) | async-done | bytes 4194320 | tf_op jit(solution)/shard_map/all_gather | solution.py:342
  464.6 64.2 %all-gather.22.cloned.1.call-done = bf16[1,1536,2048]{2,1,0:T(8,128)(2,1)} async-done(((bf16[1,192,2048]{2,1,0:T(8,128)(2,1)}), bf16[1,1536,2048]{2,1,0:T(8,128)(2,1)}) %all-gather.22.cloned.1.call-update) | async-done | bytes 6291472 | tf_op jit(solution)/shard_map/all_gather | solution.py:287
  528.8 17.0 %multiply_convert_fusion.2 = (bf16[1536,1024]{1,0:T(8,128)(2,1)S(1)}, bf16[1536,1024]{1,0:T(8,128)(2,1)S(1)}, bf16[1536,1024]{1,0:T(8,128)(2,1)}) fusion(f32[1536,2048]{1,0:T(8,128)} %fusion.64, bf16[1024,2048]{1,0:T(8,128)(2,1)} %all-gather.18.cloned.1.call-done, bf16[1,1536,2048]{2,1,0:T(8,128)(2,1)} %all-gather.22.cloned.1.call-done), kind=kOutput, calls=%fused_computation.24 | convolution fusion | flops 6467616768 | bytes 32505856 | tf_op jit(solution)/shard_map/dot_general | solution.py:23
  545.8 1.7 copy-done.34
  547.5 1.0 copy-done.35
  548.5 17.8 %convolution_convert_fusion.2 = bf16[1536,2048]{1,0:T(8,128)(2,1)} fusion(bf16[2048,2048]{1,0:T(8,128)(2,1)} %all-gather.16.cloned.1.call-done, bf16[1536,1024]{1,0:T(8,128)(2,1)S(1)} %get-tuple-element.14, bf16[1536,1024]{1,0:T(8,128)(2,1)S(1)} %get-tuple-element.13), kind=kOutput, calls=%fused_computation.15 | convolution fusion | flops 12900630528 | bytes 20971520 | tf_op jit(solution)/shard_map/dot_general | solution.py:23
  566.3 11.3 %convolution_convert_fusion.3 = bf16[1536,2048]{1,0:T(8,128)(2,1)} fusion(bf16[1536,1024]{1,0:T(8,128)(2,1)} %get-tuple-element.15, bf16[1024,2048]{1,0:T(8,128)(2,1)} %all-gather.18.cloned.1.call-done), kind=kOutput, calls=%fused_computation.16 | convolution fusion | flops 6445596672 | bytes 13631488 | tf_op jit(solution)/shard_map/dot_general | solution.py:19
  577.7 19.9 %convolution_convert_fusion.1 = bf16[2048,2048]{1,0:T(8,128)(2,1)} fusion(bf16[1536,2048]{1,0:T(8,128)(2,1)} %all-gather.14.cloned.1.call-done, bf16[1536,1024]{1,0:T(8,128)(2,1)} %copy-done.35, bf16[1536,1024]{1,0:T(8,128)(2,1)} %copy-done.34), kind=kOutput, calls=%fused_computation.14 | convolution fusion | flops 12901679104 | bytes 20971520 | tf_op jit(solution)/shard_map/dot_general | solution.py:29
  597.6 36.6 %reduce-scatter.10.cloned.1.call-done = bf16[192,2048]{1,0:T(8,128)(2,1)} async-done(((bf16[1536,2048]{1,0:T(8,128)(2,1)}), bf16[192,2048]{1,0:T(8,128)(2,1)}) %reduce-scatter.10.cloned.1.call-update) | async-done | bytes 786448 | tf_op jit(solution)/shard_map/reduce_scatter | solution.py:283
  634.3 1.5 fusion.23
  635.8 69.0 %reduce-scatter.8.cloned.1.call-done = bf16[192,2048]{1,0:T(8,128)(2,1)} async-done(((bf16[1536,2048]{1,0:T(8,128)(2,1)}), bf16[192,2048]{1,0:T(8,128)(2,1)}) %reduce-scatter.8.cloned.1.call-update) | async-done | bytes 786448 | tf_op jit(solution)/shard_map/reduce_scatter | solution.py:283
  704.8 3.0 fusion.25
  707.8 6.8 convolution_convert_fusion.8
  714.7 24.6 %all_to_all.33 = bf16[8,192,256]{2,1,0:T(8,128)(2,1)S(1)} all-to-all(bf16[8,192,256]{2,1,0:T(8,128)(2,1)S(1)} %bitcast.124), channel_id=1, replica_groups=mesh['dp'=4,'ctx'=8] {'ctx'}, dimensions={0} | all-to-all | bytes 1572864 | tf_op jit(solution)/shard_map/all_to_all | solution.py:291
  739.3 6.2 multiply_reduce_fusion
  745.5 1.3 slice-done.1
  747.0 2.6 multiply_convert_fusion
  749.6 1.4 convolution_multiply_fusion.2
  751.0 1.4 convolution_multiply_fusion.1
  755.1 2.3 convolution_convert_fusion.6
  758.3 7.1 convolution_convert_fusion.5
  765.5 11.5 %fusion.10 = bf16[1024,2048]{1,0:T(8,128)(2,1)} fusion(bf16[1536,1024]{1,0:T(8,128)(2,1)} %get-tuple-element.15, bf16[1,1536,2048]{2,1,0:T(8,128)(2,1)} %all-gather.22.cloned.1.call-done), kind=kOutput, calls=%fused_computation.27 | convolution fusion | flops 6444548096 | bytes 13631488 | tf_op jit(solution)/shard_map/dot_general | solution.py:29
  777.1 8.7 convolution_convert_fusion
  785.8 1.0 copy-done.12
  786.9 5.7 convolution_convert_fusion.4
  792.6 2.8 reduce-scatter.18.cloned.1.call-done
  795.3 5.1 all-to-all-start.5
  800.5 42.1 %reduce-scatter.14.cloned.1.call-done = bf16[512,768]{1,0:T(8,128)(2,1)} async-done(((bf16[2048,768]{1,0:T(8,128)(2,1)}), bf16[512,768]{1,0:T(8,128)(2,1)}) %reduce-scatter.14.cloned.1.call-update) | async-done | bytes 786448 | tf_op jit(solution)/shard_map/reduce_scatter | solution.py:385
  842.6 3.5 all-to-all-done.5
  846.1 7.9 all-to-all-start.4
  854.2 44.2 %reduce-scatter.20.cloned.1.call-done = bf16[256,2048]{1,0:T(8,128)(2,1)} async-done(((bf16[1024,2048]{1,0:T(8,128)(2,1)}), bf16[256,2048]{1,0:T(8,128)(2,1)}) %reduce-scatter.20.cloned.1.call-update) | async-done | bytes 1048592 | tf_op jit(solution)/shard_map/reduce_scatter | solution.py:385
  898.4 2.8 convert_element_type.189
  901.2 2.5 fusion.62
  903.7 2.2 reshape.174
  905.9 1.2 copy.69
  907.1 2.5 copy.80
  909.6 2.2 reshape.176
  911.8 1.2 copy.70
  913.1 1.2 copy.81
  915.2 3.2 broadcast_multiply_fusion
  918.5 1.3 convert_bitcast_fusion
  922.6 45.1 %reduce-scatter.12.cloned.1.call-done = bf16[192,2048]{1,0:T(8,128)(2,1)} async-done(((bf16[1536,2048]{1,0:T(8,128)(2,1)}), bf16[192,2048]{1,0:T(8,128)(2,1)}) %reduce-scatter.12.cloned.1.call-update) | async-done | bytes 786448 | tf_op jit(solution)/shard_map/reduce_scatter | solution.py:283
  967.7 1.5 fusion.26
  969.2 2.5 fusion.46
  971.7 145.8 %reduce-scatter.16.cloned.1.call-done = bf16[64,2048]{1,0:T(8,128)(2,1)} async-done(((bf16[2048,2048]{1,0:T(8,128)(2,1)}), bf16[64,2048]{1,0:T(8,128)(2,1)}) %reduce-scatter.16.cloned.1.call-update) | async-done | bytes 262160 | tf_op jit(solution)/shard_map/reduce_scatter | solution.py:401
  1117.5 1.8 convert_element_type.185
  (154 shorter events, 17.8 us)
Async XLA Ops:
  7.2 3.2 copy-start.17
  7.2 127.1 %all-gather.20.cloned.1.call-start = ((), (), s32[]{:S(2)}) async-start(), calls=%async_computation.25 | async-start | bytes 7077888 | tf_op jit(solution)/shard_map/all_gather | solution.py:287
  7.9 160.7 %all-gather.10.cloned.1.call-start = ((), (), s32[]{:S(2)}) async-start(), calls=%async_computation.13 | async-start | bytes 3932160 | tf_op jit(solution)/shard_map/all_gather | solution.py:323
  8.6 1.9 copy-start.27
  10.6 43.3 %copy-start.33 = (bf16[64]{0:T(256)(128)(2,1)S(1)}, bf16[64]{0:T(256)(128)(2,1)}, u32[]{:S(2)}) copy-start(bf16[64]{0:T(256)(128)(2,1)} %param.19) | copy-start | bytes 388
  10.6 43.3 %copy-start.13 = (bf16[64,8192]{1,0:T(8,128)(2,1)S(1)}, bf16[64,8192]{1,0:T(8,128)(2,1)}, u32[]{:S(2)}) copy-start(bf16[64,8192]{1,0:T(8,128)(2,1)} %param.20) | copy-start | bytes 3145732
  10.6 43.3 %copy-start.15 = (bf16[64,8192]{1,0:T(8,128)(2,1)S(1)}, bf16[64,8192]{1,0:T(8,128)(2,1)}, u32[]{:S(2)}) copy-start(bf16[64,8192]{1,0:T(8,128)(2,1)} %param.21) | copy-start | bytes 3145732
  53.1 203.7 %all-gather.12.cloned.1.call-start = ((), (), s32[]{:S(2)}) async-start(), calls=%async_computation.14 | async-start | bytes 8650752 | tf_op jit(solution)/shard_map/all_gather | solution.py:343
  53.8 290.8 %all-gather.16.cloned.1.call-start = ((), (), s32[]{:S(2)}) async-start(), calls=%async_computation.16 | async-start | bytes 10485760 | tf_op jit(solution)/shard_map/all_gather | solution.py:334
  53.9 0.7 copy-start.31
  130.7 278.6 %all-gather.14.cloned.1.call-start = ((), (), s32[]{:S(2)}) async-start(), calls=%async_computation.15 | async-start | bytes 7077888 | tf_op jit(solution)/shard_map/all_gather | solution.py:287
  134.3 43.9 %copy-start.7 = (f32[1536,128]{0,1:T(8,128)}, f32[1536,128]{0,1:T(8,128)S(1)}, u32[]{:S(2)}) copy-start(f32[1536,128]{0,1:T(8,128)S(1)} %get-tuple-element.41) | copy-start | bytes 2359300
  134.3 43.9 %copy-start.9 = (f32[1536,128]{0,1:T(8,128)}, f32[1536,128]{0,1:T(8,128)S(1)}, u32[]{:S(2)}) copy-start(f32[1536,128]{0,1:T(8,128)S(1)} %get-tuple-element.42) | copy-start | bytes 2359300
  138.9 38.9 %copy-start.29 = (f32[1536]{0:T(1024)}, f32[1536]{0:T(1024)S(1)}, u32[]{:S(2)}) copy-start(f32[1536]{0:T(1024)S(1)} %add_rsqrt_fusion) | copy-start | bytes 18436
  177.8 4.6 copy-start.5
  179.2 1.9 copy-start.19
  179.2 1.9 copy-start.21
  181.1 3.5 copy-start
  186.4 70.4 %copy-start.3 = (bf16[1,192,2048]{2,1,0:T(8,128)(2,1)S(1)}, bf16[1,192,2048]{2,1,0:T(8,128)(2,1)}, u32[]{:S(2)}) copy-start(bf16[1,192,2048]{2,1,0:T(8,128)(2,1)} %param.12) | copy-start | bytes 2359300
  220.2 41.9 %copy-start.11 = (bf16[8,24,8,256]{3,2,0,1:T(8,128)(2,1)}, bf16[8,24,8,256]{3,2,0,1:T(8,128)(2,1)S(1)}, u32[]{:S(2)}) copy-start(bf16[8,24,8,256]{3,2,0,1:T(8,128)(2,1)S(1)} %copy.73) | copy-start | bytes 2359300
  263.1 201.4 %all-gather.18.cloned.1.call-start = ((), (), s32[]{:S(2)}) async-start(), calls=%async_computation.17 | async-start | bytes 5242880 | tf_op jit(solution)/shard_map/all_gather | solution.py:342
  263.7 265.1 %all-gather.22.cloned.1.call-start = ((), (), s32[]{:S(2)}) async-start(), calls=%async_computation.26 | async-start | bytes 7077888 | tf_op jit(solution)/shard_map/all_gather | solution.py:287
  264.5 369.8 %reduce-scatter.10.cloned.1.call-start = ((), (), s32[]{:S(2)}) async-start(), calls=%async_computation.19 | async-start | bytes 7077888 | tf_op jit(solution)/shard_map/reduce_scatter | solution.py:283
  545.8 1.7 copy-start.34
  545.8 2.7 copy-start.35
  566.3 138.5 %reduce-scatter.8.cloned.1.call-start = ((), (), s32[]{:S(2)}) async-start(), calls=%async_computation.18 | async-start | bytes 7077888 | tf_op jit(solution)/shard_map/reduce_scatter | solution.py:283
  577.7 217.7 %reduce-scatter.18.cloned.1.call-start = ((), (), s32[]{:S(2)}) async-start(), calls=%async_computation.23 | async-start | bytes 10485760 | tf_op jit(solution)/shard_map/reduce_scatter | solution.py:385
  597.6 245.0 %reduce-scatter.14.cloned.1.call-start = ((), (), s32[]{:S(2)}) async-start(), calls=%async_computation.21 | async-start | bytes 3932160 | tf_op jit(solution)/shard_map/reduce_scatter | solution.py:385
  707.8 78.0 %copy-start.1 = (f32[192,2048]{1,0:T(8,128)}, f32[192,2048]{1,0:T(8,128)S(1)}, u32[]{:S(2)}) copy-start(f32[192,2048]{1,0:T(8,128)S(1)} %get-tuple-element.33) | copy-start | bytes 4718596
  739.3 6.2 copy-start.23
  739.3 6.2 slice-start
  739.3 7.5 slice-start.1
  739.3 7.7 slice-start.2
  747.0 2.6 copy-start.22
  749.6 1.4 copy-start.20
  752.4 1.3 copy-start.8
  752.4 1.5 copy-start.10
  754.0 1.1 copy-start.24
  754.0 4.4 slice-start.3
  755.1 3.2 slice-start.4
  755.1 3.2 copy-start.30
  757.4 0.9 copy-start.36
  765.5 132.9 %reduce-scatter.20.cloned.1.call-start = ((), (), s32[]{:S(2)}) async-start(), calls=%async_computation.24 | async-start | bytes 5242880 | tf_op jit(solution)/shard_map/reduce_scatter | solution.py:385
  777.0 190.7 %reduce-scatter.12.cloned.1.call-start = ((), (), s32[]{:S(2)}) async-start(), calls=%async_computation.20 | async-start | bytes 7077888 | tf_op jit(solution)/shard_map/reduce_scatter | solution.py:283
  785.7 1.1 copy-start.12
  785.8 331.7 %reduce-scatter.16.cloned.1.call-start = ((), (), s32[]{:S(2)}) async-start(), calls=%async_computation.22 | async-start | bytes 8650752 | tf_op jit(solution)/shard_map/reduce_scatter | solution.py:401
  792.5 61.4 %copy-start.4 = (bf16[1,192,2048]{2,1,0:T(8,128)(2,1)S(1)}, bf16[1,192,2048]{2,1,0:T(8,128)(2,1)}, u32[]{:S(2)}) copy-start(bf16[1,192,2048]{2,1,0:T(8,128)(2,1)} %param.12) | copy-start | bytes 2359300
  795.3 50.7 %all-to-all-start.5 = ((bf16[8,64,2048]{2,1,0:T(8,128)(2,1)}), bf16[8,64,2048]{2,1,0:T(8,128)(2,1)S(1)}, u32[]{:S(2)}, u32[]{:S(2)}) async-start(bf16[8,64,2048]{2,1,0:T(8,128)(2,1)} %bitcast.125), calls=%async_computation.11 | async-start | bytes 4194304 | tf_op jit(solution)/shard_map/all_to_all | solution.py:291
  846.1 72.4 %all-to-all-start.4 = ((bf16[8,64,768]{2,1,0:T(8,128)(2,1)}), bf16[8,64,768]{2,1,0:T(8,128)(2,1)}, u32[]{:S(2)}, u32[]{:S(2)}) async-start(bf16[8,64,768]{2,1,0:T(8,128)(2,1)} %bitcast.133), calls=%async_computation.8 | async-start | bytes 1572864 | tf_op jit(solution)/shard_map/all_to_all | solution.py:291
  913.1 1.6 copy-start.6
  913.1 1.8 copy-start.14
  913.1 2.2 copy-start.16
  913.1 2.2 copy-start.32
  918.5 1.6 copy-start.18
  918.5 1.6 copy-start.28
  919.8 1.3 copy-start.25
  919.8 1.3 copy-start.26
  920.0 49.3 %copy-start.2 = (f32[192,2048]{1,0:T(8,128)S(1)}, f32[192,2048]{1,0:T(8,128)}, u32[]{:S(2)}) copy-start(f32[192,2048]{1,0:T(8,128)} %copy-done.1) | copy-start | bytes 4718596
Sparse Core Ops, SparseCore 0:
  9.7 109.6 all-gather.19
  121.2 47.4 all-gather.9
  171.7 85.0 all-gather.11
  258.4 86.1 all-gather.15
  346.7 62.5 all-gather.13
  411.0 53.5 all-gather.17
  466.2 62.5 all-gather.21
  566.4 67.8 reduce-scatter.9
  636.6 68.1 reduce-scatter.7
  707.7 87.5 reduce-scatter.17
  798.6 43.9 reduce-scatter.13
  845.7 52.6 reduce-scatter.19
  900.7 66.9 reduce-scatter.11
  969.8 147.6 reduce-scatter.15

commit v2 on v1

--- a/solution.py
+++ b/solution.py
@@ -1,6 +1,7 @@
 import jax
 import jax.numpy as jnp
 from jax import lax
+from jax.sharding import Mesh
 from jax.sharding import PartitionSpec as P
 
 FF = 8192
@@ -279,16 +280,110 @@
     )
 
 
-def scatter_ctx(values):
-    return lax.psum_scatter(values, "ctx", scatter_dimension=0, tiled=True)
-
-
-def gather_ctx(values):
-    return lax.all_gather(values, "ctx", axis=0, tiled=True)
-
-
-def swap_ctx(values):
-    return lax.all_to_all(values, "ctx", split_axis=0, concat_axis=0, tiled=True)
+BF16, F32 = jnp.bfloat16, jnp.float32
+CTX = ("half", "low", "core")
+TEAM = ("x", "low", "core")
+join = lax.optimization_barrier
+
+
+def put(buffer, block, index):
+    return lax.dynamic_update_slice(buffer, block[None], (index,) + (0,) * block.ndim)
+
+
+def take(values, index):
+    return lax.dynamic_index_in_dim(values, index, 0, keepdims=False)
+
+
+def after(values, *others):
+    return join((values,) + others)[0]
+
+
+def flip(values, axis, bits=1):
+    return lax.ppermute(values, axis, [(i, i ^ bits) for i in range(lax.axis_size(axis))])
+
+
+def send_dp(own):
+    return [own] + [flip(own, ("y", "x"), bits) for bits in range(1, 4)]
+
+
+def order_dp(blocks):
+    d = lax.axis_index(("y", "x"))
+    buffer = jnp.zeros((4,) + blocks[0].shape, blocks[0].dtype)
+    for bits, block in enumerate(blocks):
+        buffer = put(buffer, block, d ^ bits)
+    return buffer
+
+
+def send_parts_dp(parts):
+    d = lax.axis_index(("y", "x"))
+    away = [flip(take(parts, d ^ bits).astype(BF16), ("y", "x"), bits) for bits in range(1, 4)]
+    return [take(parts, d)] + away
+
+
+def add_parts(parts):
+    total = parts[0]
+    for part in parts[1:]:
+        total = total + part.astype(F32)
+    return total
+
+
+def turn_chips(values, step):
+    pairs = [(c, (c + 2 * step) % 8) for c in range(8)]
+    return lax.ppermute(values, CTX, pairs)
+
+
+def send_column(rows):
+    return [rows] + [turn_chips(rows, step) for step in range(1, 4)]
+
+
+def order_column(blocks):
+    chip = lax.axis_index(("half", "low"))
+    column = jnp.zeros((4,) + blocks[0].shape, blocks[0].dtype)
+    for step, block in enumerate(blocks):
+        column = put(column, block, (chip - step) % 4)
+    return column
+
+
+def order_cores(mine, other):
+    core = lax.axis_index("core")
+    low, high = jnp.where(core == 0, mine, other), jnp.where(core == 0, other, mine)
+    return jnp.stack((low, high), axis=-3)
+
+
+def order_teams(near, far, near_y, far_y):
+    y, half = lax.axis_index("y"), lax.axis_index("half")
+    buffer = jnp.zeros((4,) + near.shape, near.dtype)
+    for block, bits in ((near, 0), (far, 1), (near_y, 2), (far_y, 3)):
+        buffer = put(buffer, block, (2 * y + half) ^ bits)
+    return buffer.reshape((2, 2) + near.shape)
+
+
+def swap(values, axes):
+    return lax.all_to_all(values, axes, split_axis=0, concat_axis=0, tiled=True)
+
+
+def gather(values, axes):
+    return lax.all_gather(values, axes, axis=0, tiled=True)
+
+
+def scatter(values, axes):
+    return lax.psum_scatter(values, axes, scatter_dimension=0, tiled=True).astype(F32)
+
+
+def other_y(parts):
+    return flip(take(parts, 1 - lax.axis_index("y")).astype(BF16), "y")
+
+
+def add_y(parts, got):
+    return take(parts, lax.axis_index("y")) + got.astype(F32)
+
+
+def other_half(parts):
+    return flip(take(parts, 1 - lax.axis_index("half")).astype(BF16), "half")
+
+
+def add_half(parts, got):
+    return take(parts, lax.axis_index("half")) + got.astype(F32)
 
 
 def head_split(
@@ -305,43 +400,28 @@
     w_down,
     cotangent,
 ):
-    bf16, f32 = jnp.bfloat16, jnp.float32
-    groups, pieces = lax.axis_size("ctx"), lax.axis_size("dp")
+    groups = 8
     tok_rows, width = tokens.shape[1:]
     span = groups * tok_rows
     shard = w_query.shape[0]
     share = w_down.shape[0]
+    slice_ff = 4 * share
     per_key = H // KVH
-
-    tok_in = tokens[0].astype(f32)
-    gain_one, gain_two = g_attn.astype(f32)[:, None], g_mlp.astype(f32)[:, None]
-
-    q_cols = (gain_one * w_query).astype(bf16).reshape(shard, H, HD)
-    k_cols = jnp.repeat((gain_one * w_key).astype(bf16).reshape(shard, KVH, HD), per_key, axis=1)
-    v_cols = jnp.repeat((gain_one * w_value).astype(bf16).reshape(shard, KVH, HD), per_key, axis=1)
+    scale = HD ** (-0.5)
+
+    tok_in = tokens[0].astype(F32)
+    gain_one, gain_two = g_attn.astype(F32)[:, None], g_mlp.astype(F32)[:, None]
+
+    q_cols = (gain_one * w_query).astype(BF16).reshape(shard, H, HD)
+    k_cols = jnp.repeat((gain_one * w_key).astype(BF16).reshape(shard, KVH, HD), per_key, axis=1)
+    v_cols = jnp.repeat((gain_one * w_value).astype(BF16).reshape(shard, KVH, HD), per_key, axis=1)
     qkv_cols = jnp.concatenate((q_cols, k_cols, v_cols), axis=2).transpose(1, 0, 2)
-    qkv_w = lax.all_gather(
-        swap_ctx(qkv_cols).reshape(groups * shard, 3 * HD), "dp", axis=0, tiled=True
-    )
-    tok_all = gather_ctx(tokens[0])
-    xn_one = normalize(tok_all.astype(f32)).astype(bf16)
-    qkv = mul_plain(xn_one, qkv_w)
 
     def gated(weight):
-        scaled = (gain_two * weight).astype(bf16).reshape(shard, pieces, groups, share)
-        return scaled.transpose(2, 0, 1, 3).reshape(groups, shard, pieces * share)
-
-    gate_up_w = lax.all_gather(
-        swap_ctx(jnp.concatenate((gated(w_gate), gated(w_up)), axis=2)).reshape(
-            groups * shard, 2 * pieces * share
-        ),
-        "dp",
-        axis=0,
-        tiled=True,
-    )
-    down_w = lax.all_gather(w_down, "dp", axis=0, tiled=True)
-    output_w = lax.all_gather(w_output, ("dp", "ctx"), axis=0, tiled=True)
-
+        scaled = (gain_two * weight).astype(BF16).reshape(shard, 4, groups, share)
+        return scaled.transpose(2, 0, 1, 3).reshape(groups, shard, slice_ff)
+
+    gate_cols, up_cols = gated(w_gate), gated(w_up)
     cosine, sine = rotary(0, span, HD)
 
     def turn(values, sine_table):
@@ -349,72 +429,138 @@
         rolled = jnp.concatenate((-values[:, half:], values[:, :half]), axis=-1)
         return values * cosine + rolled * sine_table
 
-    query = turn(qkv[:, :HD], sine).astype(bf16)
-    key = turn(qkv[:, HD : 2 * HD], sine).astype(bf16)
-    value = qkv[:, 2 * HD :].astype(bf16)
-    scores = mul_right(query, key) * HD ** (-0.5)
+    down_blocks = send_dp(w_down)
+    tok_all = gather(tokens[0], CTX)
+    qkv_rows = swap(qkv_cols, CTX).reshape(groups * shard, 3 * HD)
+    qkv_rows, out_own, gate_cols, up_cols = join((qkv_rows, w_output, gate_cols, up_cols))
+    qkv_blocks = send_dp(qkv_rows)
+    out_blocks = send_column(out_own)
+    qkv_w = order_dp(qkv_blocks).reshape(width, 3 * HD)
+    out_rows = order_column(out_blocks)
+    down_w = order_dp(down_blocks).reshape(slice_ff, width)
+    tok_all, qkv_w, down_w, gate_cols, cosine, sine = join(
+        (tok_all, qkv_w, down_w, gate_cols, cosine, sine)
+    )
+    out_mine = order_dp(send_dp(after(out_rows, qkv_w)))
+    gate_rows = swap(gate_cols, CTX).reshape(groups * shard, slice_ff)
+    xn_one = normalize(tok_all.astype(F32)).astype(BF16)
+    qkv = mul_plain(xn_one, qkv_w)
+    query = turn(qkv[:, :HD], sine).astype(BF16)
+    key = turn(qkv[:, HD : 2 * HD], sine).astype(BF16)
+    value = qkv[:, 2 * HD :].astype(BF16)
+    query, key, value, gate_rows, up_cols, out_mine = join(
+        (query, key, value, gate_rows, up_cols, out_mine)
+    )
+    gate_blocks = send_dp(gate_rows)
+    up_rows = swap(up_cols, CTX).reshape(groups * shard, slice_ff)
+    scores = mul_right(query, key) * scale
     pos = lax.iota(jnp.int32, span)
     seen = (pos[None, :] <= pos[:, None]) | (pos[None, :] < prefix[0])
     scores = jnp.where(seen, scores, NEG)
     prob = jax.nn.softmax(scores, axis=-1)
-    prob_low = prob.astype(bf16)
-    head_o = mul_plain(prob_low, value)
-
-    attn_o = swap_ctx(head_o.astype(bf16).reshape(groups, tok_rows, HD))
+    prob_low = prob.astype(BF16)
+    head_o = mul_plain(prob_low, value).astype(BF16)
+    head_o, up_rows = join((head_o, up_rows))
+    attn_o = swap(head_o.reshape(groups, tok_rows, HD), CTX)
+    up_blocks = send_dp(up_rows)
+    output_w = order_cores(out_mine, flip(out_mine, "core")).reshape(H * HD, width)
+    attn_o, output_w, gate_blocks = join((attn_o, output_w, gate_blocks))
     attn_o = attn_o.transpose(1, 0, 2).reshape(tok_rows, H * HD)
     hid_res = tok_in + mul_plain(attn_o, output_w)
     nrm_two = normalize(hid_res)
-    xn_two = gather_ctx(nrm_two.astype(bf16))
-    gate_up = mul_plain(xn_two, gate_up_w)
-    gate, up_val = gate_up[:, : pieces * share], gate_up[:, pieces * share :]
+    xn_two = gather(nrm_two.astype(BF16), CTX)
+    gate_w = order_dp(gate_blocks).reshape(width, slice_ff)
+    up_w = order_dp(up_blocks).reshape(width, slice_ff)
+    xn_two, gate_w, up_w, dy_own = join((xn_two, gate_w, up_w, cotangent[0]))
+    dy_all = gather(dy_own, CTX)
+    gate, up_val = mul_plain(xn_two, gate_w), mul_plain(xn_two, up_w)
     sigmoid_gate = jax.nn.sigmoid(gate)
-    hidden = (gate * sigmoid_gate * up_val).astype(bf16)
-    result = hid_res + scatter_ctx(mul_plain(hidden, down_w).astype(bf16)).astype(f32)
-    result = result.astype(bf16)[None]
-
-    dy_all = gather_ctx(cotangent[0])
+    hidden = (gate * sigmoid_gate * up_val).astype(BF16)
+    mlp_part = mul_plain(hidden, down_w).astype(BF16)
+    dy_all, mlp_part, gate, up_val = join((dy_all, mlp_part, gate, up_val))
+    cut = width // 2
+    mlp_low = scatter(mlp_part[:, :cut], CTX)
+    sigmoid_gate = jax.nn.sigmoid(gate)
     d_hidden = mul_right(dy_all, down_w)
     d_gate = d_hidden * up_val * sigmoid_gate * (1.0 + gate * (1.0 - sigmoid_gate))
-    d_up = d_hidden * gate * sigmoid_gate
-    d_gate_up = jnp.concatenate((d_gate.astype(bf16), d_up.astype(bf16)), axis=1)
-    dn_two = scatter_ctx(mul_right(d_gate_up, gate_up_w).astype(bf16)).astype(f32)
-    d_res = cotangent[0].astype(f32) + norm_back(hid_res, nrm_two, dn_two)
-    d_res_low = d_res.astype(bf16)
-
-    def scatter_dp(values):
-        return lax.psum_scatter(values.astype(bf16), "dp", scatter_dimension=0, tiled=True)
-
-    down_grad = scatter_dp(mul_left(hidden, dy_all)).astype(f32)
-    gate_up_sum = swap_ctx(
-        scatter_dp(mul_left(xn_two, d_gate_up)).reshape(groups, shard, 2 * pieces * share)
-    ).astype(f32)
-
-    def ungated(summed):
-        return summed.reshape(groups, shard, pieces, share).transpose(1, 2, 0, 3).reshape(shard, FF)
-
-    gate_sum = ungated(gate_up_sum[:, :, : pieces * share])
-    up_sum = ungated(gate_up_sum[:, :, pieces * share :])
-    gain_two_grad = jnp.sum(w_gate * gate_sum + w_up * up_sum, axis=1)
-
-    d_attn = mul_right(d_res_low, output_w).astype(bf16)
-    d_head = swap_ctx(d_attn.reshape(tok_rows, groups, HD).transpose(1, 0, 2)).reshape(span, HD)
-    output_grad = lax.psum_scatter(
-        mul_left(attn_o, d_res_low).astype(bf16), ("dp", "ctx"), scatter_dimension=0, tiled=True
-    ).astype(f32)
-
+    d_gate = d_gate.astype(BF16)
+    d_up = (d_hidden * gate * sigmoid_gate).astype(BF16)
+    dn_part = (mul_right(d_gate, gate_w) + mul_right(d_up, up_w)).astype(BF16)
+    hidden, d_gate, d_up, dn_part, mlp_low = join((hidden, d_gate, d_up, dn_part, mlp_low))
+    dn_two = scatter(dn_part, CTX)
+
+    def by_owner(grad):
+        return grad.reshape((4, grad.shape[0] // 4) + grad.shape[1:])
+
+    gate_parts = send_parts_dp(by_owner(mul_left(xn_two, d_gate)))
+    d_up = after(d_up, gate_parts[0])
+    up_parts = send_parts_dp(by_owner(mul_left(xn_two, d_up)))
+    hidden = after(hidden, up_parts[0])
+    down_parts = send_parts_dp(by_owner(mul_left(hidden, dy_all)))
+    dn_two, gate_parts, up_parts[0], down_parts[0] = join(
+        (dn_two, gate_parts, up_parts[0], down_parts[0])
+    )
+    gate_sum = add_parts(gate_parts).astype(BF16)
+
+    d_res = cotangent[0].astype(F32) + norm_back(hid_res, nrm_two, dn_two)
+    d_res_low = d_res.astype(BF16)
+    d_attn = mul_right(d_res_low, output_w).astype(BF16)
+    d_head = swap(d_attn.reshape(tok_rows, groups, HD).transpose(1, 0, 2), CTX)
+    attn_o_two = flip(attn_o, "core")
+    d_head, mlp_high, gate_sum, attn_o_two, d_res_low = join(
+        (d_head, mlp_part[:, cut:], gate_sum, attn_o_two, d_res_low)
+    )
+    mlp_high = scatter(mlp_high, CTX)
+    gate_sum = swap(gate_sum.reshape(groups, shard, slice_ff), CTX)
+    d_res_two = flip(d_res_low, "core")
+    d_head = d_head.reshape(span, HD)
+    core = lax.axis_index("core")
+
+    def own_columns(values):
+        values = values.reshape(tok_rows, 16, 2, shard)
+        return lax.dynamic_index_in_dim(values, core, 2, keepdims=False).reshape(tok_rows, -1)
+
+    both_o = jnp.concatenate((own_columns(attn_o), own_columns(attn_o_two)), axis=0)
+    both_d = jnp.concatenate((d_res_low, d_res_two), axis=0)
+    output_part = mul_left(both_o, both_d).reshape(4, 4, shard, width)
     d_prob = mul_right(d_head, value)
     row_delta = jnp.sum(prob * d_prob, axis=-1, keepdims=True)
-    d_score = (prob * (d_prob - row_delta)).astype(bf16)
-    d_query = turn(mul_plain(d_score, key) * HD ** (-0.5), -sine)
-    d_key = turn(mul_left(d_score, query) * HD ** (-0.5), -sine)
+    d_score = (prob * (d_prob - row_delta)).astype(BF16)
+    d_query = turn(mul_plain(d_score, key) * scale, -sine)
+    d_key = turn(mul_left(d_score, query) * scale, -sine)
     d_value = mul_left(prob_low, d_head)
-    d_qkv = jnp.concatenate((d_query, d_key, d_value), axis=1).astype(bf16)
-    dn_one = scatter_ctx(mul_right(d_qkv, qkv_w).astype(bf16)).astype(f32)
+    d_qkv = jnp.concatenate((d_query, d_key, d_value), axis=1).astype(BF16)
+    d_qkv, gate_sum, up_parts, output_part = join((d_qkv, gate_sum, up_parts, output_part))
+    output_parts = send_parts_dp(output_part)
+    up_sum = swap(add_parts(up_parts).astype(BF16).reshape(groups, shard, slice_ff), CTX)
+    dn_part_one = mul_right(d_qkv, qkv_w).astype(BF16)
+    dn_part_one, xn_one, d_qkv, mlp_high, down_parts = join(
+        (dn_part_one, xn_one, d_qkv, mlp_high, down_parts)
+    )
+    dn_one = scatter(dn_part_one, CTX)
+    result = hid_res + jnp.concatenate((mlp_low, mlp_high), axis=1)
+    result = result.astype(BF16)[None]
+    down_grad = add_parts(down_parts)
+
+    qkv_parts = send_parts_dp(mul_left(xn_one, d_qkv).reshape(4, groups * shard, 3 * HD))
+    column = add_parts(output_parts)
+    chip = lax.axis_index(("half", "low"))
+    output_grad = take(column, chip)
+    for step in range(1, 4):
+        block = take(column, (chip + step) % 4).astype(BF16)
+        output_grad = output_grad + turn_chips(block, step).astype(F32)
+    qkv_sum = add_parts(qkv_parts).astype(BF16)
+    qkv_sum = swap(qkv_sum.reshape(groups, shard, 3 * HD), CTX)
+    def ungated(summed):
+        blocks = summed.astype(F32).reshape(groups, shard, 4, share)
+        return blocks.transpose(1, 2, 0, 3).reshape(shard, FF)
+
+    gate_sum, up_sum = ungated(gate_sum), ungated(up_sum)
+    gain_two_grad = jnp.sum(w_gate * gate_sum + w_up * up_sum, axis=1)
+
     input_grad = d_res + norm_back(tok_in, normalize(tok_in), dn_one)
-    input_grad = input_grad.astype(bf16)[None]
-
-    qkv_sum = swap_ctx(scatter_dp(mul_left(xn_one, d_qkv)).reshape(groups, shard, 3 * HD))
-    qkv_sum = qkv_sum.astype(f32).transpose(1, 0, 2)
+    input_grad = input_grad.astype(BF16)[None]
+    qkv_sum = qkv_sum.astype(F32).transpose(1, 0, 2)
     q_sum = qkv_sum[:, :, :HD].reshape(shard, H * HD)
 
     def per_group(summed):
@@ -443,15 +589,15 @@
 
 
 def solution(mesh):
-    one_head_each = mesh.shape["ctx"] == H
-    rows, whole = P(("dp", "ctx")), P(("dp", "ctx"), None)
-    acts = P("dp", "ctx", None)
-    in_specs = (acts, P("dp"), rows, whole, whole, whole, whole, rows, whole, whole, whole, acts)
+    if dict(mesh.shape) == {"dp": 4, "ctx": 8}:
+        body, dp, ctx = head_split, ("y", "x"), CTX
+        mesh = Mesh(mesh.devices.reshape(2, 2, 2, 2, 2), dp + ctx)
+    else:
+        body, dp, ctx = gathered_weights, ("dp",), ("ctx",)
+    rows, whole = P(dp + ctx), P(dp + ctx, None)
+    acts = P(dp, ctx, None)
+    in_specs = (acts, P(dp), rows, whole, whole, whole, whole, rows, whole, whole, whole, acts)
     out_specs = (acts, acts, rows, whole, whole, whole, whole, rows, whole, whole, whole)
     return jax.shard_map(
-        head_split if one_head_each else gathered_weights,
-        mesh=mesh,
-        in_specs=in_specs,
-        out_specs=out_specs,
-        check_vma=False,
-    )
+        body, mesh=mesh, in_specs=in_specs, out_specs=out_specs, check_vma=False
+    )

time: 1140 us -> 803 us (0.70)
  waiting for transfers between devices: 703 us -> 310 us
  blocking collectives: 174 us -> 0 us
  local copies, waits for them, and re-layouts: 27.8 us -> 126 us
  starting transfers between devices: 13.6 us -> 94.8 us
  other arithmetic: 37.8 us -> 77.1 us
    reduce_scatter x7 -> x4, waiting for transfers between devices: 386 us -> 31.2 us  [scatter(): lax.psum_scatter(values, axes, scatter_dimension=0, tiled=True).astype(F32)]
    all_gather x7 -> x3, waiting for transfers between devices: 311 us -> 37.8 us  [gather(): return lax.all_gather(values, axes, axis=0, tiled=True)]
    ppermute x0 -> x39, waiting for transfers between devices: none -> 226 us  [the longest x33 196 us: flip(): lax.ppermute(values, axis, [(i, i ^ bits) for i in range(lax.axis_size(ax...]
    all_to_all x4 -> x0, blocking collectives: 174 us -> none  [swap_ctx(): lax.all_to_all(values, 'ctx', split_axis=0, concat_axis=0, tiled=True)]
    ppermute x0 -> x39, starting transfers between devices: none -> 47.7 us  [the longest x33 37.7 us: flip(): lax.ppermute(values, axis, [(i, i ^ bits) for i in range(lax.axis_size(ax...]
    dynamic_update_slice x0 -> x24, local copies, waits for them, and re-layouts: none -> 33.8 us  [put(): lax.dynamic_update_slice(buffer, block[None], (index,) + (0,) * block.ndim)]
    all_to_all x2 -> x8, starting transfers between devices: 13 us -> 46.4 us  [swap(): return lax.all_to_all(values, axes, split_axis=0, concat_axis=0, tiled=True)]
    convert_element_type x10 -> x16, other arithmetic: 11.4 us -> 30.1 us  [the longest x3 5.37 us: scatter(): lax.psum_scatter(values, axes, scatter_dimension=0, tiled=True).astype(F32)]
  transfers between devices with their start and end apart: 16 -> 54, of which waited for: 14 -> 23; matrix products, arithmetic and copies ran while one was open for 15% -> 40% of each run, Pallas kernels for 0% -> 0%
where the time goes in v2:
time: 803 us; the launch traced here: 789 us
  waiting for transfers between devices  310 us (39%)
  matrix products  164 us (20%)
  local copies, waits for them, and re-layouts  126 us (16%)
  starting transfers between devices  94.8 us (12%)
  other arithmetic  77.1 us (10%)
  between operations  16.5 us (2%)
    ppermute x33, waiting for transfers between devices, flip(): lax.ppermute(values, axis, [(i, i ^ bits) for i in range(lax.axis_size(ax...  196 us
    dot_general x7, matrix products, mul_right(): lax.dot_general(first_op, second_op, (((1,), (1,)), ((), ())), preferred_...  66.1 us
    dot_general x7, matrix products, mul_plain(): return jnp.dot(first_op, second_op, preferred_element_type=jnp.float32)  49 us
    dot_general x7, matrix products, mul_left(): lax.dot_general(first_op, second_op, (((0,), (0,)), ((), ())), preferred_...  48.7 us
    all_to_all x8, starting transfers between devices, swap(): return lax.all_to_all(values, axes, split_axis=0, concat_axis=0, tiled=True)  46.4 us
    all_gather x3, waiting for transfers between devices, gather(): return lax.all_gather(values, axes, axis=0, tiled=True)  37.8 us
    ppermute x33, starting transfers between devices, flip(): lax.ppermute(values, axis, [(i, i ^ bits) for i in range(lax.axis_size(ax...  37.7 us
    dynamic_update_slice x24, local copies, waits for them, and re-layouts, put(): lax.dynamic_update_slice(buffer, block[None], (index,) + (0,) * block.ndim)  33.8 us
  transfers between devices with their start and end apart: 54, of which 23 were waited for; matrix products, arithmetic and copies ran while one was open for 40% of the time, Pallas kernels for 0%

profile of v2, /device:TPU:8, one launch (start us, length us, event | category | flops | bytes accessed | tf_op | source)
XLA Modules:
  0.0 788.7 jit_solution(12661686645119320405)
XLA Ops:
  16.2 5.3 all-to-all-start
  23.3 3.8 multiply_sine_fusion
  44.5 13.6 %collective-permute-done.4 = bf16[256,2048]{1,0:T(8,128)(2,1)} collective-permute-done((bf16[256,2048]{1,0:T(8,128)(2,1)}, bf16[256,2048]{1,0:T(8,128)(2,1)}, u32[]{:S(2)}, u32[]{:S(2)}) %collective-permute-start.4) | collective-permute-done | bytes 1048608 | tf_op jit(solution)/shard_map/ppermute | solution.py:302
  77.2 30.1 %collective-permute-done.6 = bf16[64,2048]{1,0:T(8,128)(2,1)S(1)} collective-permute-done((bf16[64,2048]{1,0:T(8,128)(2,1)S(1)}, bf16[64,2048]{1,0:T(8,128)(2,1)S(1)}, u32[]{:S(2)}, u32[]{:S(2)}) %collective-permute-start.6) | collective-permute-done | bytes 262176 | tf_op jit(solution)/shard_map/ppermute | solution.py:332
  111.1 14.0 %collective-permute-done = bf16[512,768]{1,0:T(8,128)(2,1)S(1)} collective-permute-done((bf16[512,768]{1,0:T(8,128)(2,1)}, bf16[512,768]{1,0:T(8,128)(2,1)S(1)}, u32[]{:S(2)}, u32[]{:S(2)}) %collective-permute-start) | collective-permute-done | bytes 786464 | tf_op jit(solution)/shard_map/ppermute | solution.py:302
  131.4 4.1 fusion
  135.5 3.7 fusion.1
  139.2 5.5 all-to-all-start.1
  144.7 8.5 %fusion.73 = f32[1536,768]{0,1:T(8,128)S(1)} fusion(bf16[1536,2048]{1,0:T(8,128)(2,1)} %fusion.1, bf16[2048,768]{1,0:T(8,128)(2,1)} %bitcast.11), kind=kOutput, calls=%fused_computation.204 | convolution fusion | flops 4831838208 | bytes 14155776 | tf_op jit(solution)/shard_map/dot_general | solution.py:20
  160.8 14.2 %collective-permute-done.9 = bf16[4,64,2048]{2,1,0:T(8,128)(2,1)} collective-permute-done((bf16[4,64,2048]{2,1,0:T(8,128)(2,1)}, bf16[4,64,2048]{2,1,0:T(8,128)(2,1)}, u32[]{:S(2)}, u32[]{:S(2)}) %collective-permute-start.9) | collective-permute-done | bytes 1048608 | tf_op jit(solution)/shard_map/ppermute | solution.py:302
  182.8 5.3 all-to-all-start.2
  188.1 3.0 fusion.72
  197.5 13.7 %all-to-all-done.2 = bf16[8,64,1024]{2,1,0:T(8,128)(2,1)S(1)} async-done(((bf16[8,64,1024]{2,1,0:T(8,128)(2,1)}), bf16[8,64,1024]{2,1,0:T(8,128)(2,1)S(1)}, u32[]{:S(2)}, u32[]{:S(2)}) %all-to-all-start.2) | async-done | bytes 1048608 | tf_op jit(solution)/shard_map/all_to_all | solution.py:362
  212.2 6.9 all-to-all-start.3
  223.2 5.0 select_bitcast_fusion.1
  228.2 6.2 pad_maximum_fusion
  234.5 12.5 %collective-permute-done.15 = bf16[512,1024]{1,0:T(8,128)(2,1)} collective-permute-done((bf16[512,1024]{1,0:T(8,128)(2,1)}, bf16[512,1024]{1,0:T(8,128)(2,1)}, u32[]{:S(2)}, u32[]{:S(2)}) %collective-permute-start.15) | collective-permute-done | bytes 1048608 | tf_op jit(solution)/shard_map/ppermute | solution.py:302
  246.9 21.6 %collective-permute-done.14 = bf16[512,1024]{1,0:T(8,128)(2,1)} collective-permute-done((bf16[512,1024]{1,0:T(8,128)(2,1)}, bf16[512,1024]{1,0:T(8,128)(2,1)}, u32[]{:S(2)}, u32[]{:S(2)}) %collective-permute-start.14) | collective-permute-done | bytes 1048608 | tf_op jit(solution)/shard_map/ppermute | solution.py:302
  269.5 5.7 multiply_reduce_fusion.2
  280.8 21.9 %collective-permute-done.16 = bf16[512,1024]{1,0:T(8,128)(2,1)S(1)} collective-permute-done((bf16[512,1024]{1,0:T(8,128)(2,1)S(1)}, bf16[512,1024]{1,0:T(8,128)(2,1)S(1)}, u32[]{:S(2)}, u32[]{:S(2)}) %collective-permute-start.16) | collective-permute-done | bytes 1048608 | tf_op jit(solution)/shard_map/ppermute | solution.py:302
  302.8 21.4 %collective-permute-done.17 = bf16[512,1024]{1,0:T(8,128)(2,1)S(1)} collective-permute-done((bf16[512,1024]{1,0:T(8,128)(2,1)S(1)}, bf16[512,1024]{1,0:T(8,128)(2,1)S(1)}, u32[]{:S(2)}, u32[]{:S(2)}) %collective-permute-start.17) | collective-permute-done | bytes 1048608 | tf_op jit(solution)/shard_map/ppermute | solution.py:302
  339.0 10.1 %fusion.74 = f32[1536,1024]{1,0:T(8,128)S(1)} fusion(bf16[1536,2048]{1,0:T(8,128)(2,1)} %all-gather.5.cloned.1.call-done, bf16[2048,1024]{1,0:T(8,128)(2,1)} %bitcast.38), kind=kOutput, calls=%fused_computation.205 | convolution fusion | flops 6442450944 | bytes 16777216 | tf_op jit(solution)/shard_map/dot_general | solution.py:20
  349.2 9.2 %multiply_convert_fusion.3 = (bf16[1536,1024]{1,0:T(8,128)(2,1)S(1)}, f32[1536,1024]{1,0:T(8,128)}) fusion(f32[1536,1024]{1,0:T(8,128)S(1)} %fusion.74, bf16[1536,2048]{1,0:T(8,128)(2,1)S(1)} %copy-done.50, bf16[2048,1024]{1,0:T(8,128)(2,1)S(1)} %bitcast.270), kind=kOutput, calls=%fused_computation.20 | convolution fusion | flops 6451888128 | bytes 26214400 | tf_op jit(solution)/shard_map/dot_general | solution.py:20
  360.0 8.7 %convolution_convert_fusion.1 = bf16[1536,2048]{1,0:T(8,128)(2,1)} fusion(bf16[1536,1024]{1,0:T(8,128)(2,1)S(1)} %get-tuple-element.117, bf16[1024,2048]{1,0:T(8,128)(2,1)S(1)} %bitcast.269), kind=kOutput, calls=%fused_computation.16 | convolution fusion | flops 6445596672 | bytes 13631488 | tf_op jit(solution)/shard_map/dot_general | solution.py:20
  368.7 35.2 %all-gather.7.cloned.1.call-done = bf16[1536,2048]{1,0:T(8,128)(2,1)} async-done(((bf16[192,2048]{1,0:T(8,128)(2,1)}), bf16[1536,2048]{1,0:T(8,128)(2,1)}) %all-gather.7.cloned.1.call-update) | async-done | bytes 6291472 | tf_op jit(solution)/shard_map/all_gather | solution.py:366
  404.0 6.1 fusion.71
  410.4 15.3 %multiply_convert_fusion.1 = (bf16[1536,1024]{1,0:T(8,128)(2,1)S(1)}, bf16[1536,1024]{1,0:T(8,128)(2,1)S(1)}) fusion(f32[1536,1024]{1,0:T(8,128)} %copy-done.54, f32[1536,1024]{1,0:T(8,128)} %get-tuple-element.108, bf16[1536,2048]{1,0:T(8,128)(2,1)} %all-gather.7.cloned.1.call-done, bf16[1024,2048]{1,0:T(8,128)(2,1)} %bitcast.268), kind=kOutput, calls=%fused_computation.17 | convolution fusion | flops 6462898176 | bytes 29360128 | tf_op jit(solution)/shard_map/dot_general | solution.py:24
  425.7 13.7 %fusion.75 = f32[1536,2048]{1,0:T(8,128)} fusion(bf16[1536,1024]{1,0:T(8,128)(2,1)S(1)} %get-tuple-element.113, bf16[2048,1024]{1,0:T(8,128)(2,1)} %bitcast.38), kind=kOutput, calls=%fused_computation.206 | convolution fusion | flops 6442450944 | bytes 19922944 | tf_op jit(solution)/shard_map/dot_general | solution.py:24
  439.5 11.5 %add_convert_fusion = bf16[1536,2048]{1,0:T(8,128)(2,1)} fusion(f32[1536,2048]{1,0:T(8,128)} %fusion.75, bf16[1536,1024]{1,0:T(8,128)(2,1)S(1)} %get-tuple-element.115, bf16[2048,1024]{1,0:T(8,128)(2,1)S(1)} %bitcast.271), kind=kOutput, calls=%fused_computation.4 | convolution fusion | flops 6448742400 | bytes 26214400 | tf_op jit(solution)/shard_map/dot_general | solution.py:24
  453.0 10.1 %fusion.76 = f32[2048,1024]{1,0:T(8,128)S(1)} fusion(bf16[1536,2048]{1,0:T(8,128)(2,1)} %all-gather.5.cloned.1.call-done, bf16[1536,1024]{1,0:T(8,128)(2,1)} %copy-done.55), kind=kOutput, calls=%fused_computation.207 | convolution fusion | flops 6442450944 | bytes 17825792 | tf_op jit(solution)/shard_map/dot_general | solution.py:30
  470.1 9.9 %fusion.77 = f32[2048,1024]{1,0:T(8,128)S(1)} fusion(bf16[1536,2048]{1,0:T(8,128)(2,1)} %all-gather.5.cloned.1.call-done, bf16[1536,1024]{1,0:T(8,128)(2,1)S(1)} %copy-done.57), kind=kOutput, calls=%fused_computation.208 | convolution fusion | flops 6442450944 | bytes 17825792 | tf_op jit(solution)/shard_map/dot_general | solution.py:30
  480.0 3.9 copy-done.26
  485.4 6.8 fusion.78
  492.2 3.2 copy-done.25
  497.0 24.3 %reduce-scatter.7.cloned.1.call-done = bf16[192,2048]{1,0:T(8,128)(2,1)} async-done(((bf16[1536,2048]{1,0:T(8,128)(2,1)}), bf16[192,2048]{1,0:T(8,128)(2,1)}) %reduce-scatter.7.cloned.1.call-update) | async-done | bytes 786448 | tf_op jit(solution)/shard_map/reduce_scatter | solution.py:370
  523.4 6.6 convolution_convert_fusion.4
  530.9 7.5 all-to-all-start.4
  542.7 4.7 fusion.41
  550.9 4.7 fusion.44
  557.9 3.7 add_convert_fusion.2
  561.6 5.3 all-to-all-start.5
  567.1 6.7 multiply_reduce_fusion
  574.1 4.1 multiply_convert_fusion
  580.4 4.1 convolution_multiply_fusion.2
  584.6 4.1 convolution_multiply_fusion.1
  588.8 3.7 convolution_convert_fusion.2
  598.6 6.8 fusion.28
  606.2 9.2 %convolution_convert_fusion = bf16[1536,2048]{1,0:T(8,128)(2,1)} fusion(bf16[1536,768]{0,1:T(8,128)(2,1)} %pad_maximum_fusion.1, bf16[2048,768]{1,0:T(8,128)(2,1)} %bitcast.11), kind=kOutput, calls=%fused_computation.15 | convolution fusion | flops 4834983936 | bytes 11796480 | tf_op jit(solution)/shard_map/dot_general | solution.py:24
  615.4 7.0 reduce-scatter.9.cloned.1.call-done
  624.4 17.0 %collective-permute-done.28 = bf16[256,2048]{1,0:T(8,128)(2,1)} collective-permute-done((bf16[256,2048]{1,0:T(8,128)(2,1)}, bf16[256,2048]{1,0:T(8,128)(2,1)}, u32[]{:S(2)}, u32[]{:S(2)}) %collective-permute-start.28) | collective-permute-done | bytes 1048608 | tf_op jit(solution)/shard_map/ppermute | solution.py:302
  643.0 3.1 reshape.275
  651.5 3.7 add_convert_fusion.1
  655.2 5.1 all-to-all-start.7
  660.3 3.5 fusion.45
  667.4 7.3 fusion.79
  677.9 12.0 %collective-permute-done.33 = bf16[4,64,2048]{2,1,0:T(8,128)(2,1)S(1)} collective-permute-done((bf16[4,64,2048]{2,1,0:T(8,128)(2,1)S(1)}, bf16[4,64,2048]{2,1,0:T(8,128)(2,1)S(1)}, u32[]{:S(2)}, u32[]{:S(2)}) %collective-permute-start.33) | collective-permute-done | bytes 1048608 | tf_op jit(solution)/shard_map/ppermute | solution.py:302
  691.3 22.0 %collective-permute-done.35 = bf16[4,64,2048]{2,1,0:T(8,128)(2,1)S(1)} collective-permute-done((bf16[4,64,2048]{2,1,0:T(8,128)(2,1)S(1)}, bf16[4,64,2048]{2,1,0:T(8,128)(2,1)S(1)}, u32[]{:S(2)}, u32[]{:S(2)}) %collective-permute-start.35) | collective-permute-done | bytes 1048608 | tf_op jit(solution)/shard_map/ppermute | solution.py:302
  721.7 7.5 collective-permute-done.30
  731.6 14.7 %collective-permute-done.32 = bf16[512,768]{1,0:T(8,128)(2,1)S(1)} collective-permute-done((bf16[512,768]{1,0:T(8,128)(2,1)S(1)}, bf16[512,768]{1,0:T(8,128)(2,1)S(1)}, u32[]{:S(2)}, u32[]{:S(2)}) %collective-permute-start.32) | collective-permute-done | bytes 786464 | tf_op jit(solution)/shard_map/ppermute | solution.py:302
  748.8 5.4 all-to-all-start.6
  756.5 2.9 reshape.277
  764.4 3.2 broadcast_multiply_fusion
  767.7 3.8 convert_add_fusion
  777.6 3.9 fusion.52
  (327 shorter events, 184.4 us)
Async XLA Ops:
  7.2 120.7 %all-gather.9.cloned.1.call-start = ((), (), s32[]{:S(2)}) async-start(), calls=%async_computation.18 | async-start | bytes 7077888 | tf_op jit(solution)/shard_map/all_gather | solution.py:366
  7.9 34.2 %collective-permute-start.3 = (bf16[256,2048]{1,0:T(8,128)(2,1)}, bf16[256,2048]{1,0:T(8,128)(2,1)}, u32[]{:S(2)}, u32[]{:S(2)}) collective-permute-start(bf16[256,2048]{1,0:T(8,128)(2,1)} %param.22), channel_id=1, source_target_pairs={{0,8},{8,0},{16,24},{24,16},{1,9},{9,1},{17,25},{25,17},{2,10},{10... | collective-permute-start | bytes 3145736 | tf_op jit(solution)/shard_map/ppermute | solution.py:302
  9.5 50.9 %collective-permute-start.5 = (bf16[256,2048]{1,0:T(8,128)(2,1)}, bf16[256,2048]{1,0:T(8,128)(2,1)}, u32[]{:S(2)}, u32[]{:S(2)}) collective-permute-start(bf16[256,2048]{1,0:T(8,128)(2,1)} %param.22), channel_id=1, source_target_pairs={{0,24},{8,16},{16,8},{24,0},{1,25},{9,17},{17,9},{25,1},{2,26},{10... | collective-permute-start | bytes 3145736 | tf_op jit(solution)/shard_map/ppermute | solution.py:302
  11.0 47.1 %collective-permute-start.4 = (bf16[256,2048]{1,0:T(8,128)(2,1)}, bf16[256,2048]{1,0:T(8,128)(2,1)}, u32[]{:S(2)}, u32[]{:S(2)}) collective-permute-start(bf16[256,2048]{1,0:T(8,128)(2,1)} %param.22), channel_id=1, source_target_pairs={{0,16},{8,24},{16,0},{24,8},{1,17},{9,25},{17,1},{25,9},{2,18},{10... | collective-permute-start | bytes 3145736 | tf_op jit(solution)/shard_map/ppermute | solution.py:302
  16.2 46.5 %all-to-all-start = ((bf16[8,64,768]{2,1,0:T(8,128)(2,1)}), bf16[8,64,768]{2,1,0:T(8,128)(2,1)}, u32[]{:S(2)}, u32[]{:S(2)}) async-start(bf16[8,64,768]{2,1,0:T(8,128)(2,1)} %copy.77), calls=%async_computation | async-start | bytes 1572864 | tf_op jit(solution)/shard_map/all_to_all | solution.py:362
  30.3 123.3 %copy-start.2 = (f32[1536,256]{0,1:T(8,128)}, f32[1536,256]{0,1:T(8,128)S(1)}, u32[]{:S(2)}) copy-start(f32[1536,256]{0,1:T(8,128)S(1)} %get-tuple-element.82) | copy-start | bytes 4718596
  30.3 123.2 %copy-start.4 = (f32[1536,256]{0,1:T(8,128)}, f32[1536,256]{0,1:T(8,128)S(1)}, u32[]{:S(2)}) copy-start(f32[1536,256]{0,1:T(8,128)S(1)} %get-tuple-element.83) | copy-start | bytes 4718596
  42.1 20.6 %copy-start.41 = (bf16[64,2048]{1,0:T(8,128)(2,1)S(1)}, bf16[64,2048]{1,0:T(8,128)(2,1)}, u32[]{:S(2)}) copy-start(bf16[64,2048]{1,0:T(8,128)(2,1)} %param.18) | copy-start | bytes 786436
  62.7 47.7 %collective-permute-start.8 = (bf16[64,2048]{1,0:T(8,128)(2,1)S(1)}, bf16[64,2048]{1,0:T(8,128)(2,1)S(1)}, u32[]{:S(2)}, u32[]{:S(2)}) collective-permute-start(bf16[64,2048]{1,0:T(8,128)(2,1)S(1)} %copy-done.41), channel_id=1, source_target_pairs={{0,6},{1,7},{2,0},{3,1},{4,2},{5,3},{6,4},{7,5},{8,14},{9,15},{10,... | collective-permute-start | bytes 786440 | tf_op jit(solution)/shard_map/ppermute | solution.py:332
  63.1 46.5 %collective-permute-start.7 = (bf16[64,2048]{1,0:T(8,128)(2,1)S(1)}, bf16[64,2048]{1,0:T(8,128)(2,1)S(1)}, u32[]{:S(2)}, u32[]{:S(2)}) collective-permute-start(bf16[64,2048]{1,0:T(8,128)(2,1)S(1)} %copy-done.41), channel_id=1, source_target_pairs={{0,4},{1,5},{2,6},{3,7},{4,0},{5,1},{6,2},{7,3},{8,12},{9,13},{10,... | collective-permute-start | bytes 786440 | tf_op jit(solution)/shard_map/ppermute | solution.py:332
  65.7 41.5 %collective-permute-start.6 = (bf16[64,2048]{1,0:T(8,128)(2,1)S(1)}, bf16[64,2048]{1,0:T(8,128)(2,1)S(1)}, u32[]{:S(2)}, u32[]{:S(2)}) collective-permute-start(bf16[64,2048]{1,0:T(8,128)(2,1)S(1)} %copy-done.41), channel_id=1, source_target_pairs={{0,2},{1,3},{2,4},{3,5},{4,6},{5,7},{6,0},{7,1},{8,10},{9,11},{10,... | collective-permute-start | bytes 786440 | tf_op jit(solution)/shard_map/ppermute | solution.py:332
  68.2 58.7 %collective-permute-start.2 = (bf16[512,768]{1,0:T(8,128)(2,1)}, bf16[512,768]{1,0:T(8,128)(2,1)S(1)}, u32[]{:S(2)}, u32[]{:S(2)}) collective-permute-start(bf16[512,768]{1,0:T(8,128)(2,1)} %bitcast.4), channel_id=1, source_target_pairs={{0,24},{8,16},{16,8},{24,0},{1,25},{9,17},{17,9},{25,1},{2,26},{10... | collective-permute-start | bytes 2359304 | tf_op jit(solution)/shard_map/ppermute | solution.py:302
  69.7 56.4 %collective-permute-start.1 = (bf16[512,768]{1,0:T(8,128)(2,1)}, bf16[512,768]{1,0:T(8,128)(2,1)S(1)}, u32[]{:S(2)}, u32[]{:S(2)}) collective-permute-start(bf16[512,768]{1,0:T(8,128)(2,1)} %bitcast.4), channel_id=1, source_target_pairs={{0,16},{8,24},{16,0},{24,8},{1,17},{9,25},{17,1},{25,9},{2,18},{10... | collective-permute-start | bytes 2359304 | tf_op jit(solution)/shard_map/ppermute | solution.py:302
  107.3 17.8 %collective-permute-start = (bf16[512,768]{1,0:T(8,128)(2,1)}, bf16[512,768]{1,0:T(8,128)(2,1)S(1)}, u32[]{:S(2)}, u32[]{:S(2)}) collective-permute-start(bf16[512,768]{1,0:T(8,128)(2,1)} %bitcast.4), channel_id=1, source_target_pairs={{0,8},{8,0},{16,24},{24,16},{1,9},{9,1},{17,25},{25,17},{2,10},{10... | collective-permute-start | bytes 2359304 | tf_op jit(solution)/shard_map/ppermute | solution.py:302
  127.9 51.9 %collective-permute-start.11 = (bf16[4,64,2048]{2,1,0:T(8,128)(2,1)}, bf16[4,64,2048]{2,1,0:T(8,128)(2,1)}, u32[]{:S(2)}, u32[]{:S(2)}) collective-permute-start(bf16[4,64,2048]{2,1,0:T(8,128)(2,1)} %bitcast_dynamic-update-slice_fusion.20), channel_id=1, source_target_pairs={{0,24},{8,16},{16,8},{24,0},{1,25},{9,17},{17,9},{25,1},{2,26},{10... | collective-permute-start | bytes 3145736 | tf_op jit(solution)/shard_map/ppermute | solution.py:302
  130.8 46.6 %collective-permute-start.10 = (bf16[4,64,2048]{2,1,0:T(8,128)(2,1)}, bf16[4,64,2048]{2,1,0:T(8,128)(2,1)}, u32[]{:S(2)}, u32[]{:S(2)}) collective-permute-start(bf16[4,64,2048]{2,1,0:T(8,128)(2,1)} %bitcast_dynamic-update-slice_fusion.20), channel_id=1, source_target_pairs={{0,16},{8,24},{16,0},{24,8},{1,17},{9,25},{17,1},{25,9},{2,18},{10... | collective-permute-start | bytes 3145736 | tf_op jit(solution)/shard_map/ppermute | solution.py:302
  131.1 43.9 %collective-permute-start.9 = (bf16[4,64,2048]{2,1,0:T(8,128)(2,1)}, bf16[4,64,2048]{2,1,0:T(8,128)(2,1)}, u32[]{:S(2)}, u32[]{:S(2)}) collective-permute-start(bf16[4,64,2048]{2,1,0:T(8,128)(2,1)} %bitcast_dynamic-update-slice_fusion.20), channel_id=1, source_target_pairs={{0,8},{8,0},{16,24},{24,16},{1,9},{9,1},{17,25},{25,17},{2,10},{10... | collective-permute-start | bytes 3145736 | tf_op jit(solution)/shard_map/ppermute | solution.py:302
  139.2 42.9 %all-to-all-start.1 = ((bf16[8,64,1024]{2,1,0:T(8,128)(2,1)}), bf16[8,64,1024]{2,1,0:T(8,128)(2,1)}, u32[]{:S(2)}, u32[]{:S(2)}) async-start(bf16[8,64,1024]{2,1,0:T(8,128)(2,1)} %reshape.232), calls=%async_computation.1 | async-start | bytes 2097152 | tf_op jit(solution)/shard_map/all_to_all | solution.py:362
  160.8 31.7 %copy-start.36 = (bf16[1536,256]{0,1:T(8,128)(2,1)}, bf16[1536,256]{0,1:T(8,128)(2,1)S(1)}, u32[]{:S(2)}) copy-start(bf16[1536,256]{0,1:T(8,128)(2,1)S(1)} %slice.101) | copy-start | bytes 2359300
  182.1 41.1 %collective-permute-start.12 = (bf16[4,4,64,2048]{3,2,1,0:T(8,128)(2,1)}, bf16[4,4,64,2048]{3,2,1,0:T(8,128)(2,1)}, u32[]{:S(2)}, u32[]{:S(2)}) collective-permute-start(bf16[4,4,64,2048]{3,2,1,0:T(8,128)(2,1)} %bitcast_dynamic-update-slice_fusion.8), channel_id=1, source_target_pairs={{0,1},{1,0},{2,3},{3,2},{4,5},{5,4},{6,7},{7,6},{8,9},{9,8},{10,11... | collective-permute-start | bytes 12582920 | tf_op jit(solution)/shard_map/ppermute | solution.py:302
  182.8 28.5 %all-to-all-start.2 = ((bf16[8,64,1024]{2,1,0:T(8,128)(2,1)}), bf16[8,64,1024]{2,1,0:T(8,128)(2,1)S(1)}, u32[]{:S(2)}, u32[]{:S(2)}) async-start(bf16[8,64,1024]{2,1,0:T(8,128)(2,1)} %reshape.234), calls=%async_computation.2 | async-start | bytes 2097152 | tf_op jit(solution)/shard_map/all_to_all | solution.py:362
  212.2 56.4 %all-to-all-start.3 = ((bf16[8,192,256]{2,1,0:T(8,128)(2,1)}), bf16[8,192,256]{2,1,0:T(8,128)(2,1)S(1)}, u32[]{:S(2)}, u32[]{:S(2)}) async-start(bf16[8,192,256]{2,1,0:T(8,128)(2,1)} %bitcast.27), calls=%async_computation.3 | async-start | bytes 1572864 | tf_op jit(solution)/shard_map/all_to_all | solution.py:362
  219.1 119.8 %all-gather.5.cloned.1.call-start = ((), (), s32[]{:S(2)}) async-start(), calls=%async_computation.12 | async-start | bytes 7077888 | tf_op jit(solution)/shard_map/all_gather | solution.py:366
  219.6 27.3 %collective-permute-start.15 = (bf16[512,1024]{1,0:T(8,128)(2,1)}, bf16[512,1024]{1,0:T(8,128)(2,1)}, u32[]{:S(2)}, u32[]{:S(2)}) collective-permute-start(bf16[512,1024]{1,0:T(8,128)(2,1)} %bitcast.17), channel_id=1, source_target_pairs={{0,24},{8,16},{16,8},{24,0},{1,25},{9,17},{17,9},{25,1},{2,26},{10... | collective-permute-start | bytes 3145736 | tf_op jit(solution)/shard_map/ppermute | solution.py:302
  220.5 48.1 %collective-permute-start.14 = (bf16[512,1024]{1,0:T(8,128)(2,1)}, bf16[512,1024]{1,0:T(8,128)(2,1)}, u32[]{:S(2)}, u32[]{:S(2)}) collective-permute-start(bf16[512,1024]{1,0:T(8,128)(2,1)} %bitcast.17), channel_id=1, source_target_pairs={{0,16},{8,24},{16,0},{24,8},{1,17},{9,25},{17,1},{25,9},{2,18},{10... | collective-permute-start | bytes 3145736 | tf_op jit(solution)/shard_map/ppermute | solution.py:302
  222.6 46.0 %collective-permute-start.13 = (bf16[512,1024]{1,0:T(8,128)(2,1)}, bf16[512,1024]{1,0:T(8,128)(2,1)}, u32[]{:S(2)}, u32[]{:S(2)}) collective-permute-start(bf16[512,1024]{1,0:T(8,128)(2,1)} %bitcast.17), channel_id=1, source_target_pairs={{0,8},{8,0},{16,24},{24,16},{1,9},{9,1},{17,25},{25,17},{2,10},{10... | collective-permute-start | bytes 3145736 | tf_op jit(solution)/shard_map/ppermute | solution.py:302
  228.2 41.3 %copy-start.6 = (bf16[1,192,2048]{2,1,0:T(8,128)(2,1)S(1)}, bf16[1,192,2048]{2,1,0:T(8,128)(2,1)}, u32[]{:S(2)}) copy-start(bf16[1,192,2048]{2,1,0:T(8,128)(2,1)} %param.12) | copy-start | bytes 2359300
  276.2 127.8 %all-gather.7.cloned.1.call-start = ((), (), s32[]{:S(2)}) async-start(), calls=%async_computation.13 | async-start | bytes 7077888 | tf_op jit(solution)/shard_map/all_gather | solution.py:366
  276.7 26.0 %collective-permute-start.16 = (bf16[512,1024]{1,0:T(8,128)(2,1)S(1)}, bf16[512,1024]{1,0:T(8,128)(2,1)S(1)}, u32[]{:S(2)}, u32[]{:S(2)}) collective-permute-start(bf16[512,1024]{1,0:T(8,128)(2,1)S(1)} %bitcast.264), channel_id=1, source_target_pairs={{0,8},{8,0},{16,24},{24,16},{1,9},{9,1},{17,25},{25,17},{2,10},{10... | collective-permute-start | bytes 3145736 | tf_op jit(solution)/shard_map/ppermute | solution.py:302
  277.3 46.9 %collective-permute-start.17 = (bf16[512,1024]{1,0:T(8,128)(2,1)S(1)}, bf16[512,1024]{1,0:T(8,128)(2,1)S(1)}, u32[]{:S(2)}, u32[]{:S(2)}) collective-permute-start(bf16[512,1024]{1,0:T(8,128)(2,1)S(1)} %bitcast.265), channel_id=1, source_target_pairs={{0,16},{8,24},{16,0},{24,8},{1,17},{9,25},{17,1},{25,9},{2,18},{10... | collective-permute-start | bytes 3145736 | tf_op jit(solution)/shard_map/ppermute | solution.py:302
  278.7 45.6 %collective-permute-start.18 = (bf16[512,1024]{1,0:T(8,128)(2,1)S(1)}, bf16[512,1024]{1,0:T(8,128)(2,1)S(1)}, u32[]{:S(2)}, u32[]{:S(2)}) collective-permute-start(bf16[512,1024]{1,0:T(8,128)(2,1)S(1)} %bitcast.266), channel_id=1, source_target_pairs={{0,24},{8,16},{16,8},{24,0},{1,25},{9,17},{17,9},{25,1},{2,26},{10... | collective-permute-start | bytes 3145736 | tf_op jit(solution)/shard_map/ppermute | solution.py:302
  338.9 112.1 %reduce-scatter.5.cloned.1.call-start = ((), (), s32[]{:S(2)}) async-start(), calls=%async_computation.14 | async-start | bytes 3538944 | tf_op jit(solution)/shard_map/reduce_scatter | solution.py:370
  410.1 111.1 %reduce-scatter.7.cloned.1.call-start = ((), (), s32[]{:S(2)}) async-start(), calls=%async_computation.15 | async-start | bytes 7077888 | tf_op jit(solution)/shard_map/reduce_scatter | solution.py:370
  425.7 13.8 %copy-start.55 = (bf16[1536,1024]{1,0:T(8,128)(2,1)}, bf16[1536,1024]{1,0:T(8,128)(2,1)S(1)}, u32[]{:S(2)}) copy-start(bf16[1536,1024]{1,0:T(8,128)(2,1)S(1)} %get-tuple-element.113) | copy-start | bytes 9437188
  425.7 13.8 %copy-start.56 = (bf16[1536,1024]{1,0:T(8,128)(2,1)}, bf16[1536,1024]{1,0:T(8,128)(2,1)S(1)}, u32[]{:S(2)}) copy-start(bf16[1536,1024]{1,0:T(8,128)(2,1)S(1)} %get-tuple-element.115) | copy-start | bytes 9437188
  425.7 13.7 %copy-start.20 = (bf16[4,512,1024]{2,1,0:T(8,128)(2,1)S(1)}, bf16[4,512,1024]{2,1,0:T(8,128)(2,1)}, u32[]{:S(2)}) copy-start(bf16[4,512,1024]{2,1,0:T(8,128)(2,1)} %copy-done.18) | copy-start | bytes 12582916
  464.7 20.7 %slice-start.6 = ((s8[6291456]{0:T(1024)(128)(4,1)}), s8[2097152]{0:T(1024)(128)(4,1)S(1)}, s32[]{:S(2)}) async-start(s8[6291456]{0:T(1024)(128)(4,1)} %bitcast.302), calls=%async_computation.25 | async-start | bytes 4194304
  466.6 56.1 %collective-permute-start.21 = (bf16[512,1024]{1,0:T(8,128)(2,1)}, bf16[512,1024]{1,0:T(8,128)(2,1)}, u32[]{:S(2)}, u32[]{:S(2)}) collective-permute-start(bf16[512,1024]{1,0:T(8,128)(2,1)} %get-tuple-element.158), channel_id=1, source_target_pairs={{0,24},{8,16},{16,8},{24,0},{1,25},{9,17},{17,9},{25,1},{2,26},{10... | collective-permute-start | bytes 3145736 | tf_op jit(solution)/shard_map/ppermute | solution.py:302
  469.0 53.7 %collective-permute-start.20 = (bf16[512,1024]{1,0:T(8,128)(2,1)}, bf16[512,1024]{1,0:T(8,128)(2,1)}, u32[]{:S(2)}, u32[]{:S(2)}) collective-permute-start(bf16[512,1024]{1,0:T(8,128)(2,1)} %get-tuple-element.159), channel_id=1, source_target_pairs={{0,16},{8,24},{16,0},{24,8},{1,17},{9,25},{17,1},{25,9},{2,18},{10... | collective-permute-start | bytes 3145736 | tf_op jit(solution)/shard_map/ppermute | solution.py:302
  469.5 15.8 %slice-start.7 = ((s8[6291456]{0:T(1024)(128)(4,1)}), s8[4194304]{0:T(1024)(128)(4,1)S(1)}, s32[]{:S(2)}) async-start(s8[6291456]{0:T(1024)(128)(4,1)} %bitcast.302), calls=%async_computation.26 | async-start | bytes 8388608
  469.5 53.1 %collective-permute-start.19 = (bf16[512,1024]{1,0:T(8,128)(2,1)}, bf16[512,1024]{1,0:T(8,128)(2,1)}, u32[]{:S(2)}, u32[]{:S(2)}) collective-permute-start(bf16[512,1024]{1,0:T(8,128)(2,1)} %get-tuple-element.160), channel_id=1, source_target_pairs={{0,8},{8,0},{16,24},{24,16},{1,9},{9,1},{17,25},{25,17},{2,10},{10... | collective-permute-start | bytes 3145736 | tf_op jit(solution)/shard_map/ppermute | solution.py:302
  530.9 30.7 %all-to-all-start.4 = ((bf16[8,192,256]{2,1,0:T(8,128)(2,1)}), bf16[8,192,256]{2,1,0:T(8,128)(2,1)}, u32[]{:S(2)}, u32[]{:S(2)}) async-start(bf16[8,192,256]{2,1,0:T(8,128)(2,1)} %bitcast.285), calls=%async_computation.6 | async-start | bytes 1572864 | tf_op jit(solution)/shard_map/all_to_all | solution.py:362
  538.4 84.0 %reduce-scatter.9.cloned.1.call-start = ((), (), s32[]{:S(2)}) async-start(), calls=%async_computation.16 | async-start | bytes 3538944 | tf_op jit(solution)/shard_map/reduce_scatter | solution.py:370
  538.4 23.1 %collective-permute-start.22 = (bf16[192,2048]{1,0:T(8,128)(2,1)}, bf16[192,2048]{1,0:T(8,128)(2,1)}, u32[]{:S(2)}, u32[]{:S(2)}) collective-permute-start(bf16[192,2048]{1,0:T(8,128)(2,1)} %bitcast.300), channel_id=1, source_target_pairs={{0,1},{1,0},{2,3},{3,2},{4,5},{5,4},{6,7},{7,6},{8,9},{9,8},{10,11... | collective-permute-start | bytes 2359304 | tf_op jit(solution)/shard_map/ppermute | solution.py:302
  547.4 49.8 %collective-permute-start.25 = (bf16[512,1024]{1,0:T(8,128)(2,1)}, bf16[512,1024]{1,0:T(8,128)(2,1)}, u32[]{:S(2)}, u32[]{:S(2)}) collective-permute-start(bf16[512,1024]{1,0:T(8,128)(2,1)} %get-tuple-element.155), channel_id=1, source_target_pairs={{0,24},{8,16},{16,8},{24,0},{1,25},{9,17},{17,9},{25,1},{2,26},{10... | collective-permute-start | bytes 3145736 | tf_op jit(solution)/shard_map/ppermute | solution.py:302
  549.8 55.7 %collective-permute-start.24 = (bf16[512,1024]{1,0:T(8,128)(2,1)}, bf16[512,1024]{1,0:T(8,128)(2,1)}, u32[]{:S(2)}, u32[]{:S(2)}) collective-permute-start(bf16[512,1024]{1,0:T(8,128)(2,1)} %get-tuple-element.156), channel_id=1, source_target_pairs={{0,16},{8,24},{16,0},{24,8},{1,17},{9,25},{17,1},{25,9},{2,18},{10... | collective-permute-start | bytes 3145736 | tf_op jit(solution)/shard_map/ppermute | solution.py:302
  550.3 55.1 %collective-permute-start.23 = (bf16[512,1024]{1,0:T(8,128)(2,1)}, bf16[512,1024]{1,0:T(8,128)(2,1)}, u32[]{:S(2)}, u32[]{:S(2)}) collective-permute-start(bf16[512,1024]{1,0:T(8,128)(2,1)} %get-tuple-element.157), channel_id=1, source_target_pairs={{0,8},{8,0},{16,24},{24,16},{1,9},{9,1},{17,25},{25,17},{2,10},{10... | collective-permute-start | bytes 3145736 | tf_op jit(solution)/shard_map/ppermute | solution.py:302
  555.6 68.8 %collective-permute-start.29 = (bf16[256,2048]{1,0:T(8,128)(2,1)}, bf16[256,2048]{1,0:T(8,128)(2,1)}, u32[]{:S(2)}, u32[]{:S(2)}) collective-permute-start(bf16[256,2048]{1,0:T(8,128)(2,1)} %get-tuple-element.152), channel_id=1, source_target_pairs={{0,24},{8,16},{16,8},{24,0},{1,25},{9,17},{17,9},{25,1},{2,26},{10... | collective-permute-start | bytes 3145736 | tf_op jit(solution)/shard_map/ppermute | solution.py:302
  561.6 44.6 %all-to-all-start.5 = ((bf16[8,64,1024]{2,1,0:T(8,128)(2,1)}), bf16[8,64,1024]{2,1,0:T(8,128)(2,1)}, u32[]{:S(2)}, u32[]{:S(2)}) async-start(bf16[8,64,1024]{2,1,0:T(8,128)(2,1)} %bitcast.276), calls=%async_computation.7 | async-start | bytes 2097152 | tf_op jit(solution)/shard_map/all_to_all | solution.py:362
  566.9 208.8 %reduce-scatter.11.cloned.1.call-start = ((), (), s32[]{:S(2)}) async-start(), calls=%async_computation.17 | async-start | bytes 7077888 | tf_op jit(solution)/shard_map/reduce_scatter | solution.py:370
  566.9 31.0 %collective-permute-start.26 = (bf16[192,2048]{1,0:T(8,128)(2,1)}, bf16[192,2048]{1,0:T(8,128)(2,1)}, u32[]{:S(2)}, u32[]{:S(2)}) collective-permute-start(bf16[192,2048]{1,0:T(8,128)(2,1)} %copy-done.29), channel_id=1, source_target_pairs={{0,1},{1,0},{2,3},{3,2},{4,5},{5,4},{6,7},{7,6},{8,9},{9,8},{10,11... | collective-permute-start | bytes 2359304 | tf_op jit(solution)/shard_map/ppermute | solution.py:302
  597.2 44.3 %collective-permute-start.28 = (bf16[256,2048]{1,0:T(8,128)(2,1)}, bf16[256,2048]{1,0:T(8,128)(2,1)}, u32[]{:S(2)}, u32[]{:S(2)}) collective-permute-start(bf16[256,2048]{1,0:T(8,128)(2,1)} %get-tuple-element.153), channel_id=1, source_target_pairs={{0,16},{8,24},{16,0},{24,8},{1,17},{9,25},{17,1},{25,9},{2,18},{10... | collective-permute-start | bytes 3145736 | tf_op jit(solution)/shard_map/ppermute | solution.py:302
  598.0 43.6 %collective-permute-start.27 = (bf16[256,2048]{1,0:T(8,128)(2,1)}, bf16[256,2048]{1,0:T(8,128)(2,1)}, u32[]{:S(2)}, u32[]{:S(2)}) collective-permute-start(bf16[256,2048]{1,0:T(8,128)(2,1)} %get-tuple-element.154), channel_id=1, source_target_pairs={{0,8},{8,0},{16,24},{24,16},{1,9},{9,1},{17,25},{25,17},{2,10},{10... | collective-permute-start | bytes 3145736 | tf_op jit(solution)/shard_map/ppermute | solution.py:302
  655.2 93.7 %all-to-all-start.7 = ((bf16[8,64,1024]{2,1,0:T(8,128)(2,1)}), bf16[8,64,1024]{2,1,0:T(8,128)(2,1)}, u32[]{:S(2)}, u32[]{:S(2)}) async-start(bf16[8,64,1024]{2,1,0:T(8,128)(2,1)} %bitcast.277), calls=%async_computation.11 | async-start | bytes 2097152 | tf_op jit(solution)/shard_map/all_to_all | solution.py:362
  663.8 26.1 %collective-permute-start.33 = (bf16[4,64,2048]{2,1,0:T(8,128)(2,1)S(1)}, bf16[4,64,2048]{2,1,0:T(8,128)(2,1)S(1)}, u32[]{:S(2)}, u32[]{:S(2)}) collective-permute-start(bf16[4,64,2048]{2,1,0:T(8,128)(2,1)S(1)} %get-tuple-element.149), channel_id=1, source_target_pairs={{0,8},{8,0},{16,24},{24,16},{1,9},{9,1},{17,25},{25,17},{2,10},{10... | collective-permute-start | bytes 3145736 | tf_op jit(solution)/shard_map/ppermute | solution.py:302
  665.4 47.9 %collective-permute-start.35 = (bf16[4,64,2048]{2,1,0:T(8,128)(2,1)S(1)}, bf16[4,64,2048]{2,1,0:T(8,128)(2,1)S(1)}, u32[]{:S(2)}, u32[]{:S(2)}) collective-permute-start(bf16[4,64,2048]{2,1,0:T(8,128)(2,1)S(1)} %get-tuple-element.150), channel_id=1, source_target_pairs={{0,24},{8,16},{16,8},{24,0},{1,25},{9,17},{17,9},{25,1},{2,26},{10... | collective-permute-start | bytes 3145736 | tf_op jit(solution)/shard_map/ppermute | solution.py:302
  666.8 48.4 %collective-permute-start.34 = (bf16[4,64,2048]{2,1,0:T(8,128)(2,1)S(1)}, bf16[4,64,2048]{2,1,0:T(8,128)(2,1)S(1)}, u32[]{:S(2)}, u32[]{:S(2)}) collective-permute-start(bf16[4,64,2048]{2,1,0:T(8,128)(2,1)S(1)} %get-tuple-element.151), channel_id=1, source_target_pairs={{0,16},{8,24},{16,0},{24,8},{1,17},{9,25},{17,1},{25,9},{2,18},{10... | collective-permute-start | bytes 3145736 | tf_op jit(solution)/shard_map/ppermute | solution.py:302
  674.9 54.3 %collective-permute-start.30 = (bf16[512,768]{1,0:T(8,128)(2,1)S(1)}, bf16[512,768]{1,0:T(8,128)(2,1)S(1)}, u32[]{:S(2)}, u32[]{:S(2)}) collective-permute-start(bf16[512,768]{1,0:T(8,128)(2,1)S(1)} %get-tuple-element.165), channel_id=1, source_target_pairs={{0,8},{8,0},{16,24},{24,16},{1,9},{9,1},{17,25},{25,17},{2,10},{10... | collective-permute-start | bytes 2359304 | tf_op jit(solution)/shard_map/ppermute | solution.py:302
  676.5 69.8 %collective-permute-start.32 = (bf16[512,768]{1,0:T(8,128)(2,1)S(1)}, bf16[512,768]{1,0:T(8,128)(2,1)S(1)}, u32[]{:S(2)}, u32[]{:S(2)}) collective-permute-start(bf16[512,768]{1,0:T(8,128)(2,1)S(1)} %get-tuple-element.166), channel_id=1, source_target_pairs={{0,24},{8,16},{16,8},{24,0},{1,25},{9,17},{17,9},{25,1},{2,26},{10... | collective-permute-start | bytes 2359304 | tf_op jit(solution)/shard_map/ppermute | solution.py:302
  689.9 57.7 %collective-permute-start.31 = (bf16[512,768]{1,0:T(8,128)(2,1)S(1)}, bf16[512,768]{1,0:T(8,128)(2,1)S(1)}, u32[]{:S(2)}, u32[]{:S(2)}) collective-permute-start(bf16[512,768]{1,0:T(8,128)(2,1)S(1)} %get-tuple-element.167), channel_id=1, source_target_pairs={{0,16},{8,24},{16,0},{24,8},{1,17},{9,25},{17,1},{25,9},{2,18},{10... | collective-permute-start | bytes 2359304 | tf_op jit(solution)/shard_map/ppermute | solution.py:302
  719.7 34.6 %collective-permute-start.36 = (bf16[64,2048]{1,0:T(8,128)(2,1)}, bf16[64,2048]{1,0:T(8,128)(2,1)}, u32[]{:S(2)}, u32[]{:S(2)}) collective-permute-start(bf16[64,2048]{1,0:T(8,128)(2,1)} %get-tuple-element.179), channel_id=1, source_target_pairs={{0,2},{1,3},{2,4},{3,5},{4,6},{5,7},{6,0},{7,1},{8,10},{9,11},{10,... | collective-permute-start | bytes 786440 | tf_op jit(solution)/shard_map/ppermute | solution.py:332
  721.2 33.1 %collective-permute-start.38 = (bf16[64,2048]{1,0:T(8,128)(2,1)}, bf16[64,2048]{1,0:T(8,128)(2,1)}, u32[]{:S(2)}, u32[]{:S(2)}) collective-permute-start(bf16[64,2048]{1,0:T(8,128)(2,1)} %get-tuple-element.180), channel_id=1, source_target_pairs={{0,6},{1,7},{2,0},{3,1},{4,2},{5,3},{6,4},{7,5},{8,14},{9,15},{10,... | collective-permute-start | bytes 786440 | tf_op jit(solution)/shard_map/ppermute | solution.py:332
  729.2 25.0 %collective-permute-start.37 = (bf16[64,2048]{1,0:T(8,128)(2,1)S(1)}, bf16[64,2048]{1,0:T(8,128)(2,1)}, u32[]{:S(2)}, u32[]{:S(2)}) collective-permute-start(bf16[64,2048]{1,0:T(8,128)(2,1)S(1)} %get-tuple-element.181), channel_id=1, source_target_pairs={{0,4},{1,5},{2,6},{3,7},{4,0},{5,1},{6,2},{7,3},{8,12},{9,13},{10,... | collective-permute-start | bytes 786440 | tf_op jit(solution)/shard_map/ppermute | solution.py:332
  748.8 22.9 %all-to-all-start.6 = ((bf16[8,64,768]{2,1,0:T(8,128)(2,1)}), bf16[8,64,768]{2,1,0:T(8,128)(2,1)}, u32[]{:S(2)}, u32[]{:S(2)}) async-start(bf16[8,64,768]{2,1,0:T(8,128)(2,1)} %bitcast.284), calls=%async_computation.10 | async-start | bytes 1572864 | tf_op jit(solution)/shard_map/all_to_all | solution.py:362
  (56 other events, 253.2 us)
Sparse Core Ops, SparseCore 0:
  9.7 99.7 all-gather.8
  276.3 62.5 all-gather.4
  340.5 63.3 all-gather.6
  410.3 36.7 reduce-scatter.4
  453.1 68.0 reduce-scatter.6
  561.8 60.5 reduce-scatter.8
  641.7 107.9 reduce-scatter.10

commit v3 on v2

--- a/solution.py
+++ b/solution.py
@@ -314,14 +314,17 @@
     return buffer
 
 
-def send_parts_dp(parts):
+def split_parts_dp(parts):
     d = lax.axis_index(("y", "x"))
-    away = [flip(take(parts, d ^ bits).astype(BF16), ("y", "x"), bits) for bits in range(1, 4)]
-    return [take(parts, d)] + away
+    return [take(parts, d ^ bits) for bits in range(4)]
+
+
+def send_parts_dp(split, bits=(1, 2, 3)):
+    return [flip(split[b], ("y", "x"), b) for b in bits]
 
 
 def add_parts(parts):
-    total = parts[0]
+    total = parts[0].astype(F32)
     for part in parts[1:]:
         total = total + part.astype(F32)
     return total
@@ -360,6 +363,18 @@
 
 def swap(values, axes):
     return lax.all_to_all(values, axes, split_axis=0, concat_axis=0, tiled=True)
+
+
+def swap_steps(values):
+    chip, core = lax.axis_index(("half", "low")), lax.axis_index("core")
+    values = values.reshape((4, 2) + values.shape[1:])
+    got = [take(values, chip)]
+    got += [turn_chips(take(values, (chip + step) % 4), step) for step in range(1, 4)]
+    column = order_column(got)
+    mine = lax.dynamic_index_in_dim(column, core, 1, keepdims=False)
+    other = flip(lax.dynamic_index_in_dim(column, 1 - core, 1, keepdims=False), "core")
+    low, high = jnp.where(core == 0, mine, other), jnp.where(core == 0, other, mine)
+    return jnp.stack((low, high), axis=1).reshape((8,) + values.shape[2:])
 
 
 def gather(values, axes):
@@ -441,6 +456,8 @@
     tok_all, qkv_w, down_w, gate_cols, cosine, sine = join(
         (tok_all, qkv_w, down_w, gate_cols, cosine, sine)
     )
+    cut = width // 2
+    dy_left = gather(after(cotangent[0][:, :cut], tok_all), CTX)
     out_mine = order_dp(send_dp(after(out_rows, qkv_w)))
     gate_rows = swap(gate_cols, CTX).reshape(groups * shard, slice_ff)
     xn_one = normalize(tok_all.astype(F32)).astype(BF16)
@@ -451,7 +468,7 @@
     query, key, value, gate_rows, up_cols, out_mine = join(
         (query, key, value, gate_rows, up_cols, out_mine)
     )
-    gate_blocks = send_dp(gate_rows)
+    gate_w = gather(gate_rows, ("y", "x"))
     up_rows = swap(up_cols, CTX).reshape(groups * shard, slice_ff)
     scores = mul_right(query, key) * scale
     pos = lax.iota(jnp.int32, span)
@@ -462,58 +479,54 @@
     head_o = mul_plain(prob_low, value).astype(BF16)
     head_o, up_rows = join((head_o, up_rows))
     attn_o = swap(head_o.reshape(groups, tok_rows, HD), CTX)
+    output_w = order_cores(out_mine, flip(out_mine, "core")).reshape(H * HD, width)
+    attn_o, output_w = join((attn_o, output_w))
     up_blocks = send_dp(up_rows)
-    output_w = order_cores(out_mine, flip(out_mine, "core")).reshape(H * HD, width)
-    attn_o, output_w, gate_blocks = join((attn_o, output_w, gate_blocks))
     attn_o = attn_o.transpose(1, 0, 2).reshape(tok_rows, H * HD)
     hid_res = tok_in + mul_plain(attn_o, output_w)
     nrm_two = normalize(hid_res)
     xn_two = gather(nrm_two.astype(BF16), CTX)
-    gate_w = order_dp(gate_blocks).reshape(width, slice_ff)
     up_w = order_dp(up_blocks).reshape(width, slice_ff)
-    xn_two, gate_w, up_w, dy_own = join((xn_two, gate_w, up_w, cotangent[0]))
-    dy_all = gather(dy_own, CTX)
+    xn_two, gate_w, up_w, dy_left, dy_own = join(
+        (xn_two, gate_w, up_w, dy_left, cotangent[0][:, cut:])
+    )
+    dy_right = gather(dy_own, CTX)
     gate, up_val = mul_plain(xn_two, gate_w), mul_plain(xn_two, up_w)
     sigmoid_gate = jax.nn.sigmoid(gate)
     hidden = (gate * sigmoid_gate * up_val).astype(BF16)
     mlp_part = mul_plain(hidden, down_w).astype(BF16)
-    dy_all, mlp_part, gate, up_val = join((dy_all, mlp_part, gate, up_val))
-    cut = width // 2
-    mlp_low = scatter(mlp_part[:, :cut], CTX)
+    mlp_part, gate, up_val, dy_right = join((mlp_part, gate, up_val, dy_right))
+    mlp_sum = scatter(mlp_part, CTX)
     sigmoid_gate = jax.nn.sigmoid(gate)
-    d_hidden = mul_right(dy_all, down_w)
+    d_hidden = mul_right(dy_left, down_w[:, :cut]) + mul_right(dy_right, down_w[:, cut:])
     d_gate = d_hidden * up_val * sigmoid_gate * (1.0 + gate * (1.0 - sigmoid_gate))
     d_gate = d_gate.astype(BF16)
     d_up = (d_hidden * gate * sigmoid_gate).astype(BF16)
-    dn_part = (mul_right(d_gate, gate_w) + mul_right(d_up, up_w)).astype(BF16)
-    hidden, d_gate, d_up, dn_part, mlp_low = join((hidden, d_gate, d_up, dn_part, mlp_low))
-    dn_two = scatter(dn_part, CTX)
 
     def by_owner(grad):
         return grad.reshape((4, grad.shape[0] // 4) + grad.shape[1:])
 
-    gate_parts = send_parts_dp(by_owner(mul_left(xn_two, d_gate)))
-    d_up = after(d_up, gate_parts[0])
-    up_parts = send_parts_dp(by_owner(mul_left(xn_two, d_up)))
-    hidden = after(hidden, up_parts[0])
-    down_parts = send_parts_dp(by_owner(mul_left(hidden, dy_all)))
-    dn_two, gate_parts, up_parts[0], down_parts[0] = join(
-        (dn_two, gate_parts, up_parts[0], down_parts[0])
-    )
-    gate_sum = add_parts(gate_parts).astype(BF16)
-
+    gate_split = split_parts_dp(by_owner(mul_left(xn_two, d_gate).astype(BF16)))
+    up_split = split_parts_dp(by_owner(mul_left(xn_two, d_up).astype(BF16)))
+    hidden, d_gate, d_up, gate_split, up_split = join(
+        (hidden, d_gate, d_up, gate_split, up_split)
+    )
+    gate_near = send_parts_dp(gate_split, (1, 2))
+    dn_part = (mul_right(d_gate, gate_w) + mul_right(d_up, up_w)).astype(BF16)
+    hidden, dn_part, mlp_sum, gate_near, gate_split, up_split = join(
+        (hidden, dn_part, mlp_sum, gate_near, gate_split, up_split)
+    )
+    gate_up_far = send_parts_dp(gate_split, (3,)) + send_parts_dp(up_split)
+    dn_two = scatter(dn_part, CTX)
+    down_split = [
+        split_parts_dp(by_owner(mul_left(hidden, part).astype(BF16))) for part in (dy_left, dy_right)
+    ]
+    dn_two, gate_up_far, down_split = join((dn_two, gate_up_far, down_split))
     d_res = cotangent[0].astype(F32) + norm_back(hid_res, nrm_two, dn_two)
     d_res_low = d_res.astype(BF16)
     d_attn = mul_right(d_res_low, output_w).astype(BF16)
     d_head = swap(d_attn.reshape(tok_rows, groups, HD).transpose(1, 0, 2), CTX)
-    attn_o_two = flip(attn_o, "core")
-    d_head, mlp_high, gate_sum, attn_o_two, d_res_low = join(
-        (d_head, mlp_part[:, cut:], gate_sum, attn_o_two, d_res_low)
-    )
-    mlp_high = scatter(mlp_high, CTX)
-    gate_sum = swap(gate_sum.reshape(groups, shard, slice_ff), CTX)
-    d_res_two = flip(d_res_low, "core")
-    d_head = d_head.reshape(span, HD)
+    attn_o_two, d_res_two = flip(attn_o, "core"), flip(d_res_low, "core")
     core = lax.axis_index("core")
 
     def own_columns(values):
@@ -522,7 +535,16 @@
 
     both_o = jnp.concatenate((own_columns(attn_o), own_columns(attn_o_two)), axis=0)
     both_d = jnp.concatenate((d_res_low, d_res_two), axis=0)
-    output_part = mul_left(both_o, both_d).reshape(4, 4, shard, width)
+    output_part = mul_left(both_o, both_d).astype(BF16).reshape(4, 4, shard, width)
+    output_split = split_parts_dp(output_part)
+    gate_parts = gate_split[:1] + gate_near + gate_up_far[:1]
+    up_parts = up_split[:1] + gate_up_far[1:]
+    gate_up_sum = jnp.stack([add_parts(parts).astype(BF16) for parts in (gate_parts, up_parts)])
+    d_head, gate_up_sum, output_split = join((d_head, gate_up_sum, output_split))
+    output_parts = output_split[:1] + send_parts_dp(output_split)
+    gate_up_sum = gate_up_sum.reshape(2, groups, shard, slice_ff)
+    gate_up_sum = lax.all_to_all(gate_up_sum, CTX, split_axis=1, concat_axis=1, tiled=True)
+    d_head = d_head.reshape(span, HD)
     d_prob = mul_right(d_head, value)
     row_delta = jnp.sum(prob * d_prob, axis=-1, keepdims=True)
     d_score = (prob * (d_prob - row_delta)).astype(BF16)
@@ -530,27 +552,30 @@
     d_key = turn(mul_left(d_score, query) * scale, -sine)
     d_value = mul_left(prob_low, d_head)
     d_qkv = jnp.concatenate((d_query, d_key, d_value), axis=1).astype(BF16)
-    d_qkv, gate_sum, up_parts, output_part = join((d_qkv, gate_sum, up_parts, output_part))
-    output_parts = send_parts_dp(output_part)
-    up_sum = swap(add_parts(up_parts).astype(BF16).reshape(groups, shard, slice_ff), CTX)
+    d_qkv, gate_up_sum, output_parts = join((d_qkv, gate_up_sum, output_parts))
+    gate_sum, up_sum = gate_up_sum[0], gate_up_sum[1]
     dn_part_one = mul_right(d_qkv, qkv_w).astype(BF16)
-    dn_part_one, xn_one, d_qkv, mlp_high, down_parts = join(
-        (dn_part_one, xn_one, d_qkv, mlp_high, down_parts)
-    )
+    dn_part_one, xn_one, d_qkv, mlp_sum = join((dn_part_one, xn_one, d_qkv, mlp_sum))
     dn_one = scatter(dn_part_one, CTX)
-    result = hid_res + jnp.concatenate((mlp_low, mlp_high), axis=1)
-    result = result.astype(BF16)[None]
-    down_grad = add_parts(down_parts)
-
-    qkv_parts = send_parts_dp(mul_left(xn_one, d_qkv).reshape(4, groups * shard, 3 * HD))
+    result = (hid_res + mlp_sum).astype(BF16)[None]
+
+    qkv_split = split_parts_dp(
+        mul_left(xn_one, d_qkv).astype(BF16).reshape(4, groups * shard, 3 * HD)
+    )
+    qkv_parts = qkv_split[:1] + send_parts_dp(qkv_split)
     column = add_parts(output_parts)
     chip = lax.axis_index(("half", "low"))
-    output_grad = take(column, chip)
+    output_parts = [take(column, chip)]
     for step in range(1, 4):
         block = take(column, (chip + step) % 4).astype(BF16)
-        output_grad = output_grad + turn_chips(block, step).astype(F32)
+        output_parts.append(turn_chips(block, step))
+    qkv_parts, output_parts, down_split = join((qkv_parts, output_parts, down_split))
     qkv_sum = add_parts(qkv_parts).astype(BF16)
     qkv_sum = swap(qkv_sum.reshape(groups, shard, 3 * HD), CTX)
+    output_grad = add_parts(output_parts)
+    down_parts = [split[:1] + send_parts_dp(split) for split in down_split]
+    down_grad = jnp.concatenate([add_parts(parts) for parts in down_parts], axis=1)
+
     def ungated(summed):
         blocks = summed.astype(F32).reshape(groups, shard, 4, share)
         return blocks.transpose(1, 2, 0, 3).reshape(shard, FF)

time: 803 us -> 753 us (0.938)
  waiting for transfers between devices: 310 us -> 279 us
  local copies, waits for them, and re-layouts: 126 us -> 105 us
    ppermute x33, waiting for transfers between devices: 196 us -> 139 us  [flip(): lax.ppermute(values, axis, [(i, i ^ bits) for i in range(lax.axis_size(ax...]
    all_to_all x8 -> x6, waiting for transfers between devices: 14.7 us -> 34.9 us  [swap(): return lax.all_to_all(values, axes, split_axis=0, concat_axis=0, tiled=True)]
    all_gather x3 -> x5, waiting for transfers between devices: 37.8 us -> 19.4 us  [gather(): return lax.all_gather(values, axes, axis=0, tiled=True)]
    convert_element_type x5 -> x0, local copies, waits for them, and re-layouts: 15 us -> none  [send_parts_dp(): take(parts, d ^ bits).astype(BF16)]
    reduce_scatter x4 -> x3, waiting for transfers between devices: 31.2 us -> 43.3 us  [scatter(): lax.psum_scatter(values, axes, scatter_dimension=0, tiled=True).astype(F32)]
    ppermute x6, waiting for transfers between devices: 30.1 us -> 41.6 us  [turn_chips(): return lax.ppermute(values, CTX, pairs)]
    all_to_all x8 -> x6, starting transfers between devices: 46.4 us -> 37.4 us  [swap(): return lax.all_to_all(values, axes, split_axis=0, concat_axis=0, tiled=True)]
    squeeze x3 -> x6, local copies, waits for them, and re-layouts: 4.56 us -> 12.8 us  [take(): return lax.dynamic_index_in_dim(values, index, 0, keepdims=False)]
  transfers between devices with their start and end apart: 54 -> 54, of which waited for: 23 -> 24; matrix products, arithmetic and copies ran while one was open for 40% -> 42% of each run, Pallas kernels for 0% -> 0%
where the time goes in v3:
time: 753 us; the launch traced here: 744 us
  waiting for transfers between devices  279 us (37%)
  matrix products  167 us (22%)
  local copies, waits for them, and re-layouts  105 us (14%)
  starting transfers between devices  93.9 us (12%)
  other arithmetic  83.7 us (11%)
  between operations  16.4 us (2%)
    ppermute x33, waiting for transfers between devices, flip(): lax.ppermute(values, axis, [(i, i ^ bits) for i in range(lax.axis_size(ax...  139 us
    dot_general x8, matrix products, mul_right(): lax.dot_general(first_op, second_op, (((1,), (1,)), ((), ())), preferred_...  68.6 us
    dot_general x7, matrix products, mul_plain(): return jnp.dot(first_op, second_op, preferred_element_type=jnp.float32)  52.9 us
    dot_general x8, matrix products, mul_left(): lax.dot_general(first_op, second_op, (((0,), (0,)), ((), ())), preferred_...  45.5 us
    reduce_scatter x3, waiting for transfers between devices, scatter(): lax.psum_scatter(values, axes, scatter_dimension=0, tiled=True).astype(F32)  43.3 us
    ppermute x6, waiting for transfers between devices, turn_chips(): return lax.ppermute(values, CTX, pairs)  41.6 us
    ppermute x33, starting transfers between devices, flip(): lax.ppermute(values, axis, [(i, i ^ bits) for i in range(lax.axis_size(ax...  38.7 us
    all_to_all x6, starting transfers between devices, swap(): return lax.all_to_all(values, axes, split_axis=0, concat_axis=0, tiled=True)  37.4 us
  transfers between devices with their start and end apart: 54, of which 24 were waited for; matrix products, arithmetic and copies ran while one was open for 42% of the time, Pallas kernels for 0%

profile of v3, /device:TPU:8, one launch (start us, length us, event | category | flops | bytes accessed | tf_op | source)
XLA Modules:
  0.0 744.3 jit_solution(11693754825689218646)
XLA Ops:
  15.2 5.3 all-to-all-start
  43.3 13.6 %collective-permute-done.4 = bf16[256,2048]{1,0:T(8,128)(2,1)} collective-permute-done((bf16[256,2048]{1,0:T(8,128)(2,1)}, bf16[256,2048]{1,0:T(8,128)(2,1)}, u32[]{:S(2)}, u32[]{:S(2)}) %collective-permute-start.4) | collective-permute-done | bytes 1048608 | tf_op jit(solution)/shard_map/ppermute | solution.py:302
  74.3 11.5 %collective-permute-done.6 = bf16[64,2048]{1,0:T(8,128)(2,1)S(1)} collective-permute-done((bf16[64,2048]{1,0:T(8,128)(2,1)S(1)}, bf16[64,2048]{1,0:T(8,128)(2,1)S(1)}, u32[]{:S(2)}, u32[]{:S(2)}) %collective-permute-start.6) | collective-permute-done | bytes 262176 | tf_op jit(solution)/shard_map/ppermute | solution.py:335
  88.5 17.5 %collective-permute-done.7 = bf16[64,2048]{1,0:T(8,128)(2,1)S(1)} collective-permute-done((bf16[64,2048]{1,0:T(8,128)(2,1)S(1)}, bf16[64,2048]{1,0:T(8,128)(2,1)S(1)}, u32[]{:S(2)}, u32[]{:S(2)}) %collective-permute-start.7) | collective-permute-done | bytes 262176 | tf_op jit(solution)/shard_map/ppermute | solution.py:335
  115.8 4.1 fusion
  119.9 6.6 fusion.1
  126.5 6.9 all-to-all-start.1
  133.4 8.5 %fusion.54 = f32[1536,768]{0,1:T(8,128)S(1)} fusion(bf16[1536,2048]{1,0:T(8,128)(2,1)} %fusion.1, bf16[2048,768]{1,0:T(8,128)(2,1)} %bitcast.11), kind=kOutput, calls=%fused_computation.200 | convolution fusion | flops 4831838208 | bytes 14155776 | tf_op jit(solution)/shard_map/dot_general | solution.py:20
  152.3 8.5 %collective-permute-done.10 = bf16[4,64,2048]{2,1,0:T(8,128)(2,1)} collective-permute-done((bf16[4,64,2048]{2,1,0:T(8,128)(2,1)}, bf16[4,64,2048]{2,1,0:T(8,128)(2,1)}, u32[]{:S(2)}, u32[]{:S(2)}) %collective-permute-start.10) | collective-permute-done | bytes 1048608 | tf_op jit(solution)/shard_map/ppermute | solution.py:302
  165.4 11.4 %all-to-all-done.1 = bf16[8,64,1024]{2,1,0:T(8,128)(2,1)} async-done(((bf16[8,64,1024]{2,1,0:T(8,128)(2,1)}), bf16[8,64,1024]{2,1,0:T(8,128)(2,1)}, u32[]{:S(2)}, u32[]{:S(2)}) %all-to-all-start.1) | async-done | bytes 1048608 | tf_op jit(solution)/shard_map/all_to_all | solution.py:365
  177.6 7.7 %all-to-all-start.2 = ((bf16[8,64,1024]{2,1,0:T(8,128)(2,1)}), bf16[8,64,1024]{2,1,0:T(8,128)(2,1)S(1)}, u32[]{:S(2)}, u32[]{:S(2)}) async-start(bf16[8,64,1024]{2,1,0:T(8,128)(2,1)} %reshape.216), calls=%async_computation.2 | async-start | bytes 2097152 | tf_op jit(solution)/shard_map/all_to_all | solution.py:365
  185.3 3.0 fusion.53
  195.0 13.4 %all-to-all-done.2 = bf16[8,64,1024]{2,1,0:T(8,128)(2,1)S(1)} async-done(((bf16[8,64,1024]{2,1,0:T(8,128)(2,1)}), bf16[8,64,1024]{2,1,0:T(8,128)(2,1)S(1)}, u32[]{:S(2)}, u32[]{:S(2)}) %all-to-all-start.2) | async-done | bytes 1048608 | tf_op jit(solution)/shard_map/all_to_all | solution.py:365
  209.3 6.9 all-to-all-start.3
  216.3 5.1 select_bitcast_fusion.1
  221.4 6.4 pad_maximum_fusion
  227.7 6.0 all-to-all-done.3
  234.7 5.7 multiply_reduce_fusion.2
  248.9 19.0 %collective-permute-done.13 = bf16[512,1024]{1,0:T(8,128)(2,1)S(1)} collective-permute-done((bf16[512,1024]{1,0:T(8,128)(2,1)S(1)}, bf16[512,1024]{1,0:T(8,128)(2,1)S(1)}, u32[]{:S(2)}, u32[]{:S(2)}) %collective-permute-start.13) | collective-permute-done | bytes 1048608 | tf_op jit(solution)/shard_map/ppermute | solution.py:302
  268.9 21.7 %collective-permute-done.14 = bf16[512,1024]{1,0:T(8,128)(2,1)S(1)} collective-permute-done((bf16[512,1024]{1,0:T(8,128)(2,1)S(1)}, bf16[512,1024]{1,0:T(8,128)(2,1)S(1)}, u32[]{:S(2)}, u32[]{:S(2)}) %collective-permute-start.14) | collective-permute-done | bytes 1048608 | tf_op jit(solution)/shard_map/ppermute | solution.py:302
  292.8 13.1 %all-gather.7.cloned.1.call-done = bf16[1536,2048]{1,0:T(8,128)(2,1)} async-done(((bf16[192,2048]{1,0:T(8,128)(2,1)}), bf16[1536,2048]{1,0:T(8,128)(2,1)}) %all-gather.7.cloned.1.call-update) | async-done | bytes 6291472 | tf_op jit(solution)/shard_map/all_gather | solution.py:381
  306.2 10.1 %fusion.55 = f32[1536,1024]{1,0:T(8,128)S(1)} fusion(bf16[1536,2048]{1,0:T(8,128)(2,1)} %all-gather.7.cloned.1.call-done, bf16[2048,1024]{1,0:T(8,128)(2,1)} %all-gather.9.cloned.1.call-done), kind=kOutput, calls=%fused_computation.201 | convolution fusion | flops 6442450944 | bytes 16777216 | tf_op jit(solution)/shard_map/dot_general | solution.py:20
  316.3 13.1 %multiply_convert_fusion.3 = (bf16[1536,1024]{1,0:T(8,128)(2,1)S(1)}, f32[1536,1024]{1,0:T(8,128)}) fusion(f32[1536,1024]{1,0:T(8,128)S(1)} %fusion.55, bf16[1536,2048]{1,0:T(8,128)(2,1)S(1)} %copy-done.54, bf16[2048,1024]{1,0:T(8,128)(2,1)} %bitcast.39), kind=kOutput, calls=%fused_computation.20 | convolution fusion | flops 6451888128 | bytes 26214400 | tf_op jit(solution)/shard_map/dot_general | solution.py:20
  331.1 8.7 %convolution_convert_fusion.1 = bf16[1536,2048]{1,0:T(8,128)(2,1)} fusion(bf16[1536,1024]{1,0:T(8,128)(2,1)S(1)} %get-tuple-element.156, bf16[1024,2048]{1,0:T(8,128)(2,1)S(1)} %bitcast.268), kind=kOutput, calls=%fused_computation.16 | convolution fusion | flops 6445596672 | bytes 13631488 | tf_op jit(solution)/shard_map/dot_general | solution.py:20
  339.8 6.3 all-gather.13.cloned.1.call-done
  346.3 8.8 %fusion.13 = f32[1536,1024]{1,0:T(8,128)} fusion(bf16[1536,1024]{1,0:T(8,128)(2,1)} %all-gather.11.cloned.1.call-done, bf16[1024,2048]{1,0:T(8,128)(2,1)} %bitcast.267), kind=kOutput, calls=%fused_computation.53 | convolution fusion | flops 3221225472 | bytes 11534336 | tf_op jit(solution)/shard_map/dot_general | solution.py:24
  355.1 11.4 %multiply_convert_fusion.1 = (bf16[1536,1024]{1,0:T(8,128)(2,1)}, bf16[1536,1024]{1,0:T(8,128)(2,1)S(1)}) fusion(f32[1536,1024]{1,0:T(8,128)} %copy-done.61, f32[1536,1024]{1,0:T(8,128)} %get-tuple-element.137, f32[1536,1024]{1,0:T(8,128)} %fusion.13, bf16[1536,1024]{1,0:T(8,128)(2,1)S(1)} %copy-done.57, bf16[1024,2048]{1,0:T(8,128)(2,1)S(1)} %bitcast.269), kind=kOutput, calls=%fused_computation.17 | convolution fusion | flops 3243245568 | bytes 30408704 | tf_op jit(solution)/shard_map/dot_general | solution.py:24
  366.5 7.2 convolution_convert_fusion.3
  373.8 7.3 convolution_convert_fusion.2
  381.1 4.2 dynamic-slice_bitcast_fusion.4
  388.2 9.6 %fusion.56 = f32[1536,2048]{1,0:T(8,128)} fusion(bf16[1536,1024]{1,0:T(8,128)(2,1)S(1)} %get-tuple-element.140, bf16[2048,1024]{1,0:T(8,128)(2,1)S(1)} %copy-done.55), kind=kOutput, calls=%fused_computation.202 | convolution fusion | flops 6442450944 | bytes 19922944 | tf_op jit(solution)/shard_map/dot_general | solution.py:24
  397.8 13.2 %add_convert_fusion = bf16[1536,2048]{1,0:T(8,128)(2,1)} fusion(f32[1536,2048]{1,0:T(8,128)} %fusion.56, bf16[1536,1024]{1,0:T(8,128)(2,1)} %get-tuple-element.141, bf16[2048,1024]{1,0:T(8,128)(2,1)} %bitcast.39), kind=kOutput, calls=%fused_computation.4 | convolution fusion | flops 6448742400 | bytes 26214400 | tf_op jit(solution)/shard_map/dot_general | solution.py:24
  411.0 4.2 reduce-scatter.4.cloned.1.call-done
  432.3 6.5 convolution_convert_fusion.9
  441.5 3.8 convolution_convert_fusion.10
  446.8 39.2 %reduce-scatter.6.cloned.1.call-done = bf16[192,2048]{1,0:T(8,128)(2,1)} async-done(((bf16[1536,2048]{1,0:T(8,128)(2,1)}), bf16[192,2048]{1,0:T(8,128)(2,1)}) %reduce-scatter.6.cloned.1.call-update) | async-done | bytes 786448 | tf_op jit(solution)/shard_map/reduce_scatter | solution.py:385
  487.4 10.8 %collective-permute-done.21 = bf16[512,1024]{1,0:T(8,128)(2,1)} collective-permute-done((bf16[512,1024]{1,0:T(8,128)(2,1)}, bf16[512,1024]{1,0:T(8,128)(2,1)}, u32[]{:S(2)}, u32[]{:S(2)}) %collective-permute-start.21) | collective-permute-done | bytes 1048608 | tf_op jit(solution)/shard_map/ppermute | solution.py:302
  499.9 6.5 convolution_convert_fusion.8
  507.3 6.3 all-to-all-start.4
  513.7 3.2 fusion.32
  521.2 3.8 convolution_convert_fusion.4
  527.1 4.1 all-to-all-done.4
  531.2 6.7 multiply_reduce_fusion
  545.4 7.8 %all-to-all-start.5 = ((bf16[2,8,64,1024]{3,2,0,1:T(8,128)(2,1)}), bf16[2,8,64,1024]{3,2,0,1:T(8,128)(2,1)}, u32[]{:S(2)}, u32[]{:S(2)}) async-start(bf16[2,8,64,1024]{3,2,0,1:T(8,128)(2,1)} %copy.62), calls=%async_computation.7 | async-start | bytes 4194304 | tf_op jit(solution)/shard_map/all_to_all | solution.py:546
  553.5 4.1 convolution_multiply_fusion.1
  561.3 5.7 convolution_convert_fusion.6
  571.7 12.0 %collective-permute-done.24 = bf16[4,64,2048]{2,1,0:T(8,128)(2,1)S(1)} collective-permute-done((bf16[4,64,2048]{2,1,0:T(8,128)(2,1)S(1)}, bf16[4,64,2048]{2,1,0:T(8,128)(2,1)S(1)}, u32[]{:S(2)}, u32[]{:S(2)}) %collective-permute-start.24) | collective-permute-done | bytes 1048608 | tf_op jit(solution)/shard_map/ppermute | solution.py:302
  583.7 22.8 %collective-permute-done.25 = bf16[4,64,2048]{2,1,0:T(8,128)(2,1)S(1)} collective-permute-done((bf16[4,64,2048]{2,1,0:T(8,128)(2,1)S(1)}, bf16[4,64,2048]{2,1,0:T(8,128)(2,1)S(1)}, u32[]{:S(2)}, u32[]{:S(2)}) %collective-permute-start.25) | collective-permute-done | bytes 1048608 | tf_op jit(solution)/shard_map/ppermute | solution.py:302
  607.5 9.3 %convolution_convert_fusion = bf16[1536,2048]{1,0:T(8,128)(2,1)} fusion(bf16[1536,768]{0,1:T(8,128)(2,1)} %pad_maximum_fusion.1, bf16[2048,768]{1,0:T(8,128)(2,1)} %bitcast.11), kind=kOutput, calls=%fused_computation.15 | convolution fusion | flops 4834983936 | bytes 11796480 | tf_op jit(solution)/shard_map/dot_general | solution.py:24
  618.2 3.0 convert_add_fusion
  624.9 8.7 %convolution_convert_fusion.5 = bf16[2048,768]{1,0:T(8,128)(2,1)S(1)} fusion(bf16[1536,2048]{1,0:T(8,128)(2,1)} %fusion.1, bf16[1536,768]{0,1:T(8,128)(2,1)S(1)} %copy-done.26), kind=kOutput, calls=%fused_computation.27 | convolution fusion | flops 4833411072 | bytes 11796480 | tf_op jit(solution)/shard_map/dot_general | solution.py:30
  642.0 4.0 slice_convert_fusion.1
  646.0 3.2 reshape.254
  654.6 3.2 reshape.256
  657.7 2.8 copy.67
  663.8 3.8 collective-permute-done.31
  667.6 6.7 collective-permute-done.32
  675.5 3.2 broadcast_multiply_fusion
  683.4 2.9 add_convert_fusion.3
  686.4 4.2 all-to-all-start.6
  693.9 11.3 %collective-permute-done.34 = bf16[256,1024]{1,0:T(8,128)(2,1)} collective-permute-done((bf16[256,1024]{1,0:T(8,128)(2,1)}, bf16[256,1024]{1,0:T(8,128)(2,1)}, u32[]{:S(2)}, u32[]{:S(2)}) %collective-permute-start.34) | collective-permute-done | bytes 524320 | tf_op jit(solution)/shard_map/ppermute | solution.py:302
  707.0 5.1 collective-permute-done.36
  712.0 12.1 %collective-permute-done.37 = bf16[256,1024]{1,0:T(8,128)(2,1)} collective-permute-done((bf16[256,1024]{1,0:T(8,128)(2,1)}, bf16[256,1024]{1,0:T(8,128)(2,1)}, u32[]{:S(2)}, u32[]{:S(2)}) %collective-permute-start.37) | collective-permute-done | bytes 524320 | tf_op jit(solution)/shard_map/ppermute | solution.py:302
  733.1 3.9 fusion.35
  (330 shorter events, 191.3 us)
Async XLA Ops:
  7.2 105.1 %all-gather.15.cloned.1.call-start = ((), (), s32[]{:S(2)}) async-start(), calls=%async_computation.17 | async-start | bytes 7077888 | tf_op jit(solution)/shard_map/all_gather | solution.py:381
  7.9 33.0 %collective-permute-start.3 = (bf16[256,2048]{1,0:T(8,128)(2,1)}, bf16[256,2048]{1,0:T(8,128)(2,1)}, u32[]{:S(2)}, u32[]{:S(2)}) collective-permute-start(bf16[256,2048]{1,0:T(8,128)(2,1)} %param.22), channel_id=1, source_target_pairs={{0,8},{8,0},{16,24},{24,16},{1,9},{9,1},{17,25},{25,17},{2,10},{10... | collective-permute-start | bytes 3145736 | tf_op jit(solution)/shard_map/ppermute | solution.py:302
  9.5 47.4 %collective-permute-start.4 = (bf16[256,2048]{1,0:T(8,128)(2,1)}, bf16[256,2048]{1,0:T(8,128)(2,1)}, u32[]{:S(2)}, u32[]{:S(2)}) collective-permute-start(bf16[256,2048]{1,0:T(8,128)(2,1)} %param.22), channel_id=1, source_target_pairs={{0,16},{8,24},{16,0},{24,8},{1,17},{9,25},{17,1},{25,9},{2,18},{10... | collective-permute-start | bytes 3145736 | tf_op jit(solution)/shard_map/ppermute | solution.py:302
  11.0 48.2 %collective-permute-start.5 = (bf16[256,2048]{1,0:T(8,128)(2,1)}, bf16[256,2048]{1,0:T(8,128)(2,1)}, u32[]{:S(2)}, u32[]{:S(2)}) collective-permute-start(bf16[256,2048]{1,0:T(8,128)(2,1)} %param.22), channel_id=1, source_target_pairs={{0,24},{8,16},{16,8},{24,0},{1,25},{9,17},{17,9},{25,1},{2,26},{10... | collective-permute-start | bytes 3145736 | tf_op jit(solution)/shard_map/ppermute | solution.py:302
  15.2 46.4 %all-to-all-start = ((bf16[8,64,768]{2,1,0:T(8,128)(2,1)}), bf16[8,64,768]{2,1,0:T(8,128)(2,1)}, u32[]{:S(2)}, u32[]{:S(2)}) async-start(bf16[8,64,768]{2,1,0:T(8,128)(2,1)} %copy.54), calls=%async_computation | async-start | bytes 1572864 | tf_op jit(solution)/shard_map/all_to_all | solution.py:365
  20.6 272.3 %all-gather.11.cloned.1.call-start = ((), (), s32[]{:S(2)}) async-start(), calls=%async_computation.12 | async-start | bytes 3538944 | tf_op jit(solution)/shard_map/all_gather | solution.py:381
  28.6 113.7 %copy-start.1 = (f32[1536,256]{0,1:T(8,128)}, f32[1536,256]{0,1:T(8,128)S(1)}, u32[]{:S(2)}) copy-start(f32[1536,256]{0,1:T(8,128)S(1)} %pad_maximum_fusion.4) | copy-start | bytes 4718596
  28.8 113.6 %copy-start.3 = (f32[1536,256]{0,1:T(8,128)}, f32[1536,256]{0,1:T(8,128)S(1)}, u32[]{:S(2)}) copy-start(f32[1536,256]{0,1:T(8,128)S(1)} %pad_maximum_fusion.5) | copy-start | bytes 4718596
  40.9 20.7 %copy-start.45 = (bf16[64,2048]{1,0:T(8,128)(2,1)S(1)}, bf16[64,2048]{1,0:T(8,128)(2,1)}, u32[]{:S(2)}) copy-start(bf16[64,2048]{1,0:T(8,128)(2,1)} %param.18) | copy-start | bytes 786436
  61.6 24.2 %collective-permute-start.6 = (bf16[64,2048]{1,0:T(8,128)(2,1)S(1)}, bf16[64,2048]{1,0:T(8,128)(2,1)S(1)}, u32[]{:S(2)}, u32[]{:S(2)}) collective-permute-start(bf16[64,2048]{1,0:T(8,128)(2,1)S(1)} %copy-done.45), channel_id=1, source_target_pairs={{0,2},{1,3},{2,4},{3,5},{4,6},{5,7},{6,0},{7,1},{8,10},{9,11},{10,... | collective-permute-start | bytes 786440 | tf_op jit(solution)/shard_map/ppermute | solution.py:335
  63.2 42.7 %collective-permute-start.7 = (bf16[64,2048]{1,0:T(8,128)(2,1)S(1)}, bf16[64,2048]{1,0:T(8,128)(2,1)S(1)}, u32[]{:S(2)}, u32[]{:S(2)}) collective-permute-start(bf16[64,2048]{1,0:T(8,128)(2,1)S(1)} %copy-done.45), channel_id=1, source_target_pairs={{0,4},{1,5},{2,6},{3,7},{4,0},{5,1},{6,2},{7,3},{8,12},{9,13},{10,... | collective-permute-start | bytes 786440 | tf_op jit(solution)/shard_map/ppermute | solution.py:335
  64.4 44.4 %collective-permute-start.8 = (bf16[64,2048]{1,0:T(8,128)(2,1)S(1)}, bf16[64,2048]{1,0:T(8,128)(2,1)S(1)}, u32[]{:S(2)}, u32[]{:S(2)}) collective-permute-start(bf16[64,2048]{1,0:T(8,128)(2,1)S(1)} %copy-done.45), channel_id=1, source_target_pairs={{0,6},{1,7},{2,0},{3,1},{4,2},{5,3},{6,4},{7,5},{8,14},{9,15},{10,... | collective-permute-start | bytes 786440 | tf_op jit(solution)/shard_map/ppermute | solution.py:335
  66.4 43.1 %collective-permute-start = (bf16[512,768]{1,0:T(8,128)(2,1)}, bf16[512,768]{1,0:T(8,128)(2,1)S(1)}, u32[]{:S(2)}, u32[]{:S(2)}) collective-permute-start(bf16[512,768]{1,0:T(8,128)(2,1)} %bitcast.4), channel_id=1, source_target_pairs={{0,8},{8,0},{16,24},{24,16},{1,9},{9,1},{17,25},{25,17},{2,10},{10... | collective-permute-start | bytes 2359304 | tf_op jit(solution)/shard_map/ppermute | solution.py:302
  66.4 44.0 %collective-permute-start.1 = (bf16[512,768]{1,0:T(8,128)(2,1)}, bf16[512,768]{1,0:T(8,128)(2,1)S(1)}, u32[]{:S(2)}, u32[]{:S(2)}) collective-permute-start(bf16[512,768]{1,0:T(8,128)(2,1)} %bitcast.4), channel_id=1, source_target_pairs={{0,16},{8,24},{16,0},{24,8},{1,17},{9,25},{17,1},{25,9},{2,18},{10... | collective-permute-start | bytes 2359304 | tf_op jit(solution)/shard_map/ppermute | solution.py:302
  85.8 25.6 %collective-permute-start.2 = (bf16[512,768]{1,0:T(8,128)(2,1)}, bf16[512,768]{1,0:T(8,128)(2,1)S(1)}, u32[]{:S(2)}, u32[]{:S(2)}) collective-permute-start(bf16[512,768]{1,0:T(8,128)(2,1)} %bitcast.4), channel_id=1, source_target_pairs={{0,24},{8,16},{16,8},{24,0},{1,25},{9,17},{17,9},{25,1},{2,26},{10... | collective-permute-start | bytes 2359304 | tf_op jit(solution)/shard_map/ppermute | solution.py:302
  112.3 37.3 %collective-permute-start.9 = (bf16[4,64,2048]{2,1,0:T(8,128)(2,1)}, bf16[4,64,2048]{2,1,0:T(8,128)(2,1)}, u32[]{:S(2)}, u32[]{:S(2)}) collective-permute-start(bf16[4,64,2048]{2,1,0:T(8,128)(2,1)} %bitcast_dynamic-update-slice_fusion.16), channel_id=1, source_target_pairs={{0,8},{8,0},{16,24},{24,16},{1,9},{9,1},{17,25},{25,17},{2,10},{10... | collective-permute-start | bytes 3145736 | tf_op jit(solution)/shard_map/ppermute | solution.py:302
  113.8 47.0 %collective-permute-start.10 = (bf16[4,64,2048]{2,1,0:T(8,128)(2,1)}, bf16[4,64,2048]{2,1,0:T(8,128)(2,1)}, u32[]{:S(2)}, u32[]{:S(2)}) collective-permute-start(bf16[4,64,2048]{2,1,0:T(8,128)(2,1)} %bitcast_dynamic-update-slice_fusion.16), channel_id=1, source_target_pairs={{0,16},{8,24},{16,0},{24,8},{1,17},{9,25},{17,1},{25,9},{2,18},{10... | collective-permute-start | bytes 3145736 | tf_op jit(solution)/shard_map/ppermute | solution.py:302
  115.3 47.7 %collective-permute-start.11 = (bf16[4,64,2048]{2,1,0:T(8,128)(2,1)}, bf16[4,64,2048]{2,1,0:T(8,128)(2,1)}, u32[]{:S(2)}, u32[]{:S(2)}) collective-permute-start(bf16[4,64,2048]{2,1,0:T(8,128)(2,1)} %bitcast_dynamic-update-slice_fusion.16), channel_id=1, source_target_pairs={{0,24},{8,16},{16,8},{24,0},{1,25},{9,17},{17,9},{25,1},{2,26},{10... | collective-permute-start | bytes 3145736 | tf_op jit(solution)/shard_map/ppermute | solution.py:302
  126.5 50.3 %all-to-all-start.1 = ((bf16[8,64,1024]{2,1,0:T(8,128)(2,1)}), bf16[8,64,1024]{2,1,0:T(8,128)(2,1)}, u32[]{:S(2)}, u32[]{:S(2)}) async-start(bf16[8,64,1024]{2,1,0:T(8,128)(2,1)} %reshape.214), calls=%async_computation.1 | async-start | bytes 2097152 | tf_op jit(solution)/shard_map/all_to_all | solution.py:365
  133.4 159.4 %all-gather.9.cloned.1.call-start = ((), (), s32[]{:S(2)}) async-start(), calls=%async_computation.11 | async-start | bytes 5242880 | tf_op jit(solution)/shard_map/all_gather | solution.py:381
  149.6 40.1 %copy-start.37 = (bf16[1536,256]{0,1:T(8,128)(2,1)}, bf16[1536,256]{0,1:T(8,128)(2,1)S(1)}, u32[]{:S(2)}) copy-start(bf16[1536,256]{0,1:T(8,128)(2,1)S(1)} %slice.125) | copy-start | bytes 2359300
  163.0 22.2 %copy-start.39 = (bf16[1536,256]{0,1:T(8,128)(2,1)S(1)}, bf16[1536,256]{0,1:T(8,128)(2,1)}, u32[]{:S(2)}) copy-start(bf16[1536,256]{0,1:T(8,128)(2,1)} %get-tuple-element.120) | copy-start | bytes 2359300
  176.8 39.5 %collective-permute-start.12 = (bf16[4,4,64,2048]{3,2,1,0:T(8,128)(2,1)}, bf16[4,4,64,2048]{3,2,1,0:T(8,128)(2,1)}, u32[]{:S(2)}, u32[]{:S(2)}) collective-permute-start(bf16[4,4,64,2048]{3,2,1,0:T(8,128)(2,1)} %bitcast_dynamic-update-slice_fusion.4), channel_id=1, source_target_pairs={{0,1},{1,0},{2,3},{3,2},{4,5},{5,4},{6,7},{7,6},{8,9},{9,8},{10,11... | collective-permute-start | bytes 12582920 | tf_op jit(solution)/shard_map/ppermute | solution.py:302
  177.6 30.8 %all-to-all-start.2 = ((bf16[8,64,1024]{2,1,0:T(8,128)(2,1)}), bf16[8,64,1024]{2,1,0:T(8,128)(2,1)S(1)}, u32[]{:S(2)}, u32[]{:S(2)}) async-start(bf16[8,64,1024]{2,1,0:T(8,128)(2,1)} %reshape.216), calls=%async_computation.2 | async-start | bytes 2097152 | tf_op jit(solution)/shard_map/all_to_all | solution.py:365
  209.3 24.4 %all-to-all-start.3 = ((bf16[8,192,256]{2,1,0:T(8,128)(2,1)}), bf16[8,192,256]{2,1,0:T(8,128)(2,1)S(1)}, u32[]{:S(2)}, u32[]{:S(2)}) async-start(bf16[8,192,256]{2,1,0:T(8,128)(2,1)} %bitcast.27), calls=%async_computation.3 | async-start | bytes 1572864 | tf_op jit(solution)/shard_map/all_to_all | solution.py:365
  216.3 89.6 %all-gather.7.cloned.1.call-start = ((), (), s32[]{:S(2)}) async-start(), calls=%async_computation.10 | async-start | bytes 7077888 | tf_op jit(solution)/shard_map/all_gather | solution.py:381
  241.4 104.7 %all-gather.13.cloned.1.call-start = ((), (), s32[]{:S(2)}) async-start(), calls=%async_computation.13 | async-start | bytes 3538944 | tf_op jit(solution)/shard_map/all_gather | solution.py:381
  241.9 26.0 %collective-permute-start.13 = (bf16[512,1024]{1,0:T(8,128)(2,1)S(1)}, bf16[512,1024]{1,0:T(8,128)(2,1)S(1)}, u32[]{:S(2)}, u32[]{:S(2)}) collective-permute-start(bf16[512,1024]{1,0:T(8,128)(2,1)S(1)} %bitcast.263), channel_id=1, source_target_pairs={{0,8},{8,0},{16,24},{24,16},{1,9},{9,1},{17,25},{25,17},{2,10},{10... | collective-permute-start | bytes 3145736 | tf_op jit(solution)/shard_map/ppermute | solution.py:302
  243.3 47.3 %collective-permute-start.14 = (bf16[512,1024]{1,0:T(8,128)(2,1)S(1)}, bf16[512,1024]{1,0:T(8,128)(2,1)S(1)}, u32[]{:S(2)}, u32[]{:S(2)}) collective-permute-start(bf16[512,1024]{1,0:T(8,128)(2,1)S(1)} %bitcast.264), channel_id=1, source_target_pairs={{0,16},{8,24},{16,0},{24,8},{1,17},{9,25},{17,1},{25,9},{2,18},{10... | collective-permute-start | bytes 3145736 | tf_op jit(solution)/shard_map/ppermute | solution.py:302
  244.8 46.9 %collective-permute-start.15 = (bf16[512,1024]{1,0:T(8,128)(2,1)S(1)}, bf16[512,1024]{1,0:T(8,128)(2,1)S(1)}, u32[]{:S(2)}, u32[]{:S(2)}) collective-permute-start(bf16[512,1024]{1,0:T(8,128)(2,1)S(1)} %bitcast.265), channel_id=1, source_target_pairs={{0,24},{8,16},{16,8},{24,0},{1,25},{9,17},{17,9},{25,1},{2,26},{10... | collective-permute-start | bytes 3145736 | tf_op jit(solution)/shard_map/ppermute | solution.py:302
  305.9 109.2 %reduce-scatter.4.cloned.1.call-start = ((), (), s32[]{:S(2)}) async-start(), calls=%async_computation.14 | async-start | bytes 7077888 | tf_op jit(solution)/shard_map/reduce_scatter | solution.py:385
  346.2 139.7 %reduce-scatter.6.cloned.1.call-start = ((), (), s32[]{:S(2)}) async-start(), calls=%async_computation.15 | async-start | bytes 7077888 | tf_op jit(solution)/shard_map/reduce_scatter | solution.py:385
  346.3 20.3 %slice-start.3 = ((s8[6291456]{0:T(1024)(128)(4,1)}), s8[4194304]{0:T(1024)(128)(4,1)S(1)}, s32[]{:S(2)}) async-start(s8[6291456]{0:T(1024)(128)(4,1)} %bitcast.293), calls=%async_computation.21 | async-start | bytes 8388608
  385.2 32.4 %collective-permute-start.16 = (bf16[512,1024]{1,0:T(8,128)(2,1)}, bf16[512,1024]{1,0:T(8,128)(2,1)S(1)}, u32[]{:S(2)}, u32[]{:S(2)}) collective-permute-start(bf16[512,1024]{1,0:T(8,128)(2,1)} %get-tuple-element.143), channel_id=1, source_target_pairs={{0,8},{8,0},{16,24},{24,16},{1,9},{9,1},{17,25},{25,17},{2,10},{10... | collective-permute-start | bytes 3145736 | tf_op jit(solution)/shard_map/ppermute | solution.py:302
  386.7 30.9 %collective-permute-start.17 = (bf16[512,1024]{1,0:T(8,128)(2,1)}, bf16[512,1024]{1,0:T(8,128)(2,1)}, u32[]{:S(2)}, u32[]{:S(2)}) collective-permute-start(bf16[512,1024]{1,0:T(8,128)(2,1)} %get-tuple-element.144), channel_id=1, source_target_pairs={{0,16},{8,24},{16,0},{24,8},{1,17},{9,25},{17,1},{25,9},{2,18},{10... | collective-permute-start | bytes 3145736 | tf_op jit(solution)/shard_map/ppermute | solution.py:302
  418.6 3.5 collective-permute-start.22
  426.5 60.9 %collective-permute-start.18 = (bf16[512,1024]{1,0:T(8,128)(2,1)}, bf16[512,1024]{1,0:T(8,128)(2,1)}, u32[]{:S(2)}, u32[]{:S(2)}) collective-permute-start(bf16[512,1024]{1,0:T(8,128)(2,1)} %get-tuple-element.152), channel_id=1, source_target_pairs={{0,24},{8,16},{16,8},{24,0},{1,25},{9,17},{17,9},{25,1},{2,26},{10... | collective-permute-start | bytes 3145736 | tf_op jit(solution)/shard_map/ppermute | solution.py:302
  428.8 58.5 %collective-permute-start.19 = (bf16[512,1024]{1,0:T(8,128)(2,1)}, bf16[512,1024]{1,0:T(8,128)(2,1)}, u32[]{:S(2)}, u32[]{:S(2)}) collective-permute-start(bf16[512,1024]{1,0:T(8,128)(2,1)} %get-tuple-element.153), channel_id=1, source_target_pairs={{0,8},{8,0},{16,24},{24,16},{1,9},{9,1},{17,25},{25,17},{2,10},{10... | collective-permute-start | bytes 3145736 | tf_op jit(solution)/shard_map/ppermute | solution.py:302
  429.4 57.9 %collective-permute-start.20 = (bf16[512,1024]{1,0:T(8,128)(2,1)}, bf16[512,1024]{1,0:T(8,128)(2,1)}, u32[]{:S(2)}, u32[]{:S(2)}) collective-permute-start(bf16[512,1024]{1,0:T(8,128)(2,1)} %get-tuple-element.154), channel_id=1, source_target_pairs={{0,16},{8,24},{16,0},{24,8},{1,17},{9,25},{17,1},{25,9},{2,18},{10... | collective-permute-start | bytes 3145736 | tf_op jit(solution)/shard_map/ppermute | solution.py:302
  430.0 68.2 %collective-permute-start.21 = (bf16[512,1024]{1,0:T(8,128)(2,1)}, bf16[512,1024]{1,0:T(8,128)(2,1)}, u32[]{:S(2)}, u32[]{:S(2)}) collective-permute-start(bf16[512,1024]{1,0:T(8,128)(2,1)} %get-tuple-element.155), channel_id=1, source_target_pairs={{0,24},{8,16},{16,8},{24,0},{1,25},{9,17},{17,9},{25,1},{2,26},{10... | collective-permute-start | bytes 3145736 | tf_op jit(solution)/shard_map/ppermute | solution.py:302
  499.9 21.3 %collective-permute-start.23 = (bf16[192,2048]{1,0:T(8,128)(2,1)}, bf16[192,2048]{1,0:T(8,128)(2,1)}, u32[]{:S(2)}, u32[]{:S(2)}) collective-permute-start(bf16[192,2048]{1,0:T(8,128)(2,1)} %fusion.49), channel_id=1, source_target_pairs={{0,1},{1,0},{2,3},{3,2},{4,5},{5,4},{6,7},{7,6},{8,9},{9,8},{10,11... | collective-permute-start | bytes 2359304 | tf_op jit(solution)/shard_map/ppermute | solution.py:302
  507.3 23.9 %all-to-all-start.4 = ((bf16[8,192,256]{2,1,0:T(8,128)(2,1)}), bf16[8,192,256]{2,1,0:T(8,128)(2,1)}, u32[]{:S(2)}, u32[]{:S(2)}) async-start(bf16[8,192,256]{2,1,0:T(8,128)(2,1)} %bitcast.275), calls=%async_computation.6 | async-start | bytes 1572864 | tf_op jit(solution)/shard_map/all_to_all | solution.py:365
  545.4 62.1 %all-to-all-start.5 = ((bf16[2,8,64,1024]{3,2,0,1:T(8,128)(2,1)}), bf16[2,8,64,1024]{3,2,0,1:T(8,128)(2,1)}, u32[]{:S(2)}, u32[]{:S(2)}) async-start(bf16[2,8,64,1024]{3,2,0,1:T(8,128)(2,1)} %copy.62), calls=%async_computation.7 | async-start | bytes 4194304 | tf_op jit(solution)/shard_map/all_to_all | solution.py:546
  553.2 178.1 %reduce-scatter.8.cloned.1.call-start = ((), (), s32[]{:S(2)}) async-start(), calls=%async_computation.16 | async-start | bytes 7077888 | tf_op jit(solution)/shard_map/reduce_scatter | solution.py:385
  557.6 26.1 %collective-permute-start.24 = (bf16[4,64,2048]{2,1,0:T(8,128)(2,1)S(1)}, bf16[4,64,2048]{2,1,0:T(8,128)(2,1)S(1)}, u32[]{:S(2)}, u32[]{:S(2)}) collective-permute-start(bf16[4,64,2048]{2,1,0:T(8,128)(2,1)S(1)} %copy-done.31), channel_id=1, source_target_pairs={{0,8},{8,0},{16,24},{24,16},{1,9},{9,1},{17,25},{25,17},{2,10},{10... | collective-permute-start | bytes 3145736 | tf_op jit(solution)/shard_map/ppermute | solution.py:302
  559.1 47.4 %collective-permute-start.25 = (bf16[4,64,2048]{2,1,0:T(8,128)(2,1)S(1)}, bf16[4,64,2048]{2,1,0:T(8,128)(2,1)S(1)}, u32[]{:S(2)}, u32[]{:S(2)}) collective-permute-start(bf16[4,64,2048]{2,1,0:T(8,128)(2,1)S(1)} %copy-done.30), channel_id=1, source_target_pairs={{0,16},{8,24},{16,0},{24,8},{1,17},{9,25},{17,1},{25,9},{2,18},{10... | collective-permute-start | bytes 3145736 | tf_op jit(solution)/shard_map/ppermute | solution.py:302
  560.6 46.9 %collective-permute-start.26 = (bf16[4,64,2048]{2,1,0:T(8,128)(2,1)S(1)}, bf16[4,64,2048]{2,1,0:T(8,128)(2,1)}, u32[]{:S(2)}, u32[]{:S(2)}) collective-permute-start(bf16[4,64,2048]{2,1,0:T(8,128)(2,1)S(1)} %copy-done.29), channel_id=1, source_target_pairs={{0,24},{8,16},{16,8},{24,0},{1,25},{9,17},{17,9},{25,1},{2,26},{10... | collective-permute-start | bytes 3145736 | tf_op jit(solution)/shard_map/ppermute | solution.py:302
  583.7 22.8 %copy-start.35 = (bf16[4,64,2048]{2,1,0:T(8,128)(2,1)}, bf16[4,64,2048]{2,1,0:T(8,128)(2,1)S(1)}, u32[]{:S(2)}) copy-start(bf16[4,64,2048]{2,1,0:T(8,128)(2,1)S(1)} %collective-permute-done.24) | copy-start | bytes 3145732
  623.4 16.7 %collective-permute-start.30 = (bf16[64,2048]{1,0:T(8,128)(2,1)S(1)}, bf16[64,2048]{1,0:T(8,128)(2,1)S(1)}, u32[]{:S(2)}, u32[]{:S(2)}) collective-permute-start(bf16[64,2048]{1,0:T(8,128)(2,1)S(1)} %get-tuple-element.244), channel_id=1, source_target_pairs={{0,2},{1,3},{2,4},{3,5},{4,6},{5,7},{6,0},{7,1},{8,10},{9,11},{10,... | collective-permute-start | bytes 786440 | tf_op jit(solution)/shard_map/ppermute | solution.py:335
  635.3 38.9 %collective-permute-start.27 = (bf16[512,768]{1,0:T(8,128)(2,1)}, bf16[512,768]{1,0:T(8,128)(2,1)}, u32[]{:S(2)}, u32[]{:S(2)}) collective-permute-start(bf16[512,768]{1,0:T(8,128)(2,1)} %get-tuple-element.233), channel_id=1, source_target_pairs={{0,8},{8,0},{16,24},{24,16},{1,9},{9,1},{17,25},{25,17},{2,10},{10... | collective-permute-start | bytes 2359304 | tf_op jit(solution)/shard_map/ppermute | solution.py:302
  635.7 38.6 %collective-permute-start.28 = (bf16[512,768]{1,0:T(8,128)(2,1)}, bf16[512,768]{1,0:T(8,128)(2,1)}, u32[]{:S(2)}, u32[]{:S(2)}) collective-permute-start(bf16[512,768]{1,0:T(8,128)(2,1)} %get-tuple-element.232), channel_id=1, source_target_pairs={{0,16},{8,24},{16,0},{24,8},{1,17},{9,25},{17,1},{25,9},{2,18},{10... | collective-permute-start | bytes 2359304 | tf_op jit(solution)/shard_map/ppermute | solution.py:302
  637.4 36.9 %collective-permute-start.29 = (bf16[512,768]{1,0:T(8,128)(2,1)}, bf16[512,768]{1,0:T(8,128)(2,1)}, u32[]{:S(2)}, u32[]{:S(2)}) collective-permute-start(bf16[512,768]{1,0:T(8,128)(2,1)} %get-tuple-element.231), channel_id=1, source_target_pairs={{0,24},{8,16},{16,8},{24,0},{1,25},{9,17},{17,9},{25,1},{2,26},{10... | collective-permute-start | bytes 2359304 | tf_op jit(solution)/shard_map/ppermute | solution.py:302
  638.8 28.7 %collective-permute-start.31 = (bf16[64,2048]{1,0:T(8,128)(2,1)}, bf16[64,2048]{1,0:T(8,128)(2,1)}, u32[]{:S(2)}, u32[]{:S(2)}) collective-permute-start(bf16[64,2048]{1,0:T(8,128)(2,1)} %get-tuple-element.243), channel_id=1, source_target_pairs={{0,4},{1,5},{2,6},{3,7},{4,0},{5,1},{6,2},{7,3},{8,12},{9,13},{10,... | collective-permute-start | bytes 786440 | tf_op jit(solution)/shard_map/ppermute | solution.py:335
  640.1 34.2 %collective-permute-start.32 = (bf16[64,2048]{1,0:T(8,128)(2,1)}, bf16[64,2048]{1,0:T(8,128)(2,1)}, u32[]{:S(2)}, u32[]{:S(2)}) collective-permute-start(bf16[64,2048]{1,0:T(8,128)(2,1)} %get-tuple-element.242), channel_id=1, source_target_pairs={{0,6},{1,7},{2,0},{3,1},{4,2},{5,3},{6,4},{7,5},{8,14},{9,15},{10,... | collective-permute-start | bytes 786440 | tf_op jit(solution)/shard_map/ppermute | solution.py:335
  660.5 14.9 %copy-start.7 = (f32[8,8,32,256]{3,1,2,0:T(8,128)S(1)}, f32[8,8,32,256]{3,1,2,0:T(8,128)}, u32[]{:S(2)}) copy-start(f32[8,8,32,256]{3,1,2,0:T(8,128)} %copy.77) | copy-start | bytes 6291460
  660.6 14.9 %copy-start.22 = (bf16[64,8192]{1,0:T(8,128)(2,1)S(1)}, bf16[64,8192]{1,0:T(8,128)(2,1)}, u32[]{:S(2)}) copy-start(bf16[64,8192]{1,0:T(8,128)(2,1)} %param.21) | copy-start | bytes 3145732
  674.3 16.2 %collective-permute-start.33 = (bf16[256,1024]{1,0:T(8,128)(2,1)}, bf16[256,1024]{1,0:T(8,128)(2,1)}, u32[]{:S(2)}, u32[]{:S(2)}) collective-permute-start(bf16[256,1024]{1,0:T(8,128)(2,1)} %get-tuple-element.200), channel_id=1, source_target_pairs={{0,8},{8,0},{16,24},{24,16},{1,9},{9,1},{17,25},{25,17},{2,10},{10... | collective-permute-start | bytes 1572872 | tf_op jit(solution)/shard_map/ppermute | solution.py:302
  678.7 26.4 %collective-permute-start.34 = (bf16[256,1024]{1,0:T(8,128)(2,1)}, bf16[256,1024]{1,0:T(8,128)(2,1)}, u32[]{:S(2)}, u32[]{:S(2)}) collective-permute-start(bf16[256,1024]{1,0:T(8,128)(2,1)} %get-tuple-element.201), channel_id=1, source_target_pairs={{0,16},{8,24},{16,0},{24,8},{1,17},{9,25},{17,1},{25,9},{2,18},{10... | collective-permute-start | bytes 1572872 | tf_op jit(solution)/shard_map/ppermute | solution.py:302
  679.9 25.2 %collective-permute-start.35 = (bf16[256,1024]{1,0:T(8,128)(2,1)}, bf16[256,1024]{1,0:T(8,128)(2,1)}, u32[]{:S(2)}, u32[]{:S(2)}) collective-permute-start(bf16[256,1024]{1,0:T(8,128)(2,1)} %get-tuple-element.202), channel_id=1, source_target_pairs={{0,24},{8,16},{16,8},{24,0},{1,25},{9,17},{17,9},{25,1},{2,26},{10... | collective-permute-start | bytes 1572872 | tf_op jit(solution)/shard_map/ppermute | solution.py:302
  681.1 30.9 %collective-permute-start.36 = (bf16[256,1024]{1,0:T(8,128)(2,1)}, bf16[256,1024]{1,0:T(8,128)(2,1)}, u32[]{:S(2)}, u32[]{:S(2)}) collective-permute-start(bf16[256,1024]{1,0:T(8,128)(2,1)} %get-tuple-element.204), channel_id=1, source_target_pairs={{0,8},{8,0},{16,24},{24,16},{1,9},{9,1},{17,25},{25,17},{2,10},{10... | collective-permute-start | bytes 1572872 | tf_op jit(solution)/shard_map/ppermute | solution.py:302
  682.2 41.9 %collective-permute-start.37 = (bf16[256,1024]{1,0:T(8,128)(2,1)}, bf16[256,1024]{1,0:T(8,128)(2,1)}, u32[]{:S(2)}, u32[]{:S(2)}) collective-permute-start(bf16[256,1024]{1,0:T(8,128)(2,1)} %get-tuple-element.205), channel_id=1, source_target_pairs={{0,16},{8,24},{16,0},{24,8},{1,17},{9,25},{17,1},{25,9},{2,18},{10... | collective-permute-start | bytes 1572872 | tf_op jit(solution)/shard_map/ppermute | solution.py:302
  686.4 40.8 %all-to-all-start.6 = ((bf16[8,64,768]{2,1,0:T(8,128)(2,1)}), bf16[8,64,768]{2,1,0:T(8,128)(2,1)}, u32[]{:S(2)}, u32[]{:S(2)}) async-start(bf16[8,64,768]{2,1,0:T(8,128)(2,1)} %bitcast.276), calls=%async_computation.9 | async-start | bytes 1572864 | tf_op jit(solution)/shard_map/all_to_all | solution.py:365
  690.5 33.6 %copy-start.27 = (bf16[256,1024]{1,0:T(8,128)(2,1)S(1)}, bf16[256,1024]{1,0:T(8,128)(2,1)}, u32[]{:S(2)}) copy-start(bf16[256,1024]{1,0:T(8,128)(2,1)} %get-tuple-element.203) | copy-start | bytes 1572868
  690.5 33.6 %collective-permute-start.38 = (bf16[256,1024]{1,0:T(8,128)(2,1)}, bf16[256,1024]{1,0:T(8,128)(2,1)S(1)}, u32[]{:S(2)}, u32[]{:S(2)}) collective-permute-start(bf16[256,1024]{1,0:T(8,128)(2,1)} %get-tuple-element.206), channel_id=1, source_target_pairs={{0,24},{8,16},{16,8},{24,0},{1,25},{9,17},{17,9},{25,1},{2,26},{10... | collective-permute-start | bytes 1572872 | tf_op jit(solution)/shard_map/ppermute | solution.py:302
  (58 other events, 315.2 us)
Sparse Core Ops, SparseCore 0:
  9.7 99.7 all-gather.14
  120.0 55.9 all-gather.10
  177.9 56.2 all-gather.8
  241.6 64.3 all-gather.6
  308.0 38.1 all-gather.12
  348.3 66.7 reduce-scatter.3
  417.8 68.1 reduce-scatter.5
  616.9 104.7 reduce-scatter.7

commit v4 on v3

--- a/solution.py
+++ b/solution.py
@@ -1,6 +1,8 @@
 import jax
 import jax.numpy as jnp
 from jax import lax
+from jax.experimental import pallas as pl
+from jax.experimental.pallas import tpu as pltpu
 from jax.sharding import Mesh
 from jax.sharding import PartitionSpec as P
 
@@ -282,7 +284,6 @@
 
 BF16, F32 = jnp.bfloat16, jnp.float32
 CTX = ("half", "low", "core")
-TEAM = ("x", "low", "core")
 join = lax.optimization_barrier
 
 
@@ -335,8 +336,8 @@
     return lax.ppermute(values, CTX, pairs)
 
 
-def send_column(rows):
-    return [rows] + [turn_chips(rows, step) for step in range(1, 4)]
+def send_column(rows, steps=(1, 2, 3)):
+    return [turn_chips(rows, step) for step in steps]
 
 
 def order_column(blocks):
@@ -353,30 +354,10 @@
     return jnp.stack((low, high), axis=-3)
 
 
-def order_teams(near, far, near_y, far_y):
-    y, half = lax.axis_index("y"), lax.axis_index("half")
-    buffer = jnp.zeros((4,) + near.shape, near.dtype)
-    for block, bits in ((near, 0), (far, 1), (near_y, 2), (far_y, 3)):
-        buffer = put(buffer, block, (2 * y + half) ^ bits)
-    return buffer.reshape((2, 2) + near.shape)
-
-
 def swap(values, axes):
     return lax.all_to_all(values, axes, split_axis=0, concat_axis=0, tiled=True)
 
 
-def swap_steps(values):
-    chip, core = lax.axis_index(("half", "low")), lax.axis_index("core")
-    values = values.reshape((4, 2) + values.shape[1:])
-    got = [take(values, chip)]
-    got += [turn_chips(take(values, (chip + step) % 4), step) for step in range(1, 4)]
-    column = order_column(got)
-    mine = lax.dynamic_index_in_dim(column, core, 1, keepdims=False)
-    other = flip(lax.dynamic_index_in_dim(column, 1 - core, 1, keepdims=False), "core")
-    low, high = jnp.where(core == 0, mine, other), jnp.where(core == 0, other, mine)
-    return jnp.stack((low, high), axis=1).reshape((8,) + values.shape[2:])
-
-
 def gather(values, axes):
     return lax.all_gather(values, axes, axis=0, tiled=True)
 
@@ -385,20 +366,88 @@
     return lax.psum_scatter(values, axes, scatter_dimension=0, tiled=True).astype(F32)
 
 
-def other_y(parts):
-    return flip(take(parts, 1 - lax.axis_index("y")).astype(BF16), "y")
-
-
-def add_y(parts, got):
-    return take(parts, lax.axis_index("y")) + got.astype(F32)
-
-
-def other_half(parts):
-    return flip(take(parts, 1 - lax.axis_index("half")).astype(BF16), "half")
-
-
-def add_half(parts, got):
-    return take(parts, lax.axis_index("half")) + got.astype(F32)
+BLOCK = 512
+
+
+def attention_back_kernel(
+    prefix_ref,
+    query_ref,
+    key_ref,
+    value_ref,
+    grad_ref,
+    log_ref,
+    delta_ref,
+    cosine_ref,
+    sine_ref,
+    out_ref,
+    dq_ref,
+    dk_ref,
+    dv_ref,
+):
+    steps = query_ref.shape[0] // BLOCK
+    prefix = prefix_ref[0]
+    scale = HD ** (-0.5)
+    dq_ref[...] = jnp.zeros_like(dq_ref)
+    dk_ref[...] = jnp.zeros_like(dk_ref)
+    dv_ref[...] = jnp.zeros_like(dv_ref)
+    row = lax.broadcasted_iota(jnp.int32, (BLOCK, BLOCK), 0)
+    column = lax.broadcasted_iota(jnp.int32, (BLOCK, BLOCK), 1)
+
+    def query_step(i, carry):
+        here = pl.ds(pl.multiple_of(i * BLOCK, BLOCK), BLOCK)
+        query, grad = query_ref[here, :], grad_ref[here, :]
+        log_total, delta = log_ref[i], delta_ref[i]
+
+        def key_step(j, carry):
+            there = pl.ds(pl.multiple_of(j * BLOCK, BLOCK), BLOCK)
+            key, value = key_ref[there, :], value_ref[there, :]
+            key_pos, query_pos = j * BLOCK + row, i * BLOCK + column
+            seen = (key_pos <= query_pos) | (key_pos < prefix)
+            prob = jnp.exp(jnp.where(seen, mul_right(key, query) * scale, NEG) - log_total)
+            score = (prob * (mul_right(value, grad) - delta)).astype(jnp.bfloat16)
+            dv_ref[there, :] += mul_plain(prob.astype(jnp.bfloat16), grad)
+            dk_ref[there, :] += mul_plain(score, query)
+            dq_ref[here, :] += mul_left(score, key)
+            return carry
+
+        last = jnp.maximum(i + 1, (prefix + BLOCK - 1) // BLOCK)
+        return lax.fori_loop(0, jnp.minimum(last, steps), key_step, carry)
+
+    lax.fori_loop(0, steps, query_step, 0)
+
+    def turn_back(values):
+        half = HD // 2
+        rolled = jnp.concatenate((-values[:, half:], values[:, :half]), axis=1)
+        return values * cosine_ref[...] - rolled * sine_ref[...]
+
+    out_ref[:, :HD] = turn_back(dq_ref[...] * scale).astype(jnp.bfloat16)
+    out_ref[:, HD : 2 * HD] = turn_back(dk_ref[...] * scale).astype(jnp.bfloat16)
+    out_ref[:, 2 * HD :] = dv_ref[...].astype(jnp.bfloat16)
+
+
+def attention_back(prefix, query, key, value, grad, log_total, delta, cosine, sine):
+    span = query.shape[0]
+    whole = pl.BlockSpec(memory_space=pltpu.VMEM)
+    rows = (span // BLOCK, 1, BLOCK)
+    return pl.pallas_call(
+        attention_back_kernel,
+        out_shape=jax.ShapeDtypeStruct((span, 3 * HD), jnp.bfloat16),
+        in_specs=[pl.BlockSpec(memory_space=pltpu.SMEM)] + [whole] * 8,
+        out_specs=whole,
+        scratch_shapes=[pltpu.VMEM((span, HD), jnp.float32)] * 3,
+        compiler_params=pltpu.CompilerParams(vmem_limit_bytes=40 * 2**20),
+        cost_estimate=pl.CostEstimate(flops=10**6, bytes_accessed=10**4, transcendentals=0),
+    )(
+        prefix,
+        query,
+        key,
+        value,
+        grad,
+        log_total.reshape(rows),
+        delta.reshape(rows),
+        cosine,
+        sine,
+    )
 
 
 def head_split(
@@ -423,6 +472,7 @@
     slice_ff = 4 * share
     per_key = H // KVH
     scale = HD ** (-0.5)
+    cut = width // 2
 
     tok_in = tokens[0].astype(F32)
     gain_one, gain_two = g_attn.astype(F32)[:, None], g_mlp.astype(F32)[:, None]
@@ -449,14 +499,14 @@
     qkv_rows = swap(qkv_cols, CTX).reshape(groups * shard, 3 * HD)
     qkv_rows, out_own, gate_cols, up_cols = join((qkv_rows, w_output, gate_cols, up_cols))
     qkv_blocks = send_dp(qkv_rows)
-    out_blocks = send_column(out_own)
+    out_blocks = [out_own] + send_column(out_own, (1, 2))
+    out_blocks += send_column(after(out_own, *qkv_blocks), (3,))
     qkv_w = order_dp(qkv_blocks).reshape(width, 3 * HD)
     out_rows = order_column(out_blocks)
     down_w = order_dp(down_blocks).reshape(slice_ff, width)
     tok_all, qkv_w, down_w, gate_cols, cosine, sine = join(
         (tok_all, qkv_w, down_w, gate_cols, cosine, sine)
     )
-    cut = width // 2
     dy_left = gather(after(cotangent[0][:, :cut], tok_all), CTX)
     out_mine = order_dp(send_dp(after(out_rows, qkv_w)))
     gate_rows = swap(gate_cols, CTX).reshape(groups * shard, slice_ff)
@@ -474,9 +524,11 @@
     pos = lax.iota(jnp.int32, span)
     seen = (pos[None, :] <= pos[:, None]) | (pos[None, :] < prefix[0])
     scores = jnp.where(seen, scores, NEG)
-    prob = jax.nn.softmax(scores, axis=-1)
-    prob_low = prob.astype(BF16)
-    head_o = mul_plain(prob_low, value).astype(BF16)
+    row_max = jnp.max(scores, axis=-1, keepdims=True)
+    log_total = row_max + jnp.log(jnp.sum(jnp.exp(scores - row_max), axis=-1, keepdims=True))
+    prob_low = jnp.exp(scores - log_total).astype(BF16)
+    head_wide = mul_plain(prob_low, value)
+    head_o = head_wide.astype(BF16)
     head_o, up_rows = join((head_o, up_rows))
     attn_o = swap(head_o.reshape(groups, tok_rows, HD), CTX)
     output_w = order_cores(out_mine, flip(out_mine, "core")).reshape(H * HD, width)
@@ -545,13 +597,10 @@
     gate_up_sum = gate_up_sum.reshape(2, groups, shard, slice_ff)
     gate_up_sum = lax.all_to_all(gate_up_sum, CTX, split_axis=1, concat_axis=1, tiled=True)
     d_head = d_head.reshape(span, HD)
-    d_prob = mul_right(d_head, value)
-    row_delta = jnp.sum(prob * d_prob, axis=-1, keepdims=True)
-    d_score = (prob * (d_prob - row_delta)).astype(BF16)
-    d_query = turn(mul_plain(d_score, key) * scale, -sine)
-    d_key = turn(mul_left(d_score, query) * scale, -sine)
-    d_value = mul_left(prob_low, d_head)
-    d_qkv = jnp.concatenate((d_query, d_key, d_value), axis=1).astype(BF16)
+    row_delta = jnp.sum(d_head.astype(F32) * head_wide, axis=-1)
+    d_qkv = attention_back(
+        prefix, query, key, value, d_head, log_total, row_delta, cosine, sine
+    )
     d_qkv, gate_up_sum, output_parts = join((d_qkv, gate_up_sum, output_parts))
     gate_sum, up_sum = gate_up_sum[0], gate_up_sum[1]
     dn_part_one = mul_right(d_qkv, qkv_w).astype(BF16)

time: 753 us -> 742 us (0.985)
  matrix products: 167 us -> 152 us
  waiting for transfers between devices: 279 us -> 265 us
  local copies, waits for them, and re-layouts: 105 us -> 114 us
  Pallas kernels: 0 us -> 8.12 us
    ppermute x33, waiting for transfers between devices: 139 us -> 130 us  [flip(): lax.ppermute(values, axis, [(i, i ^ bits) for i in range(lax.axis_size(ax...]
    pallas_call x0 -> x1, Pallas kernels: none -> 8.12 us  [attention_back(): pl.pallas_call(attention_back_kernel, out_shape=jax.ShapeDtypeStruct((spa...]
    dot_general x8 -> x6, matrix products: 45.5 us -> 38.9 us  [mul_left(): lax.dot_general(first_op, second_op, (((0,), (0,)), ((), ())), preferred_...]
    dot_general x8 -> x7, matrix products: 68.6 us -> 63.9 us  [mul_right(): lax.dot_general(first_op, second_op, (((1,), (1,)), ((), ())), preferred_...]
    dot_general x7 -> x6, matrix products: 52.9 us -> 48.8 us  [mul_plain(): return jnp.dot(first_op, second_op, preferred_element_type=jnp.float32)]
    unnamed x142 -> x112, local copies, waits for them, and re-layouts: 23 us -> 21.9 us
  transfers between devices with their start and end apart: 54 -> 54, of which waited for: 24 -> 23; matrix products, arithmetic and copies ran while one was open for 42% -> 41% of each run, Pallas kernels for 0% -> 1%
where the time goes in v4:
time: 742 us; the launch traced here: 730 us
  waiting for transfers between devices  265 us (36%)
  matrix products  152 us (20%)
  local copies, waits for them, and re-layouts  114 us (15%)
  starting transfers between devices  96.5 us (13%)
  other arithmetic  78.8 us (11%)
  between operations  15.9 us (2%)
  Pallas kernels  8.12 us (1%)
    ppermute x33, waiting for transfers between devices, flip(): lax.ppermute(values, axis, [(i, i ^ bits) for i in range(lax.axis_size(ax...  130 us
    dot_general x7, matrix products, mul_right(): lax.dot_general(first_op, second_op, (((1,), (1,)), ((), ())), preferred_...  63.9 us
    dot_general x6, matrix products, mul_plain(): return jnp.dot(first_op, second_op, preferred_element_type=jnp.float32)  48.8 us
    ppermute x6, waiting for transfers between devices, turn_chips(): return lax.ppermute(values, CTX, pairs)  42.1 us
    reduce_scatter x3, waiting for transfers between devices, scatter(): lax.psum_scatter(values, axes, scatter_dimension=0, tiled=True).astype(F32)  41.9 us
    dot_general x6, matrix products, mul_left(): lax.dot_general(first_op, second_op, (((0,), (0,)), ((), ())), preferred_...  38.9 us
    all_to_all x6, starting transfers between devices, swap(): return lax.all_to_all(values, axes, split_axis=0, concat_axis=0, tiled=True)  38.8 us
    ppermute x33, starting transfers between devices, flip(): lax.ppermute(values, axis, [(i, i ^ bits) for i in range(lax.axis_size(ax...  38.3 us
  transfers between devices with their start and end apart: 54, of which 23 were waited for; matrix products, arithmetic and copies ran while one was open for 41% of the time, Pallas kernels for 1%

profile of v4, /device:TPU:8, one launch (start us, length us, event | category | flops | bytes accessed | tf_op | source)
XLA Modules:
  0.0 730.0 jit_solution(15935041423648110307)
XLA Ops:
  17.9 5.3 all-to-all-start
  23.3 2.8 multiply_sine_fusion
  45.5 12.6 %collective-permute-done.4 = bf16[256,2048]{1,0:T(8,128)(2,1)} collective-permute-done((bf16[256,2048]{1,0:T(8,128)(2,1)}, bf16[256,2048]{1,0:T(8,128)(2,1)}, u32[]{:S(2)}, u32[]{:S(2)}) %collective-permute-start.4) | collective-permute-done | bytes 1048608 | tf_op jit(solution)/shard_map/ppermute | solution.py:303
  76.6 25.6 %collective-permute-done.6 = bf16[64,2048]{1,0:T(8,128)(2,1)S(1)} collective-permute-done((bf16[64,2048]{1,0:T(8,128)(2,1)S(1)}, bf16[64,2048]{1,0:T(8,128)(2,1)S(1)}, u32[]{:S(2)}, u32[]{:S(2)}) %collective-permute-start.6) | collective-permute-done | bytes 262176 | tf_op jit(solution)/shard_map/ppermute | solution.py:336
  107.8 4.9 collective-permute-done.8
  116.9 4.1 fusion
  121.0 6.5 fusion.1
  127.5 5.5 all-to-all-start.1
  133.0 8.1 %fusion.47 = f32[1536,768]{1,0:T(8,128)S(1)} fusion(bf16[1536,2048]{1,0:T(8,128)(2,1)} %fusion.1, bf16[2048,768]{1,0:T(8,128)(2,1)} %bitcast.11), kind=kOutput, calls=%fused_computation.187 | convolution fusion | flops 4831838208 | bytes 14155776 | tf_op jit(solution)/shard_map/dot_general | solution.py:22
  149.2 12.4 %collective-permute-done.9 = bf16[4,64,2048]{2,1,0:T(8,128)(2,1)} collective-permute-done((bf16[4,64,2048]{2,1,0:T(8,128)(2,1)}, bf16[4,64,2048]{2,1,0:T(8,128)(2,1)}, u32[]{:S(2)}, u32[]{:S(2)}) %collective-permute-start.9) | collective-permute-done | bytes 1048608 | tf_op jit(solution)/shard_map/ppermute | solution.py:303
  168.6 9.1 %all-to-all-done.1 = bf16[8,64,1024]{2,1,0:T(8,128)(2,1)} async-done(((bf16[8,64,1024]{2,1,0:T(8,128)(2,1)}), bf16[8,64,1024]{2,1,0:T(8,128)(2,1)}, u32[]{:S(2)}, u32[]{:S(2)}) %all-to-all-start.1) | async-done | bytes 1048608 | tf_op jit(solution)/shard_map/all_to_all | solution.py:358
  178.3 8.1 %all-to-all-start.2 = ((bf16[8,64,1024]{2,1,0:T(8,128)(2,1)}), bf16[8,64,1024]{2,1,0:T(8,128)(2,1)}, u32[]{:S(2)}, u32[]{:S(2)}) async-start(bf16[8,64,1024]{2,1,0:T(8,128)(2,1)} %reshape.248), calls=%async_computation.2 | async-start | bytes 2097152 | tf_op jit(solution)/shard_map/all_to_all | solution.py:358
  186.4 4.6 fusion.45
  193.0 2.9 fusion.46
  195.9 13.6 %all-to-all-done.2 = bf16[8,64,1024]{2,1,0:T(8,128)(2,1)} async-done(((bf16[8,64,1024]{2,1,0:T(8,128)(2,1)}), bf16[8,64,1024]{2,1,0:T(8,128)(2,1)}, u32[]{:S(2)}, u32[]{:S(2)}) %all-to-all-start.2) | async-done | bytes 1048608 | tf_op jit(solution)/shard_map/all_to_all | solution.py:358
  211.8 7.7 %all-to-all-start.3 = ((bf16[8,192,256]{2,1,0:T(8,128)(2,1)}), bf16[8,192,256]{2,1,0:T(8,128)(2,1)}, u32[]{:S(2)}, u32[]{:S(2)}) async-start(bf16[8,192,256]{2,1,0:T(8,128)(2,1)} %bitcast.261), calls=%async_computation.3 | async-start | bytes 1572864 | tf_op jit(solution)/shard_map/all_to_all | solution.py:358
  219.7 5.9 select_bitcast_fusion.1
  225.6 7.5 %pad_maximum_fusion = bf16[4,4,2,64,2048]{4,3,2,1,0:T(8,128)(2,1)} fusion(bf16[4,4,1,64,2048]{4,3,2,1,0:T(8,128)(2,1)} %get-tuple-element.214, bf16[4,4,1,64,2048]{4,3,2,1,0:T(8,128)(2,1)} %get-tuple-element.213), kind=kLoop, calls=%fused_computation.11 | loop fusion | flops 4194304 | bytes 16777216 | tf_op jit(solution)/shard_map/stack | solution.py:354
  233.0 4.0 all-to-all-done.3
  238.2 5.8 multiply_reduce_fusion.2
  254.6 17.9 %collective-permute-done.13 = bf16[512,1024]{1,0:T(8,128)(2,1)S(1)} collective-permute-done((bf16[512,1024]{1,0:T(8,128)(2,1)}, bf16[512,1024]{1,0:T(8,128)(2,1)S(1)}, u32[]{:S(2)}, u32[]{:S(2)}) %collective-permute-start.13) | collective-permute-done | bytes 1048608 | tf_op jit(solution)/shard_map/ppermute | solution.py:303
  273.6 21.8 %collective-permute-done.14 = bf16[512,1024]{1,0:T(8,128)(2,1)S(1)} collective-permute-done((bf16[512,1024]{1,0:T(8,128)(2,1)}, bf16[512,1024]{1,0:T(8,128)(2,1)S(1)}, u32[]{:S(2)}, u32[]{:S(2)}) %collective-permute-start.14) | collective-permute-done | bytes 1048608 | tf_op jit(solution)/shard_map/ppermute | solution.py:303
  297.5 13.3 %all-gather.7.cloned.1.call-done = bf16[1536,2048]{1,0:T(8,128)(2,1)} async-done(((bf16[192,2048]{1,0:T(8,128)(2,1)}), bf16[1536,2048]{1,0:T(8,128)(2,1)}) %all-gather.7.cloned.1.call-update) | async-done | bytes 6291472 | tf_op jit(solution)/shard_map/all_gather | solution.py:362
  310.9 10.1 %fusion.48 = f32[1536,1024]{1,0:T(8,128)S(1)} fusion(bf16[1536,2048]{1,0:T(8,128)(2,1)} %all-gather.7.cloned.1.call-done, bf16[2048,1024]{1,0:T(8,128)(2,1)} %all-gather.9.cloned.1.call-done), kind=kOutput, calls=%fused_computation.188 | convolution fusion | flops 6442450944 | bytes 16777216 | tf_op jit(solution)/shard_map/dot_general | solution.py:22
  321.1 13.1 %multiply_convert_fusion.2 = (bf16[1536,1024]{1,0:T(8,128)(2,1)S(1)}, f32[1536,1024]{1,0:T(8,128)}) fusion(f32[1536,1024]{1,0:T(8,128)S(1)} %fusion.48, bf16[1536,2048]{1,0:T(8,128)(2,1)S(1)} %copy-done.41, bf16[2048,1024]{1,0:T(8,128)(2,1)} %bitcast.38), kind=kOutput, calls=%fused_computation.17 | convolution fusion | flops 6451888128 | bytes 26214400 | tf_op jit(solution)/shard_map/dot_general | solution.py:22
  335.8 8.7 %convolution_convert_fusion.1 = bf16[1536,2048]{1,0:T(8,128)(2,1)} fusion(bf16[1536,1024]{1,0:T(8,128)(2,1)S(1)} %get-tuple-element.158, bf16[1024,2048]{1,0:T(8,128)(2,1)S(1)} %bitcast.253), kind=kOutput, calls=%fused_computation.13 | convolution fusion | flops 6445596672 | bytes 13631488 | tf_op jit(solution)/shard_map/dot_general | solution.py:22
  344.5 6.6 all-gather.13.cloned.1.call-done
  351.2 8.8 %fusion.11 = f32[1536,1024]{1,0:T(8,128)} fusion(bf16[1536,1024]{1,0:T(8,128)(2,1)} %all-gather.11.cloned.1.call-done, bf16[1024,2048]{1,0:T(8,128)(2,1)} %bitcast.252), kind=kOutput, calls=%fused_computation.45 | convolution fusion | flops 3221225472 | bytes 11534336 | tf_op jit(solution)/shard_map/dot_general | solution.py:26
  360.0 12.2 %multiply_convert_fusion = (bf16[1536,1024]{1,0:T(8,128)(2,1)}, bf16[1536,1024]{1,0:T(8,128)(2,1)}) fusion(f32[1536,1024]{1,0:T(8,128)} %copy-done.48, f32[1536,1024]{1,0:T(8,128)} %get-tuple-element.139, f32[1536,1024]{1,0:T(8,128)} %fusion.11, bf16[1536,1024]{1,0:T(8,128)(2,1)S(1)} %copy-done.44, bf16[1024,2048]{1,0:T(8,128)(2,1)S(1)} %bitcast.254), kind=kOutput, calls=%fused_computation.14 | convolution fusion | flops 3243245568 | bytes 30408704 | tf_op jit(solution)/shard_map/dot_general | solution.py:26
  372.3 8.8 %convolution_convert_fusion.2 = bf16[2048,1024]{1,0:T(8,128)(2,1)S(1)} fusion(bf16[1536,2048]{1,0:T(8,128)(2,1)S(1)} %bitcast.279, bf16[1536,1024]{1,0:T(8,128)(2,1)} %get-tuple-element.143), kind=kOutput, calls=%fused_computation.23 | convolution fusion | flops 6444548096 | bytes 13631488 | tf_op jit(solution)/shard_map/dot_general | solution.py:32
  381.1 7.3 convolution_convert_fusion.3
  388.4 4.2 dynamic-slice_bitcast_fusion.4
  395.6 9.4 %fusion.49 = f32[1536,2048]{1,0:T(8,128)} fusion(bf16[1536,1024]{1,0:T(8,128)(2,1)S(1)} %copy-done.50, bf16[2048,1024]{1,0:T(8,128)(2,1)S(1)} %copy-done.42), kind=kOutput, calls=%fused_computation.189 | convolution fusion | flops 6442450944 | bytes 19922944 | tf_op jit(solution)/shard_map/dot_general | solution.py:26
  405.0 13.2 %add_convert_fusion = bf16[1536,2048]{1,0:T(8,128)(2,1)} fusion(f32[1536,2048]{1,0:T(8,128)} %fusion.49, bf16[1536,1024]{1,0:T(8,128)(2,1)} %get-tuple-element.143, bf16[2048,1024]{1,0:T(8,128)(2,1)} %bitcast.38), kind=kOutput, calls=%fused_computation.4 | convolution fusion | flops 6448742400 | bytes 26214400 | tf_op jit(solution)/shard_map/dot_general | solution.py:26
  436.5 6.5 convolution_convert_fusion.7
  445.8 3.9 convolution_convert_fusion.8
  451.0 39.9 %reduce-scatter.6.cloned.1.call-done = bf16[192,2048]{1,0:T(8,128)(2,1)} async-done(((bf16[1536,2048]{1,0:T(8,128)(2,1)}), bf16[192,2048]{1,0:T(8,128)(2,1)}) %reduce-scatter.6.cloned.1.call-update) | async-done | bytes 786448 | tf_op jit(solution)/shard_map/reduce_scatter | solution.py:366
  492.4 9.9 %collective-permute-done.21 = bf16[512,1024]{1,0:T(8,128)(2,1)} collective-permute-done((bf16[512,1024]{1,0:T(8,128)(2,1)}, bf16[512,1024]{1,0:T(8,128)(2,1)}, u32[]{:S(2)}, u32[]{:S(2)}) %collective-permute-start.21) | collective-permute-done | bytes 1048608 | tf_op jit(solution)/shard_map/ppermute | solution.py:303
  503.9 6.5 convolution_convert_fusion.6
  511.5 6.5 all-to-all-start.4
  518.0 3.2 fusion.26
  525.4 3.8 convolution_convert_fusion.4
  531.4 4.0 all-to-all-done.4
  535.5 3.1 copy.107
  538.6 8.0 %all-to-all-start.5 = ((bf16[2,8,64,1024]{3,2,0,1:T(8,128)(2,1)}), bf16[2,8,64,1024]{3,2,0,1:T(8,128)(2,1)}, u32[]{:S(2)}, u32[]{:S(2)}) async-start(bf16[2,8,64,1024]{3,2,0,1:T(8,128)(2,1)} %copy.107), calls=%async_computation.7 | async-start | bytes 4194304 | tf_op jit(solution)/shard_map/all_to_all | solution.py:598
  550.1 3.0 copy.106
  558.4 8.1 %shard_map.203 = bf16[1536,768]{1,0:T(8,128)(2,1)S(1)} custom-call(s32[1]{0:T(128)} %copy.150.prefix_ref, bf16[1536,256]{1,0:T(8,128)(2,1)S(1)} %copy-done.3, bf16[1536,256]{1,0:T(8,128)(2,1)S(1)} %copy-done.2, bf16[1536,256]{1,0:T(8,128)(2,1)S(1)} %copy-done.1, bf16[1536,256]{1,0:T(8,128)(2,1)} %bitcast.71.grad_ref, f32[3,1,512]{2,1,0:T(1,128)S(1)} %add.324.log_ref, ...), custom_call_target="tpu_custom_call" | custom-call | flops 1000000 | bytes 10000 | tf_op jit(solution)/shard_map/pallas_call | solution.py:432
  568.0 4.9 collective-permute-done.24
  572.9 22.9 %collective-permute-done.25 = bf16[4,64,2048]{2,1,0:T(8,128)(2,1)} collective-permute-done((bf16[4,64,2048]{2,1,0:T(8,128)(2,1)}, bf16[4,64,2048]{2,1,0:T(8,128)(2,1)}, u32[]{:S(2)}, u32[]{:S(2)}) %collective-permute-start.25) | collective-permute-done | bytes 1048608 | tf_op jit(solution)/shard_map/ppermute | solution.py:303
  595.8 9.2 %convolution_convert_fusion = bf16[1536,2048]{1,0:T(8,128)(2,1)} fusion(bf16[1536,768]{1,0:T(8,128)(2,1)} %copy-done.4, bf16[2048,768]{1,0:T(8,128)(2,1)} %bitcast.11), kind=kOutput, calls=%fused_computation.12 | convolution fusion | flops 4834983936 | bytes 11796480 | tf_op jit(solution)/shard_map/dot_general | solution.py:26
  606.4 3.0 convert_add_fusion
  612.0 8.6 %convolution_convert_fusion.5 = bf16[2048,768]{1,0:T(8,128)(2,1)S(1)} fusion(bf16[1536,2048]{1,0:T(8,128)(2,1)} %fusion.1, bf16[1536,768]{1,0:T(8,128)(2,1)S(1)} %copy-done.5), kind=kOutput, calls=%fused_computation.26 | convolution fusion | flops 4833411072 | bytes 11796480 | tf_op jit(solution)/shard_map/dot_general | solution.py:32
  630.8 3.3 slice_convert_fusion.1
  634.2 3.3 reshape.289
  637.5 2.8 copy.112
  644.8 2.8 copy.111
  650.0 11.6 %collective-permute-done.30 = bf16[64,2048]{1,0:T(8,128)(2,1)} collective-permute-done((bf16[64,2048]{1,0:T(8,128)(2,1)}, bf16[64,2048]{1,0:T(8,128)(2,1)}, u32[]{:S(2)}, u32[]{:S(2)}) %collective-permute-start.30) | collective-permute-done | bytes 262176 | tf_op jit(solution)/shard_map/ppermute | solution.py:336
  663.1 3.3 broadcast_multiply_fusion
  668.5 2.9 add_convert_fusion.3
  671.3 5.7 all-to-all-start.6
  682.5 10.2 %collective-permute-done.34 = bf16[256,1024]{1,0:T(8,128)(2,1)} collective-permute-done((bf16[256,1024]{1,0:T(8,128)(2,1)}, bf16[256,1024]{1,0:T(8,128)(2,1)}, u32[]{:S(2)}, u32[]{:S(2)}) %collective-permute-start.34) | collective-permute-done | bytes 524320 | tf_op jit(solution)/shard_map/ppermute | solution.py:303
  694.5 4.8 collective-permute-done.36
  699.3 12.6 %collective-permute-done.37 = bf16[256,1024]{1,0:T(8,128)(2,1)S(1)} collective-permute-done((bf16[256,1024]{1,0:T(8,128)(2,1)}, bf16[256,1024]{1,0:T(8,128)(2,1)S(1)}, u32[]{:S(2)}, u32[]{:S(2)}) %collective-permute-start.37) | collective-permute-done | bytes 524320 | tf_op jit(solution)/shard_map/ppermute | solution.py:303
  719.0 3.9 fusion.29
  (297 shorter events, 179.6 us)
Async XLA Ops:
  7.2 106.2 %all-gather.15.cloned.1.call-start = ((), (), s32[]{:S(2)}) async-start(), calls=%async_computation.17 | async-start | bytes 7077888 | tf_op jit(solution)/shard_map/all_gather | solution.py:362
  7.9 35.3 %collective-permute-start.3 = (bf16[256,2048]{1,0:T(8,128)(2,1)}, bf16[256,2048]{1,0:T(8,128)(2,1)}, u32[]{:S(2)}, u32[]{:S(2)}) collective-permute-start(bf16[256,2048]{1,0:T(8,128)(2,1)} %param.22), channel_id=1, source_target_pairs={{0,8},{8,0},{16,24},{24,16},{1,9},{9,1},{17,25},{25,17},{2,10},{10... | collective-permute-start | bytes 3145736 | tf_op jit(solution)/shard_map/ppermute | solution.py:303
  9.5 50.9 %collective-permute-start.5 = (bf16[256,2048]{1,0:T(8,128)(2,1)}, bf16[256,2048]{1,0:T(8,128)(2,1)}, u32[]{:S(2)}, u32[]{:S(2)}) collective-permute-start(bf16[256,2048]{1,0:T(8,128)(2,1)} %param.22), channel_id=1, source_target_pairs={{0,24},{8,16},{16,8},{24,0},{1,25},{9,17},{17,9},{25,1},{2,26},{10... | collective-permute-start | bytes 3145736 | tf_op jit(solution)/shard_map/ppermute | solution.py:303
  11.0 47.1 %collective-permute-start.4 = (bf16[256,2048]{1,0:T(8,128)(2,1)}, bf16[256,2048]{1,0:T(8,128)(2,1)}, u32[]{:S(2)}, u32[]{:S(2)}) collective-permute-start(bf16[256,2048]{1,0:T(8,128)(2,1)} %param.22), channel_id=1, source_target_pairs={{0,16},{8,24},{16,0},{24,8},{1,17},{9,25},{17,1},{25,9},{2,18},{10... | collective-permute-start | bytes 3145736 | tf_op jit(solution)/shard_map/ppermute | solution.py:303
  17.9 44.8 %all-to-all-start = ((bf16[8,64,768]{2,1,0:T(8,128)(2,1)}), bf16[8,64,768]{2,1,0:T(8,128)(2,1)}, u32[]{:S(2)}, u32[]{:S(2)}) async-start(bf16[8,64,768]{2,1,0:T(8,128)(2,1)} %copy.90), calls=%async_computation | async-start | bytes 1572864 | tf_op jit(solution)/shard_map/all_to_all | solution.py:358
  23.3 274.3 %all-gather.11.cloned.1.call-start = ((), (), s32[]{:S(2)}) async-start(), calls=%async_computation.12 | async-start | bytes 3538944 | tf_op jit(solution)/shard_map/all_gather | solution.py:362
  43.2 19.6 %copy-start.34 = (bf16[64,2048]{1,0:T(8,128)(2,1)S(1)}, bf16[64,2048]{1,0:T(8,128)(2,1)}, u32[]{:S(2)}) copy-start(bf16[64,2048]{1,0:T(8,128)(2,1)} %param.18) | copy-start | bytes 786436
  62.7 40.2 %collective-permute-start.7 = (bf16[64,2048]{1,0:T(8,128)(2,1)S(1)}, bf16[64,2048]{1,0:T(8,128)(2,1)S(1)}, u32[]{:S(2)}, u32[]{:S(2)}) collective-permute-start(bf16[64,2048]{1,0:T(8,128)(2,1)S(1)} %copy-done.34), channel_id=1, source_target_pairs={{0,4},{1,5},{2,6},{3,7},{4,0},{5,1},{6,2},{7,3},{8,12},{9,13},{10,... | collective-permute-start | bytes 786440 | tf_op jit(solution)/shard_map/ppermute | solution.py:336
  65.3 36.9 %collective-permute-start.6 = (bf16[64,2048]{1,0:T(8,128)(2,1)S(1)}, bf16[64,2048]{1,0:T(8,128)(2,1)S(1)}, u32[]{:S(2)}, u32[]{:S(2)}) collective-permute-start(bf16[64,2048]{1,0:T(8,128)(2,1)S(1)} %copy-done.34), channel_id=1, source_target_pairs={{0,2},{1,3},{2,4},{3,5},{4,6},{5,7},{6,0},{7,1},{8,10},{9,11},{10,... | collective-permute-start | bytes 786440 | tf_op jit(solution)/shard_map/ppermute | solution.py:336
  67.3 36.3 %collective-permute-start.2 = (bf16[512,768]{1,0:T(8,128)(2,1)}, bf16[512,768]{1,0:T(8,128)(2,1)S(1)}, u32[]{:S(2)}, u32[]{:S(2)}) collective-permute-start(bf16[512,768]{1,0:T(8,128)(2,1)} %bitcast.4), channel_id=1, source_target_pairs={{0,24},{8,16},{16,8},{24,0},{1,25},{9,17},{17,9},{25,1},{2,26},{10... | collective-permute-start | bytes 2359304 | tf_op jit(solution)/shard_map/ppermute | solution.py:303
  69.8 33.9 %collective-permute-start.1 = (bf16[512,768]{1,0:T(8,128)(2,1)}, bf16[512,768]{1,0:T(8,128)(2,1)S(1)}, u32[]{:S(2)}, u32[]{:S(2)}) collective-permute-start(bf16[512,768]{1,0:T(8,128)(2,1)} %bitcast.4), channel_id=1, source_target_pairs={{0,16},{8,24},{16,0},{24,8},{1,17},{9,25},{17,1},{25,9},{2,18},{10... | collective-permute-start | bytes 2359304 | tf_op jit(solution)/shard_map/ppermute | solution.py:303
  70.3 33.5 %collective-permute-start = (bf16[512,768]{1,0:T(8,128)(2,1)}, bf16[512,768]{1,0:T(8,128)(2,1)S(1)}, u32[]{:S(2)}, u32[]{:S(2)}) collective-permute-start(bf16[512,768]{1,0:T(8,128)(2,1)} %bitcast.4), channel_id=1, source_target_pairs={{0,8},{8,0},{16,24},{24,16},{1,9},{9,1},{17,25},{25,17},{2,10},{10... | collective-permute-start | bytes 2359304 | tf_op jit(solution)/shard_map/ppermute | solution.py:303
  103.8 8.9 %collective-permute-start.8 = (bf16[64,2048]{1,0:T(8,128)(2,1)S(1)}, bf16[64,2048]{1,0:T(8,128)(2,1)S(1)}, u32[]{:S(2)}, u32[]{:S(2)}) collective-permute-start(bf16[64,2048]{1,0:T(8,128)(2,1)S(1)} %copy-done.34), channel_id=1, source_target_pairs={{0,6},{1,7},{2,0},{3,1},{4,2},{5,3},{6,4},{7,5},{8,14},{9,15},{10,... | collective-permute-start | bytes 786440 | tf_op jit(solution)/shard_map/ppermute | solution.py:336
  113.4 52.9 %collective-permute-start.11 = (bf16[4,64,2048]{2,1,0:T(8,128)(2,1)}, bf16[4,64,2048]{2,1,0:T(8,128)(2,1)}, u32[]{:S(2)}, u32[]{:S(2)}) collective-permute-start(bf16[4,64,2048]{2,1,0:T(8,128)(2,1)} %bitcast_dynamic-update-slice_fusion.16), channel_id=1, source_target_pairs={{0,24},{8,16},{16,8},{24,0},{1,25},{9,17},{17,9},{25,1},{2,26},{10... | collective-permute-start | bytes 3145736 | tf_op jit(solution)/shard_map/ppermute | solution.py:303
  116.0 47.9 %collective-permute-start.10 = (bf16[4,64,2048]{2,1,0:T(8,128)(2,1)}, bf16[4,64,2048]{2,1,0:T(8,128)(2,1)}, u32[]{:S(2)}, u32[]{:S(2)}) collective-permute-start(bf16[4,64,2048]{2,1,0:T(8,128)(2,1)} %bitcast_dynamic-update-slice_fusion.16), channel_id=1, source_target_pairs={{0,16},{8,24},{16,0},{24,8},{1,17},{9,25},{17,1},{25,9},{2,18},{10... | collective-permute-start | bytes 3145736 | tf_op jit(solution)/shard_map/ppermute | solution.py:303
  116.5 45.0 %collective-permute-start.9 = (bf16[4,64,2048]{2,1,0:T(8,128)(2,1)}, bf16[4,64,2048]{2,1,0:T(8,128)(2,1)}, u32[]{:S(2)}, u32[]{:S(2)}) collective-permute-start(bf16[4,64,2048]{2,1,0:T(8,128)(2,1)} %bitcast_dynamic-update-slice_fusion.16), channel_id=1, source_target_pairs={{0,8},{8,0},{16,24},{24,16},{1,9},{9,1},{17,25},{25,17},{2,10},{10... | collective-permute-start | bytes 3145736 | tf_op jit(solution)/shard_map/ppermute | solution.py:303
  127.5 50.1 %all-to-all-start.1 = ((bf16[8,64,1024]{2,1,0:T(8,128)(2,1)}), bf16[8,64,1024]{2,1,0:T(8,128)(2,1)}, u32[]{:S(2)}, u32[]{:S(2)}) async-start(bf16[8,64,1024]{2,1,0:T(8,128)(2,1)} %reshape.246), calls=%async_computation.1 | async-start | bytes 2097152 | tf_op jit(solution)/shard_map/all_to_all | solution.py:358
  133.0 164.5 %all-gather.9.cloned.1.call-start = ((), (), s32[]{:S(2)}) async-start(), calls=%async_computation.11 | async-start | bytes 5242880 | tf_op jit(solution)/shard_map/all_gather | solution.py:362
  177.6 42.1 %collective-permute-start.12 = (bf16[4,4,64,2048]{3,2,1,0:T(8,128)(2,1)}, bf16[4,4,64,2048]{3,2,1,0:T(8,128)(2,1)}, u32[]{:S(2)}, u32[]{:S(2)}) collective-permute-start(bf16[4,4,64,2048]{3,2,1,0:T(8,128)(2,1)} %bitcast_dynamic-update-slice_fusion.4), channel_id=1, source_target_pairs={{0,1},{1,0},{2,3},{3,2},{4,5},{5,4},{6,7},{7,6},{8,9},{9,8},{10,11... | collective-permute-start | bytes 12582920 | tf_op jit(solution)/shard_map/ppermute | solution.py:303
  178.3 31.2 %all-to-all-start.2 = ((bf16[8,64,1024]{2,1,0:T(8,128)(2,1)}), bf16[8,64,1024]{2,1,0:T(8,128)(2,1)}, u32[]{:S(2)}, u32[]{:S(2)}) async-start(bf16[8,64,1024]{2,1,0:T(8,128)(2,1)} %reshape.248), calls=%async_computation.2 | async-start | bytes 2097152 | tf_op jit(solution)/shard_map/all_to_all | solution.py:358
  211.8 25.2 %all-to-all-start.3 = ((bf16[8,192,256]{2,1,0:T(8,128)(2,1)}), bf16[8,192,256]{2,1,0:T(8,128)(2,1)}, u32[]{:S(2)}, u32[]{:S(2)}) async-start(bf16[8,192,256]{2,1,0:T(8,128)(2,1)} %bitcast.261), calls=%async_computation.3 | async-start | bytes 1572864 | tf_op jit(solution)/shard_map/all_to_all | solution.py:358
  219.5 91.3 %all-gather.7.cloned.1.call-start = ((), (), s32[]{:S(2)}) async-start(), calls=%async_computation.10 | async-start | bytes 7077888 | tf_op jit(solution)/shard_map/all_gather | solution.py:362
  246.2 104.9 %all-gather.13.cloned.1.call-start = ((), (), s32[]{:S(2)}) async-start(), calls=%async_computation.13 | async-start | bytes 3538944 | tf_op jit(solution)/shard_map/all_gather | solution.py:362
  246.3 26.3 %collective-permute-start.13 = (bf16[512,1024]{1,0:T(8,128)(2,1)}, bf16[512,1024]{1,0:T(8,128)(2,1)S(1)}, u32[]{:S(2)}, u32[]{:S(2)}) collective-permute-start(bf16[512,1024]{1,0:T(8,128)(2,1)} %bitcast.26), channel_id=1, source_target_pairs={{0,8},{8,0},{16,24},{24,16},{1,9},{9,1},{17,25},{25,17},{2,10},{10... | collective-permute-start | bytes 3145736 | tf_op jit(solution)/shard_map/ppermute | solution.py:303
  247.8 47.5 %collective-permute-start.14 = (bf16[512,1024]{1,0:T(8,128)(2,1)}, bf16[512,1024]{1,0:T(8,128)(2,1)S(1)}, u32[]{:S(2)}, u32[]{:S(2)}) collective-permute-start(bf16[512,1024]{1,0:T(8,128)(2,1)} %bitcast.26), channel_id=1, source_target_pairs={{0,16},{8,24},{16,0},{24,8},{1,17},{9,25},{17,1},{25,9},{2,18},{10... | collective-permute-start | bytes 3145736 | tf_op jit(solution)/shard_map/ppermute | solution.py:303
  249.3 47.2 %collective-permute-start.15 = (bf16[512,1024]{1,0:T(8,128)(2,1)}, bf16[512,1024]{1,0:T(8,128)(2,1)S(1)}, u32[]{:S(2)}, u32[]{:S(2)}) collective-permute-start(bf16[512,1024]{1,0:T(8,128)(2,1)} %bitcast.26), channel_id=1, source_target_pairs={{0,24},{8,16},{16,8},{24,0},{1,25},{9,17},{17,9},{25,1},{2,26},{10... | collective-permute-start | bytes 3145736 | tf_op jit(solution)/shard_map/ppermute | solution.py:303
  310.8 109.2 %reduce-scatter.4.cloned.1.call-start = ((), (), s32[]{:S(2)}) async-start(), calls=%async_computation.14 | async-start | bytes 7077888 | tf_op jit(solution)/shard_map/reduce_scatter | solution.py:366
  321.1 13.1 %copy-start.48 = (f32[1536,1024]{1,0:T(8,128)}, f32[1536,1024]{1,0:T(8,128)S(1)}, u32[]{:S(2)}) copy-start(f32[1536,1024]{1,0:T(8,128)S(1)} %fusion.48) | copy-start | bytes 18874372
  321.1 14.8 %copy-start.18 = (bf16[4,256,2048]{2,1,0:T(8,128)(2,1)S(1)}, bf16[4,256,2048]{2,1,0:T(8,128)(2,1)}, u32[]{:S(2)}) copy-start(bf16[4,256,2048]{2,1,0:T(8,128)(2,1)} %bitcast_dynamic-update-slice_fusion.8) | copy-start | bytes 12582916
  351.1 139.8 %reduce-scatter.6.cloned.1.call-start = ((), (), s32[]{:S(2)}) async-start(), calls=%async_computation.15 | async-start | bytes 7077888 | tf_op jit(solution)/shard_map/reduce_scatter | solution.py:366
  351.2 21.1 %slice-start = ((s8[6291456]{0:T(1024)(128)(4,1)}), s8[4194304]{0:T(1024)(128)(4,1)S(1)}, s32[]{:S(2)}) async-start(s8[6291456]{0:T(1024)(128)(4,1)} %bitcast.278), calls=%async_computation.18 | async-start | bytes 8388608
  392.6 30.0 %collective-permute-start.16 = (bf16[512,1024]{1,0:T(8,128)(2,1)}, bf16[512,1024]{1,0:T(8,128)(2,1)}, u32[]{:S(2)}, u32[]{:S(2)}) collective-permute-start(bf16[512,1024]{1,0:T(8,128)(2,1)} %get-tuple-element.145), channel_id=1, source_target_pairs={{0,8},{8,0},{16,24},{24,16},{1,9},{9,1},{17,25},{25,17},{2,10},{10... | collective-permute-start | bytes 3145736 | tf_op jit(solution)/shard_map/ppermute | solution.py:303
  394.1 28.5 %collective-permute-start.17 = (bf16[512,1024]{1,0:T(8,128)(2,1)}, bf16[512,1024]{1,0:T(8,128)(2,1)}, u32[]{:S(2)}, u32[]{:S(2)}) collective-permute-start(bf16[512,1024]{1,0:T(8,128)(2,1)} %get-tuple-element.146), channel_id=1, source_target_pairs={{0,16},{8,24},{16,0},{24,8},{1,17},{9,25},{17,1},{25,9},{2,18},{10... | collective-permute-start | bytes 3145736 | tf_op jit(solution)/shard_map/ppermute | solution.py:303
  422.6 3.5 collective-permute-start.22
  430.7 61.8 %collective-permute-start.18 = (bf16[512,1024]{1,0:T(8,128)(2,1)}, bf16[512,1024]{1,0:T(8,128)(2,1)}, u32[]{:S(2)}, u32[]{:S(2)}) collective-permute-start(bf16[512,1024]{1,0:T(8,128)(2,1)} %get-tuple-element.154), channel_id=1, source_target_pairs={{0,24},{8,16},{16,8},{24,0},{1,25},{9,17},{17,9},{25,1},{2,26},{10... | collective-permute-start | bytes 3145736 | tf_op jit(solution)/shard_map/ppermute | solution.py:303
  433.0 59.4 %collective-permute-start.19 = (bf16[512,1024]{1,0:T(8,128)(2,1)}, bf16[512,1024]{1,0:T(8,128)(2,1)}, u32[]{:S(2)}, u32[]{:S(2)}) collective-permute-start(bf16[512,1024]{1,0:T(8,128)(2,1)} %get-tuple-element.155), channel_id=1, source_target_pairs={{0,8},{8,0},{16,24},{24,16},{1,9},{9,1},{17,25},{25,17},{2,10},{10... | collective-permute-start | bytes 3145736 | tf_op jit(solution)/shard_map/ppermute | solution.py:303
  433.6 58.8 %collective-permute-start.20 = (bf16[512,1024]{1,0:T(8,128)(2,1)}, bf16[512,1024]{1,0:T(8,128)(2,1)}, u32[]{:S(2)}, u32[]{:S(2)}) collective-permute-start(bf16[512,1024]{1,0:T(8,128)(2,1)} %get-tuple-element.156), channel_id=1, source_target_pairs={{0,16},{8,24},{16,0},{24,8},{1,17},{9,25},{17,1},{25,9},{2,18},{10... | collective-permute-start | bytes 3145736 | tf_op jit(solution)/shard_map/ppermute | solution.py:303
  434.2 68.1 %collective-permute-start.21 = (bf16[512,1024]{1,0:T(8,128)(2,1)}, bf16[512,1024]{1,0:T(8,128)(2,1)}, u32[]{:S(2)}, u32[]{:S(2)}) collective-permute-start(bf16[512,1024]{1,0:T(8,128)(2,1)} %get-tuple-element.157), channel_id=1, source_target_pairs={{0,24},{8,16},{16,8},{24,0},{1,25},{9,17},{17,9},{25,1},{2,26},{10... | collective-permute-start | bytes 3145736 | tf_op jit(solution)/shard_map/ppermute | solution.py:303
  510.5 15.0 %collective-permute-start.23 = (bf16[192,2048]{1,0:T(8,128)(2,1)}, bf16[192,2048]{1,0:T(8,128)(2,1)}, u32[]{:S(2)}, u32[]{:S(2)}) collective-permute-start(bf16[192,2048]{1,0:T(8,128)(2,1)} %fusion.43), channel_id=1, source_target_pairs={{0,1},{1,0},{2,3},{3,2},{4,5},{5,4},{6,7},{7,6},{8,9},{9,8},{10,11... | collective-permute-start | bytes 2359304 | tf_op jit(solution)/shard_map/ppermute | solution.py:303
  511.5 24.0 %all-to-all-start.4 = ((bf16[8,192,256]{2,1,0:T(8,128)(2,1)}), bf16[8,192,256]{2,1,0:T(8,128)(2,1)}, u32[]{:S(2)}, u32[]{:S(2)}) async-start(bf16[8,192,256]{2,1,0:T(8,128)(2,1)} %bitcast.260), calls=%async_computation.6 | async-start | bytes 1572864 | tf_op jit(solution)/shard_map/all_to_all | solution.py:358
  538.6 57.2 %all-to-all-start.5 = ((bf16[2,8,64,1024]{3,2,0,1:T(8,128)(2,1)}), bf16[2,8,64,1024]{3,2,0,1:T(8,128)(2,1)}, u32[]{:S(2)}, u32[]{:S(2)}) async-start(bf16[2,8,64,1024]{3,2,0,1:T(8,128)(2,1)} %copy.107), calls=%async_computation.7 | async-start | bytes 4194304 | tf_op jit(solution)/shard_map/all_to_all | solution.py:598
  546.6 170.6 %reduce-scatter.8.cloned.1.call-start = ((), (), s32[]{:S(2)}) async-start(), calls=%async_computation.16 | async-start | bytes 7077888 | tf_op jit(solution)/shard_map/reduce_scatter | solution.py:366
  546.6 26.3 %collective-permute-start.24 = (bf16[4,64,2048]{2,1,0:T(8,128)(2,1)}, bf16[4,64,2048]{2,1,0:T(8,128)(2,1)}, u32[]{:S(2)}, u32[]{:S(2)}) collective-permute-start(bf16[4,64,2048]{2,1,0:T(8,128)(2,1)} %get-tuple-element.171), channel_id=1, source_target_pairs={{0,8},{8,0},{16,24},{24,16},{1,9},{9,1},{17,25},{25,17},{2,10},{10... | collective-permute-start | bytes 3145736 | tf_op jit(solution)/shard_map/ppermute | solution.py:303
  548.1 47.7 %collective-permute-start.25 = (bf16[4,64,2048]{2,1,0:T(8,128)(2,1)}, bf16[4,64,2048]{2,1,0:T(8,128)(2,1)}, u32[]{:S(2)}, u32[]{:S(2)}) collective-permute-start(bf16[4,64,2048]{2,1,0:T(8,128)(2,1)} %get-tuple-element.172), channel_id=1, source_target_pairs={{0,16},{8,24},{16,0},{24,8},{1,17},{9,25},{17,1},{25,9},{2,18},{10... | collective-permute-start | bytes 3145736 | tf_op jit(solution)/shard_map/ppermute | solution.py:303
  549.6 46.3 %collective-permute-start.26 = (bf16[4,64,2048]{2,1,0:T(8,128)(2,1)}, bf16[4,64,2048]{2,1,0:T(8,128)(2,1)}, u32[]{:S(2)}, u32[]{:S(2)}) collective-permute-start(bf16[4,64,2048]{2,1,0:T(8,128)(2,1)} %get-tuple-element.173), channel_id=1, source_target_pairs={{0,24},{8,16},{16,8},{24,0},{1,25},{9,17},{17,9},{25,1},{2,26},{10... | collective-permute-start | bytes 3145736 | tf_op jit(solution)/shard_map/ppermute | solution.py:303
  611.6 16.9 %collective-permute-start.32 = (bf16[64,2048]{1,0:T(8,128)(2,1)S(1)}, bf16[64,2048]{1,0:T(8,128)(2,1)S(1)}, u32[]{:S(2)}, u32[]{:S(2)}) collective-permute-start(bf16[64,2048]{1,0:T(8,128)(2,1)S(1)} %get-tuple-element.242), channel_id=1, source_target_pairs={{0,6},{1,7},{2,0},{3,1},{4,2},{5,3},{6,4},{7,5},{8,14},{9,15},{10,... | collective-permute-start | bytes 786440 | tf_op jit(solution)/shard_map/ppermute | solution.py:336
  622.4 39.2 %collective-permute-start.29 = (bf16[512,768]{1,0:T(8,128)(2,1)}, bf16[512,768]{1,0:T(8,128)(2,1)}, u32[]{:S(2)}, u32[]{:S(2)}) collective-permute-start(bf16[512,768]{1,0:T(8,128)(2,1)} %get-tuple-element.233), channel_id=1, source_target_pairs={{0,24},{8,16},{16,8},{24,0},{1,25},{9,17},{17,9},{25,1},{2,26},{10... | collective-permute-start | bytes 2359304 | tf_op jit(solution)/shard_map/ppermute | solution.py:303
  624.4 37.2 %collective-permute-start.28 = (bf16[512,768]{1,0:T(8,128)(2,1)}, bf16[512,768]{1,0:T(8,128)(2,1)}, u32[]{:S(2)}, u32[]{:S(2)}) collective-permute-start(bf16[512,768]{1,0:T(8,128)(2,1)} %get-tuple-element.234), channel_id=1, source_target_pairs={{0,16},{8,24},{16,0},{24,8},{1,17},{9,25},{17,1},{25,9},{2,18},{10... | collective-permute-start | bytes 2359304 | tf_op jit(solution)/shard_map/ppermute | solution.py:303
  625.1 36.6 %collective-permute-start.27 = (bf16[512,768]{1,0:T(8,128)(2,1)}, bf16[512,768]{1,0:T(8,128)(2,1)}, u32[]{:S(2)}, u32[]{:S(2)}) collective-permute-start(bf16[512,768]{1,0:T(8,128)(2,1)} %get-tuple-element.235), channel_id=1, source_target_pairs={{0,8},{8,0},{16,24},{24,16},{1,9},{9,1},{17,25},{25,17},{2,10},{10... | collective-permute-start | bytes 2359304 | tf_op jit(solution)/shard_map/ppermute | solution.py:303
  625.9 24.1 %collective-permute-start.31 = (bf16[64,2048]{1,0:T(8,128)(2,1)}, bf16[64,2048]{1,0:T(8,128)(2,1)}, u32[]{:S(2)}, u32[]{:S(2)}) collective-permute-start(bf16[64,2048]{1,0:T(8,128)(2,1)} %get-tuple-element.243), channel_id=1, source_target_pairs={{0,4},{1,5},{2,6},{3,7},{4,0},{5,1},{6,2},{7,3},{8,12},{9,13},{10,... | collective-permute-start | bytes 786440 | tf_op jit(solution)/shard_map/ppermute | solution.py:336
  628.5 33.2 %collective-permute-start.30 = (bf16[64,2048]{1,0:T(8,128)(2,1)}, bf16[64,2048]{1,0:T(8,128)(2,1)}, u32[]{:S(2)}, u32[]{:S(2)}) collective-permute-start(bf16[64,2048]{1,0:T(8,128)(2,1)} %get-tuple-element.244), channel_id=1, source_target_pairs={{0,2},{1,3},{2,4},{3,5},{4,6},{5,7},{6,0},{7,1},{8,10},{9,11},{10,... | collective-permute-start | bytes 786440 | tf_op jit(solution)/shard_map/ppermute | solution.py:336
  647.6 15.5 %copy-start.12 = (f32[8,8,32,256]{3,1,2,0:T(8,128)S(1)}, f32[8,8,32,256]{3,1,2,0:T(8,128)}, u32[]{:S(2)}) copy-start(f32[8,8,32,256]{3,1,2,0:T(8,128)} %copy.123) | copy-start | bytes 6291460
  647.6 15.5 %copy-start.21 = (bf16[64,8192]{1,0:T(8,128)(2,1)S(1)}, bf16[64,8192]{1,0:T(8,128)(2,1)}, u32[]{:S(2)}) copy-start(bf16[64,8192]{1,0:T(8,128)(2,1)} %param.21) | copy-start | bytes 3145732
  647.6 15.5 %copy-start.23 = (bf16[64,8192]{1,0:T(8,128)(2,1)S(1)}, bf16[64,8192]{1,0:T(8,128)(2,1)}, u32[]{:S(2)}) copy-start(bf16[64,8192]{1,0:T(8,128)(2,1)} %param.20) | copy-start | bytes 3145732
  647.6 15.4 %copy-start.40 = (f32[64]{0:T(128)S(1)}, f32[64]{0:T(128)}, u32[]{:S(2)}) copy-start(f32[64]{0:T(128)} %copy-done.39) | copy-start | bytes 772
  661.6 17.6 %collective-permute-start.33 = (bf16[256,1024]{1,0:T(8,128)(2,1)}, bf16[256,1024]{1,0:T(8,128)(2,1)}, u32[]{:S(2)}, u32[]{:S(2)}) collective-permute-start(bf16[256,1024]{1,0:T(8,128)(2,1)} %get-tuple-element.202), channel_id=1, source_target_pairs={{0,8},{8,0},{16,24},{24,16},{1,9},{9,1},{17,25},{25,17},{2,10},{10... | collective-permute-start | bytes 1572872 | tf_op jit(solution)/shard_map/ppermute | solution.py:303
  666.3 26.4 %copy-start.26 = (bf16[256,1024]{1,0:T(8,128)(2,1)S(1)}, bf16[256,1024]{1,0:T(8,128)(2,1)}, u32[]{:S(2)}) copy-start(bf16[256,1024]{1,0:T(8,128)(2,1)} %get-tuple-element.201) | copy-start | bytes 1572868
  666.3 26.4 %collective-permute-start.34 = (bf16[256,1024]{1,0:T(8,128)(2,1)}, bf16[256,1024]{1,0:T(8,128)(2,1)}, u32[]{:S(2)}, u32[]{:S(2)}) collective-permute-start(bf16[256,1024]{1,0:T(8,128)(2,1)} %get-tuple-element.203), channel_id=1, source_target_pairs={{0,16},{8,24},{16,0},{24,8},{1,17},{9,25},{17,1},{25,9},{2,18},{10... | collective-permute-start | bytes 1572872 | tf_op jit(solution)/shard_map/ppermute | solution.py:303
  667.1 25.6 %collective-permute-start.35 = (bf16[256,1024]{1,0:T(8,128)(2,1)}, bf16[256,1024]{1,0:T(8,128)(2,1)}, u32[]{:S(2)}, u32[]{:S(2)}) collective-permute-start(bf16[256,1024]{1,0:T(8,128)(2,1)} %get-tuple-element.204), channel_id=1, source_target_pairs={{0,24},{8,16},{16,8},{24,0},{1,25},{9,17},{17,9},{25,1},{2,26},{10... | collective-permute-start | bytes 1572872 | tf_op jit(solution)/shard_map/ppermute | solution.py:303
  671.3 42.4 %all-to-all-start.6 = ((bf16[8,64,768]{2,1,0:T(8,128)(2,1)}), bf16[8,64,768]{2,1,0:T(8,128)(2,1)S(1)}, u32[]{:S(2)}, u32[]{:S(2)}) async-start(bf16[8,64,768]{2,1,0:T(8,128)(2,1)} %bitcast.85), calls=%async_computation.9 | async-start | bytes 1572864 | tf_op jit(solution)/shard_map/all_to_all | solution.py:358
  677.1 34.8 %copy-start.25 = (bf16[256,1024]{1,0:T(8,128)(2,1)S(1)}, bf16[256,1024]{1,0:T(8,128)(2,1)}, u32[]{:S(2)}) copy-start(bf16[256,1024]{1,0:T(8,128)(2,1)} %get-tuple-element.205) | copy-start | bytes 1572868
  677.1 22.2 %collective-permute-start.36 = (bf16[256,1024]{1,0:T(8,128)(2,1)}, bf16[256,1024]{1,0:T(8,128)(2,1)S(1)}, u32[]{:S(2)}, u32[]{:S(2)}) collective-permute-start(bf16[256,1024]{1,0:T(8,128)(2,1)} %get-tuple-element.206), channel_id=1, source_target_pairs={{0,8},{8,0},{16,24},{24,16},{1,9},{9,1},{17,25},{25,17},{2,10},{10... | collective-permute-start | bytes 1572872 | tf_op jit(solution)/shard_map/ppermute | solution.py:303
  678.5 33.4 %collective-permute-start.37 = (bf16[256,1024]{1,0:T(8,128)(2,1)}, bf16[256,1024]{1,0:T(8,128)(2,1)S(1)}, u32[]{:S(2)}, u32[]{:S(2)}) collective-permute-start(bf16[256,1024]{1,0:T(8,128)(2,1)} %get-tuple-element.207), channel_id=1, source_target_pairs={{0,16},{8,24},{16,0},{24,8},{1,17},{9,25},{17,1},{25,9},{2,18},{10... | collective-permute-start | bytes 1572872 | tf_op jit(solution)/shard_map/ppermute | solution.py:303
  679.2 32.7 %collective-permute-start.38 = (bf16[256,1024]{1,0:T(8,128)(2,1)}, bf16[256,1024]{1,0:T(8,128)(2,1)S(1)}, u32[]{:S(2)}, u32[]{:S(2)}) collective-permute-start(bf16[256,1024]{1,0:T(8,128)(2,1)} %get-tuple-element.208), channel_id=1, source_target_pairs={{0,24},{8,16},{16,8},{24,0},{1,25},{9,17},{17,9},{25,1},{2,26},{10... | collective-permute-start | bytes 1572872 | tf_op jit(solution)/shard_map/ppermute | solution.py:303
  (43 other events, 211.9 us)
Sparse Core Ops, SparseCore 0:
  9.7 94.3 all-gather.14
  121.1 56.0 all-gather.10
  179.1 61.0 all-gather.8
  246.4 64.4 all-gather.6
  312.9 38.1 all-gather.12
  353.3 66.7 reduce-scatter.3
  422.8 68.1 reduce-scatter.5
  605.1 104.5 reduce-scatter.7

commit v5 on v4

--- a/solution.py
+++ b/solution.py
@@ -601,16 +601,17 @@
     d_qkv = attention_back(
         prefix, query, key, value, d_head, log_total, row_delta, cosine, sine
     )
-    d_qkv, gate_up_sum, output_parts = join((d_qkv, gate_up_sum, output_parts))
+    qkv_split = split_parts_dp(
+        mul_left(xn_one, d_qkv).astype(BF16).reshape(4, groups * shard, 3 * HD)
+    )
+    d_qkv, gate_up_sum, output_parts, qkv_split = join(
+        (d_qkv, gate_up_sum, output_parts, qkv_split)
+    )
     gate_sum, up_sum = gate_up_sum[0], gate_up_sum[1]
     dn_part_one = mul_right(d_qkv, qkv_w).astype(BF16)
-    dn_part_one, xn_one, d_qkv, mlp_sum = join((dn_part_one, xn_one, d_qkv, mlp_sum))
+    dn_part_one, mlp_sum = join((dn_part_one, mlp_sum))
     dn_one = scatter(dn_part_one, CTX)
     result = (hid_res + mlp_sum).astype(BF16)[None]
-
-    qkv_split = split_parts_dp(
-        mul_left(xn_one, d_qkv).astype(BF16).reshape(4, groups * shard, 3 * HD)
-    )
     qkv_parts = qkv_split[:1] + send_parts_dp(qkv_split)
     column = add_parts(output_parts)
     chip = lax.axis_index(("half", "low"))

time: 742 us -> 731 us (0.985)
    all_to_all x6, waiting for transfers between devices: 30.6 us -> 21.8 us  [swap(): return lax.all_to_all(values, axes, split_axis=0, concat_axis=0, tiled=True)]
    unnamed x112 -> x116, local copies, waits for them, and re-layouts: 21.9 us -> 18 us
  transfers between devices with their start and end apart: 54 -> 54, of which waited for: 23 -> 22; matrix products, arithmetic and copies ran while one was open for 41% -> 42% of each run, Pallas kernels for 1% -> 1%
where the time goes in v5:
time: 731 us; the launch traced here: 718 us
  waiting for transfers between devices  265 us (36%)
  matrix products  154 us (21%)
  local copies, waits for them, and re-layouts  110 us (15%)
  starting transfers between devices  91.9 us (13%)
  other arithmetic  72.1 us (10%)
  between operations  16.2 us (2%)
  Pallas kernels  8.88 us (1%)
    ppermute x33, waiting for transfers between devices, flip(): lax.ppermute(values, axis, [(i, i ^ bits) for i in range(lax.axis_size(ax...  133 us
    dot_general x7, matrix products, mul_right(): lax.dot_general(first_op, second_op, (((1,), (1,)), ((), ())), preferred_...  63.5 us
    dot_general x6, matrix products, mul_plain(): return jnp.dot(first_op, second_op, preferred_element_type=jnp.float32)  49.1 us
    ppermute x6, waiting for transfers between devices, turn_chips(): return lax.ppermute(values, CTX, pairs)  48 us
    reduce_scatter x3, waiting for transfers between devices, scatter(): lax.psum_scatter(values, axes, scatter_dimension=0, tiled=True).astype(F32)  42 us
    dot_general x6, matrix products, mul_left(): lax.dot_general(first_op, second_op, (((0,), (0,)), ((), ())), preferred_...  41.1 us
    ppermute x33, starting transfers between devices, flip(): lax.ppermute(values, axis, [(i, i ^ bits) for i in range(lax.axis_size(ax...  38.4 us
    all_to_all x6, starting transfers between devices, swap(): return lax.all_to_all(values, axes, split_axis=0, concat_axis=0, tiled=True)  36.4 us
  transfers between devices with their start and end apart: 54, of which 22 were waited for; matrix products, arithmetic and copies ran while one was open for 42% of the time, Pallas kernels for 1%

profile of v5, /device:TPU:8, one launch (start us, length us, event | category | flops | bytes accessed | tf_op | source)
XLA Modules:
  0.0 718.2 jit_solution(18124333803211308263)
XLA Ops:
  17.9 5.3 all-to-all-start
  23.3 2.8 multiply_sine_fusion
  45.6 12.5 %collective-permute-done.4 = bf16[256,2048]{1,0:T(8,128)(2,1)} collective-permute-done((bf16[256,2048]{1,0:T(8,128)(2,1)}, bf16[256,2048]{1,0:T(8,128)(2,1)}, u32[]{:S(2)}, u32[]{:S(2)}) %collective-permute-start.4) | collective-permute-done | bytes 1048608 | tf_op jit(solution)/shard_map/ppermute | solution.py:303
  76.6 25.6 %collective-permute-done.6 = bf16[64,2048]{1,0:T(8,128)(2,1)S(1)} collective-permute-done((bf16[64,2048]{1,0:T(8,128)(2,1)S(1)}, bf16[64,2048]{1,0:T(8,128)(2,1)S(1)}, u32[]{:S(2)}, u32[]{:S(2)}) %collective-permute-start.6) | collective-permute-done | bytes 262176 | tf_op jit(solution)/shard_map/ppermute | solution.py:336
  107.4 4.8 collective-permute-done.8
  113.0 4.1 fusion
  117.0 2.7 collective-permute-start.11
  120.6 5.5 all-to-all-start.1
  126.6 8.4 %fusion.7 = f32[1536,768]{1,0:T(8,128)S(1)} fusion(bf16[2048,768]{1,0:T(8,128)(2,1)} %bitcast.11, bf16[1536,2048]{1,0:T(8,128)(2,1)} %bitcast.244, f32[1536]{0:T(1024)S(1)} %add_rsqrt_fusion), kind=kOutput, calls=%fused_computation.31 | convolution fusion | flops 4841275392 | bytes 14161920 | tf_op jit(solution)/shard_map/dot_general | solution.py:22
  143.1 22.2 %collective-permute-done.9 = bf16[4,64,2048]{2,1,0:T(8,128)(2,1)} collective-permute-done((bf16[4,64,2048]{2,1,0:T(8,128)(2,1)}, bf16[4,64,2048]{2,1,0:T(8,128)(2,1)}, u32[]{:S(2)}, u32[]{:S(2)}) %collective-permute-start.9) | collective-permute-done | bytes 1048608 | tf_op jit(solution)/shard_map/ppermute | solution.py:303
  172.9 6.0 all-to-all-start.2
  178.9 4.6 fusion.48
  185.5 2.9 fusion.49
  188.5 13.6 %all-to-all-done.2 = bf16[8,64,1024]{2,1,0:T(8,128)(2,1)} async-done(((bf16[8,64,1024]{2,1,0:T(8,128)(2,1)}), bf16[8,64,1024]{2,1,0:T(8,128)(2,1)}, u32[]{:S(2)}, u32[]{:S(2)}) %all-to-all-start.2) | async-done | bytes 1048608 | tf_op jit(solution)/shard_map/all_to_all | solution.py:358
  204.6 7.4 %all-to-all-start.3 = ((bf16[8,192,256]{2,1,0:T(8,128)(2,1)}), bf16[8,192,256]{2,1,0:T(8,128)(2,1)}, u32[]{:S(2)}, u32[]{:S(2)}) async-start(bf16[8,192,256]{2,1,0:T(8,128)(2,1)} %bitcast.260), calls=%async_computation.3 | async-start | bytes 1572864 | tf_op jit(solution)/shard_map/all_to_all | solution.py:358
  212.1 5.8 select_bitcast_fusion.1
  217.9 7.5 %pad_maximum_fusion = bf16[4,4,2,64,2048]{4,3,2,1,0:T(8,128)(2,1)} fusion(bf16[4,4,1,64,2048]{4,3,2,1,0:T(8,128)(2,1)} %get-tuple-element.218, bf16[4,4,1,64,2048]{4,3,2,1,0:T(8,128)(2,1)} %get-tuple-element.217), kind=kLoop, calls=%fused_computation.11 | loop fusion | flops 4194304 | bytes 16777216 | tf_op jit(solution)/shard_map/stack | solution.py:354
  225.4 4.2 all-to-all-done.3
  230.8 5.8 multiply_reduce_fusion.2
  247.3 17.9 %collective-permute-done.13 = bf16[512,1024]{1,0:T(8,128)(2,1)S(1)} collective-permute-done((bf16[512,1024]{1,0:T(8,128)(2,1)}, bf16[512,1024]{1,0:T(8,128)(2,1)S(1)}, u32[]{:S(2)}, u32[]{:S(2)}) %collective-permute-start.13) | collective-permute-done | bytes 1048608 | tf_op jit(solution)/shard_map/ppermute | solution.py:303
  266.3 21.8 %collective-permute-done.14 = bf16[512,1024]{1,0:T(8,128)(2,1)S(1)} collective-permute-done((bf16[512,1024]{1,0:T(8,128)(2,1)}, bf16[512,1024]{1,0:T(8,128)(2,1)S(1)}, u32[]{:S(2)}, u32[]{:S(2)}) %collective-permute-start.14) | collective-permute-done | bytes 1048608 | tf_op jit(solution)/shard_map/ppermute | solution.py:303
  290.3 12.4 %all-gather.7.cloned.1.call-done = bf16[1536,2048]{1,0:T(8,128)(2,1)} async-done(((bf16[192,2048]{1,0:T(8,128)(2,1)}), bf16[1536,2048]{1,0:T(8,128)(2,1)}) %all-gather.7.cloned.1.call-update) | async-done | bytes 6291472 | tf_op jit(solution)/shard_map/all_gather | solution.py:362
  302.8 10.1 %fusion.50 = f32[1536,1024]{1,0:T(8,128)S(1)} fusion(bf16[1536,2048]{1,0:T(8,128)(2,1)} %all-gather.7.cloned.1.call-done, bf16[2048,1024]{1,0:T(8,128)(2,1)} %all-gather.9.cloned.1.call-done), kind=kOutput, calls=%fused_computation.188 | convolution fusion | flops 6442450944 | bytes 16777216 | tf_op jit(solution)/shard_map/dot_general | solution.py:22
  312.9 13.1 %multiply_convert_fusion.2 = (bf16[1536,1024]{1,0:T(8,128)(2,1)S(1)}, f32[1536,1024]{1,0:T(8,128)}) fusion(f32[1536,1024]{1,0:T(8,128)S(1)} %fusion.50, bf16[1536,2048]{1,0:T(8,128)(2,1)S(1)} %copy-done.43, bf16[2048,1024]{1,0:T(8,128)(2,1)} %bitcast.38), kind=kOutput, calls=%fused_computation.17 | convolution fusion | flops 6451888128 | bytes 26214400 | tf_op jit(solution)/shard_map/dot_general | solution.py:22
  327.7 8.7 %convolution_convert_fusion.1 = bf16[1536,2048]{1,0:T(8,128)(2,1)} fusion(bf16[1536,1024]{1,0:T(8,128)(2,1)S(1)} %get-tuple-element.160, bf16[1024,2048]{1,0:T(8,128)(2,1)S(1)} %bitcast.252), kind=kOutput, calls=%fused_computation.13 | convolution fusion | flops 6445596672 | bytes 13631488 | tf_op jit(solution)/shard_map/dot_general | solution.py:22
  336.4 6.5 all-gather.13.cloned.1.call-done
  343.1 8.9 %fusion.14 = f32[1536,1024]{1,0:T(8,128)} fusion(bf16[1536,1024]{1,0:T(8,128)(2,1)} %all-gather.11.cloned.1.call-done, bf16[1024,2048]{1,0:T(8,128)(2,1)} %bitcast.251), kind=kOutput, calls=%fused_computation.46 | convolution fusion | flops 3221225472 | bytes 11534336 | tf_op jit(solution)/shard_map/dot_general | solution.py:26
  351.9 11.9 %multiply_convert_fusion = (bf16[1536,1024]{1,0:T(8,128)(2,1)}, bf16[1536,1024]{1,0:T(8,128)(2,1)}) fusion(f32[1536,1024]{1,0:T(8,128)} %copy-done.50, f32[1536,1024]{1,0:T(8,128)} %get-tuple-element.141, f32[1536,1024]{1,0:T(8,128)} %fusion.14, bf16[1536,1024]{1,0:T(8,128)(2,1)S(1)} %copy-done.46, bf16[1024,2048]{1,0:T(8,128)(2,1)S(1)} %bitcast.253), kind=kOutput, calls=%fused_computation.14 | convolution fusion | flops 3243245568 | bytes 30408704 | tf_op jit(solution)/shard_map/dot_general | solution.py:26
  363.9 8.8 %convolution_convert_fusion.2 = bf16[2048,1024]{1,0:T(8,128)(2,1)S(1)} fusion(bf16[1536,2048]{1,0:T(8,128)(2,1)S(1)} %bitcast.278, bf16[1536,1024]{1,0:T(8,128)(2,1)} %get-tuple-element.145), kind=kOutput, calls=%fused_computation.23 | convolution fusion | flops 6444548096 | bytes 13631488 | tf_op jit(solution)/shard_map/dot_general | solution.py:32
  372.7 7.3 %convolution_convert_fusion.3 = bf16[2048,1024]{1,0:T(8,128)(2,1)S(1)} fusion(bf16[1536,2048]{1,0:T(8,128)(2,1)S(1)} %bitcast.278, bf16[1536,1024]{1,0:T(8,128)(2,1)S(1)} %copy-done.51), kind=kOutput, calls=%fused_computation.24 | convolution fusion | flops 6444548096 | bytes 13631488 | tf_op jit(solution)/shard_map/dot_general | solution.py:32
  380.0 4.2 dynamic-slice_bitcast_fusion.4
  387.2 9.6 %fusion.51 = f32[1536,2048]{1,0:T(8,128)} fusion(bf16[1536,1024]{1,0:T(8,128)(2,1)S(1)} %copy-done.52, bf16[2048,1024]{1,0:T(8,128)(2,1)S(1)} %copy-done.44), kind=kOutput, calls=%fused_computation.189 | convolution fusion | flops 6442450944 | bytes 19922944 | tf_op jit(solution)/shard_map/dot_general | solution.py:26
  396.8 13.1 %add_convert_fusion = bf16[1536,2048]{1,0:T(8,128)(2,1)} fusion(f32[1536,2048]{1,0:T(8,128)} %fusion.51, bf16[1536,1024]{1,0:T(8,128)(2,1)} %get-tuple-element.145, bf16[2048,1024]{1,0:T(8,128)(2,1)} %bitcast.38), kind=kOutput, calls=%fused_computation.4 | convolution fusion | flops 6448742400 | bytes 26214400 | tf_op jit(solution)/shard_map/dot_general | solution.py:26
  428.3 6.5 convolution_convert_fusion.7
  437.6 3.8 convolution_convert_fusion.8
  442.8 40.0 %reduce-scatter.6.cloned.1.call-done = bf16[192,2048]{1,0:T(8,128)(2,1)} async-done(((bf16[1536,2048]{1,0:T(8,128)(2,1)}), bf16[192,2048]{1,0:T(8,128)(2,1)}) %reduce-scatter.6.cloned.1.call-update) | async-done | bytes 786448 | tf_op jit(solution)/shard_map/reduce_scatter | solution.py:366
  484.3 9.8 %collective-permute-done.21 = bf16[512,1024]{1,0:T(8,128)(2,1)} collective-permute-done((bf16[512,1024]{1,0:T(8,128)(2,1)}, bf16[512,1024]{1,0:T(8,128)(2,1)}, u32[]{:S(2)}, u32[]{:S(2)}) %collective-permute-start.21) | collective-permute-done | bytes 1048608 | tf_op jit(solution)/shard_map/ppermute | solution.py:303
  495.7 6.5 convolution_convert_fusion.6
  503.3 6.5 all-to-all-start.4
  509.8 3.2 fusion.29
  513.0 2.8 fusion.30
  517.3 3.8 convolution_convert_fusion.4
  523.3 4.0 all-to-all-done.4
  527.3 3.1 copy.107
  530.4 8.0 %all-to-all-start.5 = ((bf16[2,8,64,1024]{3,2,0,1:T(8,128)(2,1)}), bf16[2,8,64,1024]{3,2,0,1:T(8,128)(2,1)}, u32[]{:S(2)}, u32[]{:S(2)}) async-start(bf16[2,8,64,1024]{3,2,0,1:T(8,128)(2,1)} %copy.107), calls=%async_computation.7 | async-start | bytes 4194304 | tf_op jit(solution)/shard_map/all_to_all | solution.py:598
  538.4 3.0 copy.106
  550.3 8.9 %shard_map.203 = bf16[1536,768]{1,0:T(8,128)(2,1)S(1)} custom-call(s32[1]{0:T(128)} %copy.150.prefix_ref, bf16[1536,256]{1,0:T(8,128)(2,1)S(1)} %copy-done.3, bf16[1536,256]{1,0:T(8,128)(2,1)S(1)} %copy-done.2, bf16[1536,256]{1,0:T(8,128)(2,1)S(1)} %copy-done.1, bf16[1536,256]{1,0:T(8,128)(2,1)} %bitcast.71.grad_ref, f32[3,1,512]{2,1,0:T(1,128)S(1)} %add.324.log_ref, ...), custom_call_target="tpu_custom_call" | custom-call | flops 1000000 | bytes 10000 | tf_op jit(solution)/shard_map/pallas_call | solution.py:432
  559.2 10.9 %convolution_convert_fusion.5 = bf16[2048,768]{1,0:T(8,128)(2,1)S(1)} fusion(bf16[1536,768]{1,0:T(8,128)(2,1)S(1)} %shard_map.203, bf16[1536,2048]{1,0:T(8,128)(2,1)} %bitcast.245, f32[1536]{0:T(1024)S(1)} %copy-done.40), kind=kOutput, calls=%fused_computation.26 | convolution fusion | flops 4842848256 | bytes 11802624 | tf_op jit(solution)/shard_map/dot_general | solution.py:32
  571.9 20.8 %collective-permute-done.25 = bf16[4,64,2048]{2,1,0:T(8,128)(2,1)} collective-permute-done((bf16[4,64,2048]{2,1,0:T(8,128)(2,1)}, bf16[4,64,2048]{2,1,0:T(8,128)(2,1)}, u32[]{:S(2)}, u32[]{:S(2)}) %collective-permute-start.25) | collective-permute-done | bytes 1048608 | tf_op jit(solution)/shard_map/ppermute | solution.py:303
  592.7 8.8 %convolution_convert_fusion = bf16[1536,2048]{1,0:T(8,128)(2,1)} fusion(bf16[1536,768]{1,0:T(8,128)(2,1)S(1)} %copy-done.5, bf16[2048,768]{1,0:T(8,128)(2,1)} %bitcast.11), kind=kOutput, calls=%fused_computation.12 | convolution fusion | flops 4834983936 | bytes 11796480 | tf_op jit(solution)/shard_map/dot_general | solution.py:26
  601.6 2.9 convert_add_fusion
  612.3 9.6 %collective-permute-done.32 = bf16[64,2048]{1,0:T(8,128)(2,1)S(1)} collective-permute-done((bf16[64,2048]{1,0:T(8,128)(2,1)S(1)}, bf16[64,2048]{1,0:T(8,128)(2,1)S(1)}, u32[]{:S(2)}, u32[]{:S(2)}) %collective-permute-start.32) | collective-permute-done | bytes 262176 | tf_op jit(solution)/shard_map/ppermute | solution.py:336
  622.0 3.3 slice_convert_fusion.1
  625.3 3.4 reshape.289
  628.7 2.9 copy.112
  636.0 2.8 copy.111
  641.2 8.0 %collective-permute-done.30 = bf16[64,2048]{1,0:T(8,128)(2,1)} collective-permute-done((bf16[64,2048]{1,0:T(8,128)(2,1)}, bf16[64,2048]{1,0:T(8,128)(2,1)}, u32[]{:S(2)}, u32[]{:S(2)}) %collective-permute-start.30) | collective-permute-done | bytes 262176 | tf_op jit(solution)/shard_map/ppermute | solution.py:336
  650.7 3.3 broadcast_multiply_fusion
  656.0 2.9 add_convert_fusion.3
  658.9 5.7 all-to-all-start.6
  670.1 10.3 %collective-permute-done.34 = bf16[256,1024]{1,0:T(8,128)(2,1)} collective-permute-done((bf16[256,1024]{1,0:T(8,128)(2,1)}, bf16[256,1024]{1,0:T(8,128)(2,1)}, u32[]{:S(2)}, u32[]{:S(2)}) %collective-permute-start.34) | collective-permute-done | bytes 524320 | tf_op jit(solution)/shard_map/ppermute | solution.py:303
  682.0 4.8 collective-permute-done.36
  686.9 12.9 %collective-permute-done.37 = bf16[256,1024]{1,0:T(8,128)(2,1)S(1)} collective-permute-done((bf16[256,1024]{1,0:T(8,128)(2,1)}, bf16[256,1024]{1,0:T(8,128)(2,1)S(1)}, u32[]{:S(2)}, u32[]{:S(2)}) %collective-permute-start.37) | collective-permute-done | bytes 524320 | tf_op jit(solution)/shard_map/ppermute | solution.py:303
  707.0 3.9 fusion.32
  (300 shorter events, 168.6 us)
Async XLA Ops:
  7.2 105.8 %all-gather.15.cloned.1.call-start = ((), (), s32[]{:S(2)}) async-start(), calls=%async_computation.17 | async-start | bytes 7077888 | tf_op jit(solution)/shard_map/all_gather | solution.py:362
  7.9 35.3 %collective-permute-start.3 = (bf16[256,2048]{1,0:T(8,128)(2,1)}, bf16[256,2048]{1,0:T(8,128)(2,1)}, u32[]{:S(2)}, u32[]{:S(2)}) collective-permute-start(bf16[256,2048]{1,0:T(8,128)(2,1)} %param.22), channel_id=1, source_target_pairs={{0,8},{8,0},{16,24},{24,16},{1,9},{9,1},{17,25},{25,17},{2,10},{10... | collective-permute-start | bytes 3145736 | tf_op jit(solution)/shard_map/ppermute | solution.py:303
  9.5 50.9 %collective-permute-start.5 = (bf16[256,2048]{1,0:T(8,128)(2,1)}, bf16[256,2048]{1,0:T(8,128)(2,1)}, u32[]{:S(2)}, u32[]{:S(2)}) collective-permute-start(bf16[256,2048]{1,0:T(8,128)(2,1)} %param.22), channel_id=1, source_target_pairs={{0,24},{8,16},{16,8},{24,0},{1,25},{9,17},{17,9},{25,1},{2,26},{10... | collective-permute-start | bytes 3145736 | tf_op jit(solution)/shard_map/ppermute | solution.py:303
  11.0 47.1 %collective-permute-start.4 = (bf16[256,2048]{1,0:T(8,128)(2,1)}, bf16[256,2048]{1,0:T(8,128)(2,1)}, u32[]{:S(2)}, u32[]{:S(2)}) collective-permute-start(bf16[256,2048]{1,0:T(8,128)(2,1)} %param.22), channel_id=1, source_target_pairs={{0,16},{8,24},{16,0},{24,8},{1,17},{9,25},{17,1},{25,9},{2,18},{10... | collective-permute-start | bytes 3145736 | tf_op jit(solution)/shard_map/ppermute | solution.py:303
  17.9 44.8 %all-to-all-start = ((bf16[8,64,768]{2,1,0:T(8,128)(2,1)}), bf16[8,64,768]{2,1,0:T(8,128)(2,1)}, u32[]{:S(2)}, u32[]{:S(2)}) async-start(bf16[8,64,768]{2,1,0:T(8,128)(2,1)} %copy.90), calls=%async_computation | async-start | bytes 1572864 | tf_op jit(solution)/shard_map/all_to_all | solution.py:358
  23.3 267.0 %all-gather.11.cloned.1.call-start = ((), (), s32[]{:S(2)}) async-start(), calls=%async_computation.12 | async-start | bytes 3538944 | tf_op jit(solution)/shard_map/all_gather | solution.py:362
  43.2 19.6 %copy-start.34 = (bf16[64,2048]{1,0:T(8,128)(2,1)S(1)}, bf16[64,2048]{1,0:T(8,128)(2,1)}, u32[]{:S(2)}) copy-start(bf16[64,2048]{1,0:T(8,128)(2,1)} %param.18) | copy-start | bytes 786436
  62.7 40.1 %collective-permute-start.7 = (bf16[64,2048]{1,0:T(8,128)(2,1)S(1)}, bf16[64,2048]{1,0:T(8,128)(2,1)S(1)}, u32[]{:S(2)}, u32[]{:S(2)}) collective-permute-start(bf16[64,2048]{1,0:T(8,128)(2,1)S(1)} %copy-done.34), channel_id=1, source_target_pairs={{0,4},{1,5},{2,6},{3,7},{4,0},{5,1},{6,2},{7,3},{8,12},{9,13},{10,... | collective-permute-start | bytes 786440 | tf_op jit(solution)/shard_map/ppermute | solution.py:336
  65.3 36.8 %collective-permute-start.6 = (bf16[64,2048]{1,0:T(8,128)(2,1)S(1)}, bf16[64,2048]{1,0:T(8,128)(2,1)S(1)}, u32[]{:S(2)}, u32[]{:S(2)}) collective-permute-start(bf16[64,2048]{1,0:T(8,128)(2,1)S(1)} %copy-done.34), channel_id=1, source_target_pairs={{0,2},{1,3},{2,4},{3,5},{4,6},{5,7},{6,0},{7,1},{8,10},{9,11},{10,... | collective-permute-start | bytes 786440 | tf_op jit(solution)/shard_map/ppermute | solution.py:336
  67.3 36.3 %collective-permute-start.2 = (bf16[512,768]{1,0:T(8,128)(2,1)}, bf16[512,768]{1,0:T(8,128)(2,1)S(1)}, u32[]{:S(2)}, u32[]{:S(2)}) collective-permute-start(bf16[512,768]{1,0:T(8,128)(2,1)} %bitcast.4), channel_id=1, source_target_pairs={{0,24},{8,16},{16,8},{24,0},{1,25},{9,17},{17,9},{25,1},{2,26},{10... | collective-permute-start | bytes 2359304 | tf_op jit(solution)/shard_map/ppermute | solution.py:303
  69.8 33.9 %collective-permute-start.1 = (bf16[512,768]{1,0:T(8,128)(2,1)}, bf16[512,768]{1,0:T(8,128)(2,1)S(1)}, u32[]{:S(2)}, u32[]{:S(2)}) collective-permute-start(bf16[512,768]{1,0:T(8,128)(2,1)} %bitcast.4), channel_id=1, source_target_pairs={{0,16},{8,24},{16,0},{24,8},{1,17},{9,25},{17,1},{25,9},{2,18},{10... | collective-permute-start | bytes 2359304 | tf_op jit(solution)/shard_map/ppermute | solution.py:303
  70.3 33.5 %collective-permute-start = (bf16[512,768]{1,0:T(8,128)(2,1)}, bf16[512,768]{1,0:T(8,128)(2,1)S(1)}, u32[]{:S(2)}, u32[]{:S(2)}) collective-permute-start(bf16[512,768]{1,0:T(8,128)(2,1)} %bitcast.4), channel_id=1, source_target_pairs={{0,8},{8,0},{16,24},{24,16},{1,9},{9,1},{17,25},{25,17},{2,10},{10... | collective-permute-start | bytes 2359304 | tf_op jit(solution)/shard_map/ppermute | solution.py:303
  103.8 8.4 %collective-permute-start.8 = (bf16[64,2048]{1,0:T(8,128)(2,1)S(1)}, bf16[64,2048]{1,0:T(8,128)(2,1)S(1)}, u32[]{:S(2)}, u32[]{:S(2)}) collective-permute-start(bf16[64,2048]{1,0:T(8,128)(2,1)S(1)} %copy-done.34), channel_id=1, source_target_pairs={{0,6},{1,7},{2,0},{3,1},{4,2},{5,3},{6,4},{7,5},{8,14},{9,15},{10,... | collective-permute-start | bytes 786440 | tf_op jit(solution)/shard_map/ppermute | solution.py:336
  117.0 52.9 %collective-permute-start.11 = (bf16[4,64,2048]{2,1,0:T(8,128)(2,1)}, bf16[4,64,2048]{2,1,0:T(8,128)(2,1)}, u32[]{:S(2)}, u32[]{:S(2)}) collective-permute-start(bf16[4,64,2048]{2,1,0:T(8,128)(2,1)} %bitcast_dynamic-update-slice_fusion.16), channel_id=1, source_target_pairs={{0,24},{8,16},{16,8},{24,0},{1,25},{9,17},{17,9},{25,1},{2,26},{10... | collective-permute-start | bytes 3145736 | tf_op jit(solution)/shard_map/ppermute | solution.py:303
  119.7 47.8 %collective-permute-start.10 = (bf16[4,64,2048]{2,1,0:T(8,128)(2,1)}, bf16[4,64,2048]{2,1,0:T(8,128)(2,1)}, u32[]{:S(2)}, u32[]{:S(2)}) collective-permute-start(bf16[4,64,2048]{2,1,0:T(8,128)(2,1)} %bitcast_dynamic-update-slice_fusion.16), channel_id=1, source_target_pairs={{0,16},{8,24},{16,0},{24,8},{1,17},{9,25},{17,1},{25,9},{2,18},{10... | collective-permute-start | bytes 3145736 | tf_op jit(solution)/shard_map/ppermute | solution.py:303
  120.2 45.0 %collective-permute-start.9 = (bf16[4,64,2048]{2,1,0:T(8,128)(2,1)}, bf16[4,64,2048]{2,1,0:T(8,128)(2,1)}, u32[]{:S(2)}, u32[]{:S(2)}) collective-permute-start(bf16[4,64,2048]{2,1,0:T(8,128)(2,1)} %bitcast_dynamic-update-slice_fusion.16), channel_id=1, source_target_pairs={{0,8},{8,0},{16,24},{24,16},{1,9},{9,1},{17,25},{25,17},{2,10},{10... | collective-permute-start | bytes 3145736 | tf_op jit(solution)/shard_map/ppermute | solution.py:303
  120.6 51.7 %all-to-all-start.1 = ((bf16[8,64,1024]{2,1,0:T(8,128)(2,1)}), bf16[8,64,1024]{2,1,0:T(8,128)(2,1)}, u32[]{:S(2)}, u32[]{:S(2)}) async-start(bf16[8,64,1024]{2,1,0:T(8,128)(2,1)} %reshape.246), calls=%async_computation.1 | async-start | bytes 2097152 | tf_op jit(solution)/shard_map/all_to_all | solution.py:358
  126.1 164.2 %all-gather.9.cloned.1.call-start = ((), (), s32[]{:S(2)}) async-start(), calls=%async_computation.11 | async-start | bytes 5242880 | tf_op jit(solution)/shard_map/all_gather | solution.py:362
  172.2 39.8 %collective-permute-start.12 = (bf16[4,4,64,2048]{3,2,1,0:T(8,128)(2,1)}, bf16[4,4,64,2048]{3,2,1,0:T(8,128)(2,1)}, u32[]{:S(2)}, u32[]{:S(2)}) collective-permute-start(bf16[4,4,64,2048]{3,2,1,0:T(8,128)(2,1)} %bitcast_dynamic-update-slice_fusion.4), channel_id=1, source_target_pairs={{0,1},{1,0},{2,3},{3,2},{4,5},{5,4},{6,7},{7,6},{8,9},{9,8},{10,11... | collective-permute-start | bytes 12582920 | tf_op jit(solution)/shard_map/ppermute | solution.py:303
  172.9 29.2 %all-to-all-start.2 = ((bf16[8,64,1024]{2,1,0:T(8,128)(2,1)}), bf16[8,64,1024]{2,1,0:T(8,128)(2,1)}, u32[]{:S(2)}, u32[]{:S(2)}) async-start(bf16[8,64,1024]{2,1,0:T(8,128)(2,1)} %reshape.248), calls=%async_computation.2 | async-start | bytes 2097152 | tf_op jit(solution)/shard_map/all_to_all | solution.py:358
  204.6 24.9 %all-to-all-start.3 = ((bf16[8,192,256]{2,1,0:T(8,128)(2,1)}), bf16[8,192,256]{2,1,0:T(8,128)(2,1)}, u32[]{:S(2)}, u32[]{:S(2)}) async-start(bf16[8,192,256]{2,1,0:T(8,128)(2,1)} %bitcast.260), calls=%async_computation.3 | async-start | bytes 1572864 | tf_op jit(solution)/shard_map/all_to_all | solution.py:358
  212.0 90.7 %all-gather.7.cloned.1.call-start = ((), (), s32[]{:S(2)}) async-start(), calls=%async_computation.10 | async-start | bytes 7077888 | tf_op jit(solution)/shard_map/all_gather | solution.py:362
  238.8 104.2 %all-gather.13.cloned.1.call-start = ((), (), s32[]{:S(2)}) async-start(), calls=%async_computation.13 | async-start | bytes 3538944 | tf_op jit(solution)/shard_map/all_gather | solution.py:362
  239.0 26.3 %collective-permute-start.13 = (bf16[512,1024]{1,0:T(8,128)(2,1)}, bf16[512,1024]{1,0:T(8,128)(2,1)S(1)}, u32[]{:S(2)}, u32[]{:S(2)}) collective-permute-start(bf16[512,1024]{1,0:T(8,128)(2,1)} %bitcast.26), channel_id=1, source_target_pairs={{0,8},{8,0},{16,24},{24,16},{1,9},{9,1},{17,25},{25,17},{2,10},{10... | collective-permute-start | bytes 3145736 | tf_op jit(solution)/shard_map/ppermute | solution.py:303
  240.6 47.5 %collective-permute-start.14 = (bf16[512,1024]{1,0:T(8,128)(2,1)}, bf16[512,1024]{1,0:T(8,128)(2,1)S(1)}, u32[]{:S(2)}, u32[]{:S(2)}) collective-permute-start(bf16[512,1024]{1,0:T(8,128)(2,1)} %bitcast.26), channel_id=1, source_target_pairs={{0,16},{8,24},{16,0},{24,8},{1,17},{9,25},{17,1},{25,9},{2,18},{10... | collective-permute-start | bytes 3145736 | tf_op jit(solution)/shard_map/ppermute | solution.py:303
  241.3 47.9 %collective-permute-start.15 = (bf16[512,1024]{1,0:T(8,128)(2,1)}, bf16[512,1024]{1,0:T(8,128)(2,1)S(1)}, u32[]{:S(2)}, u32[]{:S(2)}) collective-permute-start(bf16[512,1024]{1,0:T(8,128)(2,1)} %bitcast.26), channel_id=1, source_target_pairs={{0,24},{8,16},{16,8},{24,0},{1,25},{9,17},{17,9},{25,1},{2,26},{10... | collective-permute-start | bytes 3145736 | tf_op jit(solution)/shard_map/ppermute | solution.py:303
  302.7 109.2 %reduce-scatter.4.cloned.1.call-start = ((), (), s32[]{:S(2)}) async-start(), calls=%async_computation.14 | async-start | bytes 7077888 | tf_op jit(solution)/shard_map/reduce_scatter | solution.py:366
  312.9 13.1 %copy-start.50 = (f32[1536,1024]{1,0:T(8,128)}, f32[1536,1024]{1,0:T(8,128)S(1)}, u32[]{:S(2)}) copy-start(f32[1536,1024]{1,0:T(8,128)S(1)} %fusion.50) | copy-start | bytes 18874372
  312.9 14.8 %copy-start.18 = (bf16[4,256,2048]{2,1,0:T(8,128)(2,1)S(1)}, bf16[4,256,2048]{2,1,0:T(8,128)(2,1)}, u32[]{:S(2)}) copy-start(bf16[4,256,2048]{2,1,0:T(8,128)(2,1)} %bitcast_dynamic-update-slice_fusion.8) | copy-start | bytes 12582916
  343.0 139.8 %reduce-scatter.6.cloned.1.call-start = ((), (), s32[]{:S(2)}) async-start(), calls=%async_computation.15 | async-start | bytes 7077888 | tf_op jit(solution)/shard_map/reduce_scatter | solution.py:366
  343.1 20.8 %slice-start = ((s8[6291456]{0:T(1024)(128)(4,1)}), s8[4194304]{0:T(1024)(128)(4,1)S(1)}, s32[]{:S(2)}) async-start(s8[6291456]{0:T(1024)(128)(4,1)} %bitcast.277), calls=%async_computation.18 | async-start | bytes 8388608
  351.9 11.9 %slice-start.1 = ((s8[6291456]{0:T(1024)(128)(4,1)}), s8[2097152]{0:T(1024)(128)(4,1)S(1)}, s32[]{:S(2)}) async-start(s8[6291456]{0:T(1024)(128)(4,1)} %bitcast.277), calls=%async_computation.19 | async-start | bytes 4194304
  384.2 30.2 %collective-permute-start.16 = (bf16[512,1024]{1,0:T(8,128)(2,1)}, bf16[512,1024]{1,0:T(8,128)(2,1)}, u32[]{:S(2)}, u32[]{:S(2)}) collective-permute-start(bf16[512,1024]{1,0:T(8,128)(2,1)} %get-tuple-element.147), channel_id=1, source_target_pairs={{0,8},{8,0},{16,24},{24,16},{1,9},{9,1},{17,25},{25,17},{2,10},{10... | collective-permute-start | bytes 3145736 | tf_op jit(solution)/shard_map/ppermute | solution.py:303
  385.7 28.7 %collective-permute-start.17 = (bf16[512,1024]{1,0:T(8,128)(2,1)}, bf16[512,1024]{1,0:T(8,128)(2,1)}, u32[]{:S(2)}, u32[]{:S(2)}) collective-permute-start(bf16[512,1024]{1,0:T(8,128)(2,1)} %get-tuple-element.148), channel_id=1, source_target_pairs={{0,16},{8,24},{16,0},{24,8},{1,17},{9,25},{17,1},{25,9},{2,18},{10... | collective-permute-start | bytes 3145736 | tf_op jit(solution)/shard_map/ppermute | solution.py:303
  414.5 3.5 collective-permute-start.22
  422.5 61.8 %collective-permute-start.18 = (bf16[512,1024]{1,0:T(8,128)(2,1)}, bf16[512,1024]{1,0:T(8,128)(2,1)}, u32[]{:S(2)}, u32[]{:S(2)}) collective-permute-start(bf16[512,1024]{1,0:T(8,128)(2,1)} %get-tuple-element.156), channel_id=1, source_target_pairs={{0,24},{8,16},{16,8},{24,0},{1,25},{9,17},{17,9},{25,1},{2,26},{10... | collective-permute-start | bytes 3145736 | tf_op jit(solution)/shard_map/ppermute | solution.py:303
  424.9 59.4 %collective-permute-start.19 = (bf16[512,1024]{1,0:T(8,128)(2,1)}, bf16[512,1024]{1,0:T(8,128)(2,1)}, u32[]{:S(2)}, u32[]{:S(2)}) collective-permute-start(bf16[512,1024]{1,0:T(8,128)(2,1)} %get-tuple-element.157), channel_id=1, source_target_pairs={{0,8},{8,0},{16,24},{24,16},{1,9},{9,1},{17,25},{25,17},{2,10},{10... | collective-permute-start | bytes 3145736 | tf_op jit(solution)/shard_map/ppermute | solution.py:303
  425.4 58.8 %collective-permute-start.20 = (bf16[512,1024]{1,0:T(8,128)(2,1)}, bf16[512,1024]{1,0:T(8,128)(2,1)}, u32[]{:S(2)}, u32[]{:S(2)}) collective-permute-start(bf16[512,1024]{1,0:T(8,128)(2,1)} %get-tuple-element.158), channel_id=1, source_target_pairs={{0,16},{8,24},{16,0},{24,8},{1,17},{9,25},{17,1},{25,9},{2,18},{10... | collective-permute-start | bytes 3145736 | tf_op jit(solution)/shard_map/ppermute | solution.py:303
  426.0 68.1 %collective-permute-start.21 = (bf16[512,1024]{1,0:T(8,128)(2,1)}, bf16[512,1024]{1,0:T(8,128)(2,1)}, u32[]{:S(2)}, u32[]{:S(2)}) collective-permute-start(bf16[512,1024]{1,0:T(8,128)(2,1)} %get-tuple-element.159), channel_id=1, source_target_pairs={{0,24},{8,16},{16,8},{24,0},{1,25},{9,17},{17,9},{25,1},{2,26},{10... | collective-permute-start | bytes 3145736 | tf_op jit(solution)/shard_map/ppermute | solution.py:303
  502.3 15.0 %collective-permute-start.23 = (bf16[192,2048]{1,0:T(8,128)(2,1)}, bf16[192,2048]{1,0:T(8,128)(2,1)}, u32[]{:S(2)}, u32[]{:S(2)}) collective-permute-start(bf16[192,2048]{1,0:T(8,128)(2,1)} %fusion.46), channel_id=1, source_target_pairs={{0,1},{1,0},{2,3},{3,2},{4,5},{5,4},{6,7},{7,6},{8,9},{9,8},{10,11... | collective-permute-start | bytes 2359304 | tf_op jit(solution)/shard_map/ppermute | solution.py:303
  503.3 24.0 %all-to-all-start.4 = ((bf16[8,192,256]{2,1,0:T(8,128)(2,1)}), bf16[8,192,256]{2,1,0:T(8,128)(2,1)}, u32[]{:S(2)}, u32[]{:S(2)}) async-start(bf16[8,192,256]{2,1,0:T(8,128)(2,1)} %bitcast.259), calls=%async_computation.6 | async-start | bytes 1572864 | tf_op jit(solution)/shard_map/all_to_all | solution.py:358
  530.4 62.2 %all-to-all-start.5 = ((bf16[2,8,64,1024]{3,2,0,1:T(8,128)(2,1)}), bf16[2,8,64,1024]{3,2,0,1:T(8,128)(2,1)}, u32[]{:S(2)}, u32[]{:S(2)}) async-start(bf16[2,8,64,1024]{3,2,0,1:T(8,128)(2,1)} %copy.107), calls=%async_computation.7 | async-start | bytes 4194304 | tf_op jit(solution)/shard_map/all_to_all | solution.py:598
  538.4 166.8 %reduce-scatter.8.cloned.1.call-start = ((), (), s32[]{:S(2)}) async-start(), calls=%async_computation.16 | async-start | bytes 7077888 | tf_op jit(solution)/shard_map/reduce_scatter | solution.py:366
  543.4 28.5 %collective-permute-start.24 = (bf16[4,64,2048]{2,1,0:T(8,128)(2,1)}, bf16[4,64,2048]{2,1,0:T(8,128)(2,1)}, u32[]{:S(2)}, u32[]{:S(2)}) collective-permute-start(bf16[4,64,2048]{2,1,0:T(8,128)(2,1)} %get-tuple-element.173), channel_id=1, source_target_pairs={{0,8},{8,0},{16,24},{24,16},{1,9},{9,1},{17,25},{25,17},{2,10},{10... | collective-permute-start | bytes 3145736 | tf_op jit(solution)/shard_map/ppermute | solution.py:303
  545.0 47.7 %collective-permute-start.25 = (bf16[4,64,2048]{2,1,0:T(8,128)(2,1)}, bf16[4,64,2048]{2,1,0:T(8,128)(2,1)}, u32[]{:S(2)}, u32[]{:S(2)}) collective-permute-start(bf16[4,64,2048]{2,1,0:T(8,128)(2,1)} %get-tuple-element.174), channel_id=1, source_target_pairs={{0,16},{8,24},{16,0},{24,8},{1,17},{9,25},{17,1},{25,9},{2,18},{10... | collective-permute-start | bytes 3145736 | tf_op jit(solution)/shard_map/ppermute | solution.py:303
  546.4 46.2 %collective-permute-start.26 = (bf16[4,64,2048]{2,1,0:T(8,128)(2,1)}, bf16[4,64,2048]{2,1,0:T(8,128)(2,1)}, u32[]{:S(2)}, u32[]{:S(2)}) collective-permute-start(bf16[4,64,2048]{2,1,0:T(8,128)(2,1)} %get-tuple-element.175), channel_id=1, source_target_pairs={{0,24},{8,16},{16,8},{24,0},{1,25},{9,17},{17,9},{25,1},{2,26},{10... | collective-permute-start | bytes 3145736 | tf_op jit(solution)/shard_map/ppermute | solution.py:303
  570.1 22.5 %copy-start.5 = (bf16[1536,768]{1,0:T(8,128)(2,1)S(1)}, bf16[1536,768]{1,0:T(8,128)(2,1)}, u32[]{:S(2)}) copy-start(bf16[1536,768]{1,0:T(8,128)(2,1)} %copy-done.4) | copy-start | bytes 7077892
  604.5 17.4 %copy-start.15 = (f32[4,64,2048]{2,1,0:T(8,128)}, f32[4,64,2048]{2,1,0:T(8,128)S(1)}, u32[]{:S(2)}) copy-start(f32[4,64,2048]{2,1,0:T(8,128)S(1)} %convert_add_fusion) | copy-start | bytes 6291460
  605.6 16.3 %collective-permute-start.32 = (bf16[64,2048]{1,0:T(8,128)(2,1)S(1)}, bf16[64,2048]{1,0:T(8,128)(2,1)S(1)}, u32[]{:S(2)}, u32[]{:S(2)}) collective-permute-start(bf16[64,2048]{1,0:T(8,128)(2,1)S(1)} %get-tuple-element.246), channel_id=1, source_target_pairs={{0,6},{1,7},{2,0},{3,1},{4,2},{5,3},{6,4},{7,5},{8,14},{9,15},{10,... | collective-permute-start | bytes 786440 | tf_op jit(solution)/shard_map/ppermute | solution.py:336
  606.2 43.0 %collective-permute-start.27 = (bf16[512,768]{1,0:T(8,128)(2,1)}, bf16[512,768]{1,0:T(8,128)(2,1)}, u32[]{:S(2)}, u32[]{:S(2)}) collective-permute-start(bf16[512,768]{1,0:T(8,128)(2,1)} %get-tuple-element.181), channel_id=1, source_target_pairs={{0,8},{8,0},{16,24},{24,16},{1,9},{9,1},{17,25},{25,17},{2,10},{10... | collective-permute-start | bytes 2359304 | tf_op jit(solution)/shard_map/ppermute | solution.py:303
  607.4 41.7 %collective-permute-start.28 = (bf16[512,768]{1,0:T(8,128)(2,1)}, bf16[512,768]{1,0:T(8,128)(2,1)}, u32[]{:S(2)}, u32[]{:S(2)}) collective-permute-start(bf16[512,768]{1,0:T(8,128)(2,1)} %get-tuple-element.182), channel_id=1, source_target_pairs={{0,16},{8,24},{16,0},{24,8},{1,17},{9,25},{17,1},{25,9},{2,18},{10... | collective-permute-start | bytes 2359304 | tf_op jit(solution)/shard_map/ppermute | solution.py:303
  608.3 40.9 %collective-permute-start.29 = (bf16[512,768]{1,0:T(8,128)(2,1)}, bf16[512,768]{1,0:T(8,128)(2,1)}, u32[]{:S(2)}, u32[]{:S(2)}) collective-permute-start(bf16[512,768]{1,0:T(8,128)(2,1)} %get-tuple-element.183), channel_id=1, source_target_pairs={{0,24},{8,16},{16,8},{24,0},{1,25},{9,17},{17,9},{25,1},{2,26},{10... | collective-permute-start | bytes 2359304 | tf_op jit(solution)/shard_map/ppermute | solution.py:303
  609.8 31.4 %collective-permute-start.31 = (bf16[64,2048]{1,0:T(8,128)(2,1)}, bf16[64,2048]{1,0:T(8,128)(2,1)}, u32[]{:S(2)}, u32[]{:S(2)}) collective-permute-start(bf16[64,2048]{1,0:T(8,128)(2,1)} %get-tuple-element.247), channel_id=1, source_target_pairs={{0,4},{1,5},{2,6},{3,7},{4,0},{5,1},{6,2},{7,3},{8,12},{9,13},{10,... | collective-permute-start | bytes 786440 | tf_op jit(solution)/shard_map/ppermute | solution.py:336
  622.0 27.2 %collective-permute-start.30 = (bf16[64,2048]{1,0:T(8,128)(2,1)}, bf16[64,2048]{1,0:T(8,128)(2,1)}, u32[]{:S(2)}, u32[]{:S(2)}) collective-permute-start(bf16[64,2048]{1,0:T(8,128)(2,1)} %get-tuple-element.248), channel_id=1, source_target_pairs={{0,2},{1,3},{2,4},{3,5},{4,6},{5,7},{6,0},{7,1},{8,10},{9,11},{10,... | collective-permute-start | bytes 786440 | tf_op jit(solution)/shard_map/ppermute | solution.py:336
  638.8 11.8 %copy-start.12 = (f32[8,8,32,256]{3,1,2,0:T(8,128)S(1)}, f32[8,8,32,256]{3,1,2,0:T(8,128)}, u32[]{:S(2)}) copy-start(f32[8,8,32,256]{3,1,2,0:T(8,128)} %copy.123) | copy-start | bytes 6291460
  649.2 17.2 %collective-permute-start.33 = (bf16[256,1024]{1,0:T(8,128)(2,1)}, bf16[256,1024]{1,0:T(8,128)(2,1)}, u32[]{:S(2)}, u32[]{:S(2)}) collective-permute-start(bf16[256,1024]{1,0:T(8,128)(2,1)} %get-tuple-element.206), channel_id=1, source_target_pairs={{0,8},{8,0},{16,24},{24,16},{1,9},{9,1},{17,25},{25,17},{2,10},{10... | collective-permute-start | bytes 1572872 | tf_op jit(solution)/shard_map/ppermute | solution.py:303
  653.9 26.4 %copy-start.26 = (bf16[256,1024]{1,0:T(8,128)(2,1)S(1)}, bf16[256,1024]{1,0:T(8,128)(2,1)}, u32[]{:S(2)}) copy-start(bf16[256,1024]{1,0:T(8,128)(2,1)} %get-tuple-element.205) | copy-start | bytes 1572868
  653.9 26.4 %collective-permute-start.34 = (bf16[256,1024]{1,0:T(8,128)(2,1)}, bf16[256,1024]{1,0:T(8,128)(2,1)}, u32[]{:S(2)}, u32[]{:S(2)}) collective-permute-start(bf16[256,1024]{1,0:T(8,128)(2,1)} %get-tuple-element.207), channel_id=1, source_target_pairs={{0,16},{8,24},{16,0},{24,8},{1,17},{9,25},{17,1},{25,9},{2,18},{10... | collective-permute-start | bytes 1572872 | tf_op jit(solution)/shard_map/ppermute | solution.py:303
  654.3 26.0 %collective-permute-start.35 = (bf16[256,1024]{1,0:T(8,128)(2,1)}, bf16[256,1024]{1,0:T(8,128)(2,1)}, u32[]{:S(2)}, u32[]{:S(2)}) collective-permute-start(bf16[256,1024]{1,0:T(8,128)(2,1)} %get-tuple-element.208), channel_id=1, source_target_pairs={{0,24},{8,16},{16,8},{24,0},{1,25},{9,17},{17,9},{25,1},{2,26},{10... | collective-permute-start | bytes 1572872 | tf_op jit(solution)/shard_map/ppermute | solution.py:303
  658.9 42.7 %all-to-all-start.6 = ((bf16[8,64,768]{2,1,0:T(8,128)(2,1)}), bf16[8,64,768]{2,1,0:T(8,128)(2,1)S(1)}, u32[]{:S(2)}, u32[]{:S(2)}) async-start(bf16[8,64,768]{2,1,0:T(8,128)(2,1)} %bitcast.85), calls=%async_computation.9 | async-start | bytes 1572864 | tf_op jit(solution)/shard_map/all_to_all | solution.py:358
  664.6 35.2 %copy-start.25 = (bf16[256,1024]{1,0:T(8,128)(2,1)S(1)}, bf16[256,1024]{1,0:T(8,128)(2,1)}, u32[]{:S(2)}) copy-start(bf16[256,1024]{1,0:T(8,128)(2,1)} %get-tuple-element.209) | copy-start | bytes 1572868
  664.6 22.2 %collective-permute-start.36 = (bf16[256,1024]{1,0:T(8,128)(2,1)}, bf16[256,1024]{1,0:T(8,128)(2,1)S(1)}, u32[]{:S(2)}, u32[]{:S(2)}) collective-permute-start(bf16[256,1024]{1,0:T(8,128)(2,1)} %get-tuple-element.210), channel_id=1, source_target_pairs={{0,8},{8,0},{16,24},{24,16},{1,9},{9,1},{17,25},{25,17},{2,10},{10... | collective-permute-start | bytes 1572872 | tf_op jit(solution)/shard_map/ppermute | solution.py:303
  666.0 33.8 %collective-permute-start.37 = (bf16[256,1024]{1,0:T(8,128)(2,1)}, bf16[256,1024]{1,0:T(8,128)(2,1)S(1)}, u32[]{:S(2)}, u32[]{:S(2)}) collective-permute-start(bf16[256,1024]{1,0:T(8,128)(2,1)} %get-tuple-element.211), channel_id=1, source_target_pairs={{0,16},{8,24},{16,0},{24,8},{1,17},{9,25},{17,1},{25,9},{2,18},{10... | collective-permute-start | bytes 1572872 | tf_op jit(solution)/shard_map/ppermute | solution.py:303
  666.4 33.4 %collective-permute-start.38 = (bf16[256,1024]{1,0:T(8,128)(2,1)}, bf16[256,1024]{1,0:T(8,128)(2,1)S(1)}, u32[]{:S(2)}, u32[]{:S(2)}) collective-permute-start(bf16[256,1024]{1,0:T(8,128)(2,1)} %get-tuple-element.212), channel_id=1, source_target_pairs={{0,24},{8,16},{16,8},{24,0},{1,25},{9,17},{17,9},{25,1},{2,26},{10... | collective-permute-start | bytes 1572872 | tf_op jit(solution)/shard_map/ppermute | solution.py:303
  (45 other events, 254.7 us)
Sparse Core Ops, SparseCore 0:
  9.7 94.3 all-gather.14
  113.1 55.7 all-gather.10
  172.4 54.5 all-gather.8
  238.9 63.7 all-gather.6
  304.8 38.1 all-gather.12
  345.1 66.7 reduce-scatter.3
  414.6 68.1 reduce-scatter.5
  601.7 103.5 reduce-scatter.7
